TPU v7x, 32 devices: a whole 2x2x4 slice. The times are simulated.
32 devices in a mesh: dp: 16 (over z, y, x), tensor: 2 (over core).
Axes of the slice: x: 2, y: 2, z: 4, core: 2. Of those that a mesh axis runs over, the one named last changes fastest.
Arguments:
- tokens: bfloat16 [8192, 768], P(('dp', 'tensor')), may hold values from -6 to 6
- query_weight: bfloat16 [768, 768], P('dp', 'tensor'), may hold values from -0.21875 to 0.21875
- key_weight: bfloat16 [768, 768], P('dp', 'tensor'), may hold values from -0.21875 to 0.21875
- value_weight: bfloat16 [768, 768], P('dp', 'tensor'), may hold values from -0.21875 to 0.21875
- output_weight: bfloat16 [768, 768], P('dp', 'tensor'), may hold values from -1.75 to 1.75
- inner_weight: bfloat16 [768, 3072], P('dp', 'tensor'), may hold values from -0.21875 to 0.21875
- outer_weight: bfloat16 [768, 3072], P('dp', 'tensor'), may hold values from -0.109375 to 0.109375
- attn_gain: float32 [768], replicated, may hold values from 0.5 to 1.5
- attn_shift: float32 [768], replicated, may hold values from -3 to 3
- ffn_gain: float32 [768], replicated, may hold values from 0.5 to 1.5
- ffn_shift: float32 [768], replicated, may hold values from -3 to 3
- teacher: bfloat16 [8192, 768], P(('dp', 'tensor')), may hold values from -6 to 6
- segments: int32 [2, 4096], replicated, may hold values from 0 to 4, as said below
- random_blocks: int32 [12, 64, 3], P('tensor'), may hold values from 0 to 63
- valid_tokens: int32 [8192], P(('dp', 'tensor')), may hold values from 0 to 1, as said below
Outputs:
- output: bfloat16 [8192, 768], P(('dp', 'tensor'))
- loss_value: float32 [], replicated
- grad_tokens: float32 [8192, 768], P(('dp', 'tensor'))
- grad_query: float32 [768, 768], P('dp', 'tensor')
- grad_key: float32 [768, 768], P('dp', 'tensor')
- grad_value: float32 [768, 768], P('dp', 'tensor')
- grad_output: float32 [768, 768], P('dp', 'tensor')
- grad_inner: float32 [768, 3072], P('dp', 'tensor')
- grad_outer: float32 [768, 3072], P('dp', 'tensor')
- grad_attn_gain: float32 [768], P(('dp', 'tensor'))
- grad_attn_shift: float32 [768], P(('dp', 'tensor'))
- grad_ffn_gain: float32 [768], P(('dp', 'tensor'))
- grad_ffn_shift: float32 [768], P(('dp', 'tensor'))
Inputs may be any that keep to these rules, and one draw needn't show every extreme that they name: `segments`: each sequence holds five documents numbered 0 to 4 in order; document 2 covers at least positions 1843 to 2251. `valid_tokens`: the first token of every sequence is valid.
All inputs are finite; a program needn't handle non-finite values.
Results may differ from a plain program's by a relative error of at most 0.015.
Values may be sent and summed in bfloat16 or wider, within the bound.
No kernel may reach another device: no remote copies, remote signals or barrier semaphores. Data moves between devices by JAX's collectives and lax.ppermute only.
A program may use at most 192 MiB of HBM per device.

v0:
```python
import functools

import jax
import jax.numpy as jnp
from jax import lax
from jax.experimental import pallas as pl
from jax.experimental.pallas import tpu as pltpu
from jax.sharding import PartitionSpec as P

BLOCK = 64
HEAD = 64
PAIR = 2 * HEAD
SLOTS = 6
ROUTES = ((0, 1, 2), (1, 2, 0), (2, 0, 1))

epsilon = 1e-05
masked_value = -1e30
score_scale = 0.125


def swap_mask(block, mask):
    count = lax.axis_size("dp")
    return lax.ppermute(block, "dp", [(one, one ^ mask) for one in range(count)])


def swap_core(block):
    return lax.ppermute(block, "tensor", [(0, 1), (1, 0)])


def dot_plain(left_side, right_side):
    return jnp.dot(left_side, right_side, preferred_element_type=jnp.float32)


def dot_cols(left_side, right_side):
    return lax.dot_general(
        left_side, right_side, (((1,), (1,)), ((), ())), preferred_element_type=jnp.float32
    )


def dot_rows(left_side, right_side):
    return lax.dot_general(
        left_side, right_side, (((0,), (0,)), ((), ())), preferred_element_type=jnp.float32
    )


def params(megabytes):
    return pltpu.CompilerParams(vmem_limit_bytes=int(megabytes) << 20)


def cost(flops=0, moved=0, transcendentals=0):
    return pl.CostEstimate(flops=int(flops), bytes_accessed=int(moved), transcendentals=int(transcendentals))


def in_vmem(count):
    return [pl.BlockSpec(memory_space=pltpu.VMEM)] * count


def in_smem(count):
    return [pl.BlockSpec(memory_space=pltpu.SMEM)] * count


def shaped(shape, dtype=jnp.float32):
    return jax.ShapeDtypeStruct(tuple(shape), dtype)


def local_call(kernel, outs, vmem_inputs, smem_inputs=(), scratch=(), flops=0, transcendentals=0, spare=8, free=0):
    moved = sum(one.size * one.dtype.itemsize for one in list(vmem_inputs) + list(outs))
    held = sum(one.size * one.dtype.itemsize for one in (shaped(s.shape, s.dtype) for s in scratch))
    held = held // (1 << 20) + 1 + spare
    return pl.pallas_call(
        kernel,
        out_shape=tuple(
            one if len(outs) - at <= free else pltpu.VMEM(one.shape, one.dtype) for at, one in enumerate(outs)
        ),
        in_specs=in_smem(len(smem_inputs)) + in_vmem(len(vmem_inputs)),
        out_specs=tuple(in_vmem(len(outs))),
        scratch_shapes=list(scratch),
        compiler_params=params(held),
        cost_estimate=pl.CostEstimate(flops=1000, bytes_accessed=1000, transcendentals=0),
    )(*smem_inputs, *[pltpu.with_memory_space_constraint(one, pltpu.VMEM) for one in vmem_inputs])


def slot_masks(bits):
    return [
        sum(((slot >> at) & 1) << bit for at, bit in enumerate(bits))
        for slot in range(1 << len(bits))
    ]


def in_pieces(values):
    high = values.astype(jnp.bfloat16).astype(jnp.float32)
    middle = (values - high).astype(jnp.bfloat16).astype(jnp.float32)
    return high + pltpu.roll(middle, 8, 1) + pltpu.roll(values - high - middle, 16, 1)


def from_pieces(pieces):
    lanes = pieces.shape[1]
    total = pieces + pltpu.roll(pieces, lanes - 8, 1) + pltpu.roll(pieces, lanes - 16, 1)
    return jnp.where(lax.broadcasted_iota(jnp.int32, pieces.shape, 1) % PAIR < 8, total, 0.0)


def fold_kernel(*refs, thirds, arrivals, plain):
    outs = refs[thirds * (1 + arrivals) :]
    for third in range(thirds):
        keep_ref = refs[third * (1 + arrivals)]
        came = refs[third * (1 + arrivals) + 1 : (third + 1) * (1 + arrivals)]
        half, lines = keep_ref.shape[0] // 2, keep_ref.shape[1]
        most = lines if plain is None else min(plain, lines)
        for side in range(2):
            part = slice(side * half, (side + 1) * half)
            total = sum([one[part, :most].astype(jnp.float32) for one in came], keep_ref[part, :most])
            out_ref = outs[2 * third + side]
            out_ref[:, :most] = total.astype(out_ref.dtype)
            if most == lines:
                continue
            for at in range(half):
                total = keep_ref[side * half + at, most:]
                for one in came:
                    total += from_pieces(one[side * half + at, most:].astype(jnp.float32))
                out_ref[at, most:] = (in_pieces(total) if side else total).astype(out_ref.dtype)


def fold(keeps, arrivals, plain=None):
    outs = []
    for keep in keeps:
        half = (keep.shape[0] // 2,) + keep.shape[1:]
        outs += [shaped(half), shaped(half, jnp.bfloat16)]
    operands = []
    for keep, came in zip(keeps, arrivals):
        operands += [keep] + list(came)
    kernel = functools.partial(fold_kernel, thirds=len(keeps), arrivals=len(arrivals[0]), plain=plain)
    outs = local_call(kernel, outs, operands)
    return list(outs[::2]), list(outs[1::2])


def pick(chosen, table):
    return lax.dot_general(
        chosen.astype(jnp.bfloat16), table.astype(jnp.bfloat16), (((chosen.ndim - 1,), (0,)), ((), ())),
        preferred_element_type=jnp.float32,
    )


def attention_tables(random_blocks, segment_all, place, core, span, row_blocks):
    heads, blocks, draws = random_blocks.shape
    half, pairs = row_blocks // 2, heads // 2
    local = jnp.arange(row_blocks, dtype=jnp.int32)
    owner = jnp.where(local < half, core, 1 - core)
    absolute = place * row_blocks + owner * half + local % half
    every = jnp.arange(blocks, dtype=jnp.int32)
    mine = absolute[:, None] == every
    edge = (every == 0) | (every == blocks - 1)
    fixed = (jnp.abs(absolute[:, None] - every) <= 1) | edge | edge[absolute][:, None]
    segment_table = segment_all.reshape(blocks, BLOCK).astype(jnp.float32)
    low, high = jnp.min(segment_table, 1), jnp.max(segment_table, 1)
    reach = (jnp.max(jnp.where(mine, low, -1.0), 1)[:, None] <= high) & (
        low <= jnp.max(jnp.where(mine, high, -1.0), 1)[:, None]
    )
    drawn = pick(mine, random_blocks.transpose(1, 0, 2).reshape(blocks, heads * draws))
    drawn = drawn.reshape(row_blocks, heads, draws, 1) == every.astype(jnp.float32)
    allowed = (jnp.any(drawn, 2) | fixed[:, None]) & reach[:, None]
    allowed = allowed.reshape(row_blocks, pairs, 2, blocks)
    listed = jnp.any(allowed, 2)
    rank = pick(listed, every[:, None] < every[None, :])
    count = jnp.max(jnp.sum(listed.astype(jnp.int32), -1), -1)
    chunks = -(-count // SLOTS)
    ends = jnp.sum(jnp.where(local[:, None] >= local[None, :], chunks[None, :], 0), 1)
    most = (row_blocks - 1) * -(-min(blocks, 5 + 2 * draws) // SLOTS) + -(-blocks // SLOTS)
    if span == 1:
        most += -(-blocks // SLOTS)
    items = jnp.arange(most, dtype=jnp.int32)
    item_query = jnp.minimum(jnp.sum((items[:, None] >= ends[None, :]).astype(jnp.int32), 1), row_blocks - 1)
    item_is = item_query[:, None] == local
    first = jnp.sum(jnp.where(item_is, (ends - chunks)[None, :], 0), 1)
    spots = ((items - first) * SLOTS)[:, None] + jnp.arange(SLOTS, dtype=jnp.int32)
    stored = (
        jnp.where((every % row_blocks) // half == core, 0, span * half)
        + ((every // row_blocks) ^ place) * half + every % half
    )
    rows = jnp.concatenate([jnp.where(listed, rank, -1.0)[:, :, None], allowed.astype(jnp.float32)], 2)
    rows = pick(item_is, rows.reshape(row_blocks, -1)).reshape(most, pairs, 3, blocks)
    here = rows[:, :, 0, None, :] == spots[:, None, :, None].astype(jnp.float32)
    code = rows[:, :, 1, None, :] * 256.0 + rows[:, :, 2, None, :] * 512.0 + stored.astype(jnp.float32)
    codes = jnp.sum(jnp.where(here, code, 0.0), -1).astype(jnp.int32)
    order = jnp.arange(2 * span * half, dtype=jnp.int32)
    order_block = (
        ((order % (span * half)) // half) ^ place
    ) * row_blocks + jnp.where(order < span * half, core, 1 - core) * half + order % half
    key_side = pick(order_block[:, None] == every, segment_table).reshape(-1, 1)
    query_side = pick(mine, segment_table)
    query_side = jnp.concatenate([query_side, query_side], 1)
    numbers = [ends[-1:], item_query, (items == first), codes.reshape(-1)]
    return (
        jnp.concatenate([one.astype(jnp.int32) for one in numbers]),
        query_side,
        jnp.broadcast_to(key_side, (key_side.shape[0], PAIR)),
    )


def two_heads(rows, low_lanes):
    rows = rows.astype(jnp.float32)
    zero = jnp.zeros_like(rows)
    return jnp.concatenate(
        [jnp.where(low_lanes, rows, zero), jnp.where(low_lanes, zero, rows)], 0
    )


def item_blocks(numbers_ref, first, side, key_side_ref):
    low_row = lax.broadcasted_iota(jnp.int32, (1, PAIR), 1) < HEAD
    spots, masks = [], []
    for slot in range(SLOTS):
        code = numbers_ref[first + slot]
        spot = pl.ds(pl.multiple_of((code & 255) * BLOCK, BLOCK), BLOCK)
        flags = jnp.where(low_row, code & 256, code & 512)
        spots.append(spot)
        masks.append(key_side_ref[spot, :] == jnp.where(flags != 0, side, -1.0))
    return spots, jnp.concatenate(masks, 0)


def attend_kernel(
    numbers_ref, query_side_ref, key_side_ref,
    own_query_ref, own_kv_ref, other_ref, query_weight_ref, kv_weight_ref,
    mixed_ref, mass_ref, q_ref, kv_ref, state_ref, mixture_ref, *, pairs
):
    half_rows, half_kv = own_query_ref.shape[0], own_kv_ref.shape[0]
    q_ref[:half_rows, :] = own_query_ref[...]
    q_ref[half_rows:, :] = dot_plain(other_ref[:half_rows, :], query_weight_ref[...]).astype(jnp.bfloat16)
    kv_ref[:half_kv, :] = own_kv_ref[...]
    step = 512
    for start in range(0, half_kv, step):
        kv_ref[half_kv + start : half_kv + start + step, :] = dot_plain(
            other_ref[start : start + step, :], kv_weight_ref[...]
        ).astype(jnp.bfloat16)
    low_lanes = lax.broadcasted_iota(jnp.int32, (BLOCK, PAIR), 1) < HEAD
    most = (numbers_ref.shape[0] - 1) // (2 + pairs * SLOTS)

    def one_item(item, carry):
        query = numbers_ref[1 + item]
        fresh = numbers_ref[1 + most + item] == 1
        side = query_side_ref[pl.ds(query, 1), :]
        rows = pl.ds(pl.multiple_of(query * BLOCK, BLOCK), BLOCK)
        held = []
        for pair in range(pairs):
            both = two_heads(q_ref[rows, pair * PAIR : (pair + 1) * PAIR], low_lanes).astype(jnp.bfloat16)
            spots, mask = item_blocks(
                numbers_ref, 1 + 2 * most + (item * pairs + pair) * SLOTS, side, key_side_ref
            )
            start = pair * 2 * PAIR
            keys = jnp.concatenate([kv_ref[spot, start : start + PAIR] for spot in spots], 0)
            values = jnp.concatenate([kv_ref[spot, start + PAIR : start + 2 * PAIR] for spot in spots], 0)
            held.append((jnp.where(mask, dot_cols(keys, both) * score_scale, masked_value), values))
        done = []
        for pair in range(pairs):
            scores, values = held[pair]
            place = query * pairs + pair
            state = state_ref[place]
            old_top = jnp.where(fresh, masked_value, state[0:1, :])
            top = jnp.maximum(old_top, jnp.max(scores, axis=0, keepdims=True))
            raised = jnp.exp(scores - top)
            shrunk = jnp.exp(old_top - top)
            total = jnp.where(fresh, 0.0, state[1:2, :] * shrunk) + jnp.sum(raised, axis=0, keepdims=True)
            mixture = jnp.where(fresh, 0.0, mixture_ref[place] * shrunk) + dot_rows(
                values, raised.astype(jnp.bfloat16)
            )
            done.append((top, total, mixture))
        for pair in range(pairs):
            top, total, mixture = done[pair]
            place = query * pairs + pair
            state_ref[place, 0:1, :] = top
            state_ref[place, 1:2, :] = total
            mixture_ref[place] = mixture
            normed = (mixture / total).T
            mixed_ref[rows, pair * PAIR : (pair + 1) * PAIR] = jnp.where(
                low_lanes, normed[:BLOCK], normed[BLOCK:]
            )
            mass_ref[place] = jnp.broadcast_to(top + jnp.log(total), (8, PAIR))
        return carry

    lax.fori_loop(0, numbers_ref[0], one_item, 0)


def attend(tables, own_query, own_kv, other, query_weight, kv_weight):
    rows, width = 2 * own_query.shape[0], own_query.shape[1]
    pairs, row_blocks = width // PAIR, rows // BLOCK
    places = pairs * row_blocks
    return local_call(
        functools.partial(attend_kernel, pairs=pairs),
        [
            shaped((rows, width)),
            shaped((places, 8, PAIR)),
            shaped((rows, width), jnp.bfloat16),
            shaped((2 * own_kv.shape[0], own_kv.shape[1]), jnp.bfloat16),
        ],
        list(tables[1:]) + [own_query, own_kv, other, query_weight, kv_weight],
        tables[:1],
        [
            pltpu.VMEM((places, 8, PAIR), jnp.float32),
            pltpu.VMEM((places, PAIR, PAIR), jnp.float32),
        ],
        flops=8e9, transcendentals=4e6, spare=12,
    )


def attend_back_kernel(
    numbers_ref, query_side_ref, key_side_ref, q_ref, kv_ref,
    mixed_ref, mass_ref, own_grad_ref, other_grad_ref, weight_ref,
    query_grad_ref, kv_grad_ref, sum_ref, grad_ref, query_sum_ref, *, pairs
):
    half_rows = own_grad_ref.shape[0]
    grad_ref[:half_rows, :] = dot_plain(own_grad_ref[...], weight_ref[...]).astype(jnp.bfloat16)
    grad_ref[half_rows:, :] = dot_plain(other_grad_ref[...], weight_ref[...]).astype(jnp.bfloat16)
    low_lanes = lax.broadcasted_iota(jnp.int32, (BLOCK, PAIR), 1) < HEAD
    most = (numbers_ref.shape[0] - 1) // (2 + pairs * SLOTS)
    sum_ref[...] = jnp.zeros_like(sum_ref)

    def one_item(item, carry):
        query = numbers_ref[1 + item]
        fresh = numbers_ref[1 + most + item] == 1
        side = query_side_ref[pl.ds(query, 1), :]
        rows = pl.ds(pl.multiple_of(query * BLOCK, BLOCK), BLOCK)
        held = []
        for pair in range(pairs):
            lanes = slice(pair * PAIR, (pair + 1) * PAIR)
            both = two_heads(q_ref[rows, lanes], low_lanes).astype(jnp.bfloat16)
            grads = grad_ref[rows, lanes].astype(jnp.float32)
            turned = (grads * mixed_ref[rows, lanes]).T
            inner = jnp.concatenate(
                [jnp.sum(turned[:HEAD], axis=0, keepdims=True), jnp.sum(turned[HEAD:], axis=0, keepdims=True)], 1
            )
            grads = two_heads(grads, low_lanes).astype(jnp.bfloat16)
            spots, mask = item_blocks(
                numbers_ref, 1 + 2 * most + (item * pairs + pair) * SLOTS, side, key_side_ref
            )
            start = pair * 2 * PAIR
            kv = jnp.concatenate([kv_ref[spot, start : start + 2 * PAIR] for spot in spots], 0)
            blank = jnp.zeros_like(both)
            sides = jnp.concatenate(
                [jnp.concatenate([both, blank], 1), jnp.concatenate([blank, grads], 1)], 0
            )
            held.append((dot_cols(kv, sides), inner, sides, kv, spots, mask))
        done = []
        for pair in range(pairs):
            products, inner, sides, kv, spots, mask = held[pair]
            place = query * pairs + pair
            scores = jnp.where(mask, products[:, :PAIR] * score_scale, masked_value)
            chances = jnp.exp(scores - mass_ref[place, 0:1, :])
            score_grads = (chances * (products[:, PAIR:] - inner)).astype(jnp.bfloat16)
            query_grad = dot_rows(score_grads, kv[:, :PAIR])
            kv_grad = dot_plain(jnp.concatenate([score_grads, chances.astype(jnp.bfloat16)], 1), sides)
            done.append((query_grad, kv_grad))
        for pair in range(pairs):
            lanes = slice(pair * PAIR, (pair + 1) * PAIR)
            start = pair * 2 * PAIR
            query_grad, kv_grad = done[pair]
            spots = held[pair][4]
            query_grad = jnp.where(low_lanes, query_grad[:BLOCK], query_grad[BLOCK:])
            query_sum_ref[rows, lanes] = jnp.where(fresh, 0.0, query_sum_ref[rows, lanes]) + query_grad
            for slot, spot in enumerate(spots):
                sum_ref[spot, start : start + 2 * PAIR] += kv_grad[slot * BLOCK : (slot + 1) * BLOCK]
        return carry

    lax.fori_loop(0, numbers_ref[0], one_item, 0)
    query_grad_ref[...] = (query_sum_ref[...] * score_scale).astype(jnp.bfloat16)
    for pair in range(pairs):
        start = pair * 2 * PAIR
        kv_grad_ref[:, start : start + PAIR] = (sum_ref[:, start : start + PAIR] * score_scale).astype(jnp.bfloat16)
        kv_grad_ref[:, start + PAIR : start + 2 * PAIR] = sum_ref[:, start + PAIR : start + 2 * PAIR].astype(
            jnp.bfloat16
        )


def attend_back(tables, queries, kv, mixed, mass, own_grad, other_grad, weight):
    rows, width = queries.shape
    pairs = width // PAIR
    return local_call(
        functools.partial(attend_back_kernel, pairs=pairs),
        [shaped((rows, width), jnp.bfloat16), shaped(kv.shape, jnp.bfloat16)],
        list(tables[1:]) + [queries, kv, mixed, mass, own_grad, other_grad, weight],
        tables[:1],
        [
            pltpu.VMEM(kv.shape, jnp.float32),
            pltpu.VMEM((rows, width), jnp.bfloat16),
            pltpu.VMEM((rows, width), jnp.float32),
        ],
        flops=10e9, transcendentals=4e6, spare=12,
    )


LANES = 2 * PAIR


def packed_rows(slot_rows, columns):
    return columns // LANES * slot_rows + (slot_rows // 2 if columns % LANES else 0)


def put_packed(out_ref, base, source_ref, first, columns, slot_rows):
    for chunk in range(columns // LANES):
        at = first + chunk * LANES
        out_ref[base : base + slot_rows, :] = source_ref[:, at : at + LANES]
        base += slot_rows
    if columns % LANES:
        half, at = slot_rows // 2, first + columns - PAIR
        out_ref[base : base + half, :PAIR] = source_ref[:half, at : at + PAIR]
        out_ref[base : base + half, PAIR:] = source_ref[half:, at : at + PAIR]


def unpacked(packed, slot_rows):
    full = packed.shape[0] // slot_rows
    parts = [packed[at * slot_rows : (at + 1) * slot_rows] for at in range(full)]
    tail = packed[full * slot_rows :]
    if tail.shape[0]:
        parts.append(jnp.concatenate([tail[:, :PAIR], tail[:, PAIR:]], 0))
    return jnp.concatenate(parts, 1)


def fetched(far, near, arrived):
    copies = [
        pltpu.make_async_copy(far_ref, near_ref, arrived.at[at])
        for at, (far_ref, near_ref) in enumerate(zip(far, near))
    ]
    for copy in copies:
        copy.start()
    for copy in copies:
        copy.wait()


def weight_start_kernel(*refs, cut):
    near = refs[9:-1]
    fetched(refs[:7], near, refs[-1])
    query_ref, key_ref, value_ref, inner_ref, outer_ref, output_ref, valid_ref = near
    first_ref, second_ref = refs[7:9]
    width = query_ref.shape[1]
    for at, one in enumerate((query_ref, key_ref, value_ref)):
        first_ref[:, at * width : (at + 1) * width] = one[...]
    second_ref[:, :cut] = inner_ref[:, :cut]
    second_ref[:, cut : 2 * cut] = outer_ref[:, :cut]
    at = 2 * cut
    for one, first in ((inner_ref, cut), (outer_ref, cut), (output_ref, 0)):
        size = one.shape[1] - first
        second_ref[:, at : at + size] = one[:, first:]
        at += size
    count = jnp.sum(valid_ref[...].astype(jnp.float32), axis=1, keepdims=True)
    second_ref[:, at:] = jnp.broadcast_to(count, (second_ref.shape[0], PAIR)).astype(jnp.bfloat16)


def token_start_kernel(tokens_ref, *refs):
    near_ref, arrived = refs[3:]
    fetched([tokens_ref], [near_ref], arrived)
    columns = refs[0].shape[1]
    for at in range(3):
        refs[at][...] = near_ref[:, at * columns : (at + 1) * columns]


def fetching_call(kernel, outs, sources):
    return pl.pallas_call(
        kernel,
        out_shape=[pltpu.VMEM(one.shape, one.dtype) for one in outs],
        in_specs=[pl.BlockSpec(memory_space=pltpu.HBM)] * len(sources),
        out_specs=in_vmem(len(outs)),
        scratch_shapes=[pltpu.VMEM(one.shape, one.dtype) for one in sources]
        + [pltpu.SemaphoreType.DMA((len(sources),))],
        compiler_params=params(8),
    )(*[pltpu.with_memory_space_constraint(one, pltpu.HBM) for one in sources])


def first_pack_kernel(*refs, slot_rows):
    sent, came, weights_ref, outs = refs[:3], refs[3:6], refs[6], refs[7:]
    rows = sent[0].shape[0]
    third = weights_ref.shape[1] // 3
    for at in range(3):
        outs[at][:rows, :] = sent[at][...]
        outs[at][rows : 2 * rows, :] = came[at][...]
        put_packed(outs[at], 2 * rows, weights_ref, at * third, third, slot_rows)


def second_pack_kernel(*refs, rows, slot_rows, cuts):
    second_ref, outs = refs[6], refs[7:]
    for at in range(3):
        sent_ref, came_ref, out_ref = refs[2 * at], refs[2 * at + 1], outs[at]
        tail = sent_ref.shape[0] - rows
        out_ref[:rows, :] = sent_ref[:rows, :]
        out_ref[rows : 2 * rows, :] = came_ref[:rows, :]
        out_ref[2 * rows : 2 * rows + tail, :] = sent_ref[rows:, :]
        out_ref[2 * rows + tail : 2 * (rows + tail), :] = came_ref[rows:, :]
        put_packed(out_ref, 2 * (rows + tail), second_ref, cuts[at], cuts[at + 1] - cuts[at], slot_rows)


def third_pack_kernel(*refs, masks, rows, tail):
    out_ref = refs[6]
    columns = refs[0].shape[1]
    for at in range(3):
        tokens = len(masks[2 * at]) * rows
        for side in range(2):
            piece, target = refs[2 * at + side], refs[7 + at]
            for slot, mask in enumerate(masks[2 * at + side]):
                out_ref[mask * rows : (mask + 1) * rows, at * columns : (at + 1) * columns] = piece[
                    slot * rows : (slot + 1) * rows, :
                ]
            target[side * tail : (side + 1) * tail, :] = piece[tokens : tokens + tail, :]
            rest = piece.shape[0] - tokens - tail
            base = 2 * tail + side * rest
            target[base : base + rest, :] = piece[tokens + tail :, :]


def fourth_pack_kernel(*refs, skip):
    for at in range(3):
        rest = refs[2 * at].shape[0] - skip
        for side in range(2):
            refs[6 + at][side * rest : (side + 1) * rest, :] = refs[2 * at + side][skip:, :]


def place_packed_kernel(owner_ref, *refs, plan, slot_rows, rows):
    pieces, outs = refs[: len(plan)], refs[len(plan) :]
    for piece, (masks, units) in zip(pieces, plan):
        size = packed_rows(slot_rows, len(units) * PAIR)
        for slot, mask in enumerate(masks):
            for far in range(2):
                lines = pl.ds(pl.multiple_of(owner_ref[mask * 2 + far] * rows, rows), rows)
                unit = 0
                while unit < len(units):
                    out, column = units[unit]
                    base = slot * size + unit // 2 * slot_rows
                    if unit + 1 == len(units) and unit % 2 == 0:
                        outs[out][lines, column : column + PAIR] = piece[
                            base : base + rows, far * PAIR : (far + 1) * PAIR
                        ]
                        unit += 1
                        continue
                    base += far * rows
                    if unit % 2 == 0 and units[unit + 1] == (out, column + PAIR):
                        outs[out][lines, column : column + LANES] = piece[base : base + rows, :]
                        unit += 2
                        continue
                    side = unit % 2 * PAIR
                    outs[out][lines, column : column + PAIR] = piece[base : base + rows, side : side + PAIR]
                    unit += 1


def place_packed(owner, pieces, plan, widths, rows):
    blocks = owner.shape[0]
    far_count = blocks // 8
    slot_rows = far_count * rows
    outs = [shaped((blocks * rows, width), jnp.bfloat16) for width in widths]
    if rows % 16 == 0 and far_count == 2:
        kernel = functools.partial(place_packed_kernel, plan=plan, slot_rows=slot_rows, rows=rows)
        return local_call(kernel, outs, pieces, [owner], spare=12)
    made = [jnp.zeros(out.shape, out.dtype) for out in outs]
    for piece, (masks, units) in zip(pieces, plan):
        size = packed_rows(slot_rows, len(units) * PAIR)
        for slot, mask in enumerate(masks):
            block = unpacked(piece[slot * size : (slot + 1) * size], slot_rows)
            lines = owner.reshape(8, far_count)[mask][:, None] * rows + jnp.arange(rows, dtype=jnp.int32)
            for unit, (out, column) in enumerate(units):
                made[out] = made[out].at[lines.reshape(-1), column : column + PAIR].set(
                    block[:, unit * PAIR : (unit + 1) * PAIR]
                )
    return made


def units_of(targets):
    return tuple((out, column + at) for out, column, size in targets for at in range(0, size, PAIR))


def placed_blocks(grad, owner, masks):
    blocks = owner.shape[0]
    rows = grad.shape[0] // blocks
    spots = owner.reshape(8, -1)[jnp.array(masks)].reshape(-1)
    return jnp.take(grad.reshape(blocks, rows, grad.shape[1]), spots, axis=0)


def token_kernel(x_ref, query_weight_ref, kv_weight_ref, query_ref, kv_ref):
    rows = query_ref.shape[0]
    query_ref[...] = dot_plain(x_ref[:rows, :], query_weight_ref[...]).astype(jnp.bfloat16)
    step = 512
    for start in range(0, kv_ref.shape[0], step):
        kv_ref[start : start + step, :] = dot_plain(x_ref[start : start + step, :], kv_weight_ref[...]).astype(
            jnp.bfloat16
        )


def project_kernel(mixed_ref, weight_ref, counts_ref, own_ref, other_ref, low_ref, count_ref, *, each):
    count = jnp.sum(counts_ref[...].astype(jnp.float32), axis=0, keepdims=True) / each
    count_ref[...] = jnp.broadcast_to(count, count_ref.shape)
    low = mixed_ref[...].astype(jnp.bfloat16)
    low_ref[...] = low
    total = dot_cols(low, weight_ref[...])
    half = own_ref.shape[0]
    own_ref[...] = total[:half]
    other_ref[...] = total[half:].astype(jnp.bfloat16)


def normed_rows(values):
    centred = values - jnp.mean(values, axis=-1, keepdims=True)
    spread = jnp.mean(centred * centred, axis=-1, keepdims=True)
    scale = lax.rsqrt(spread + epsilon)
    return centred * scale, scale


def norm_back(grads, normed, scale, gain):
    inner = grads * gain
    middle = jnp.mean(inner, axis=-1, keepdims=True)
    slant = jnp.mean(inner * normed, axis=-1, keepdims=True)
    return scale * (inner - middle - normed * slant)


def first_norm_kernel(tokens_ref, own_ref, came_ref, gain_ref, shift_ref, sum_ref, hidden_ref, low_ref):
    total = tokens_ref[...].astype(jnp.float32) + (own_ref[...] + came_ref[...].astype(jnp.float32))
    sum_ref[...] = total
    normed, _ = normed_rows(total)
    hidden = normed * gain_ref[...] + shift_ref[...]
    hidden_ref[...] = hidden
    low_ref[...] = hidden.astype(jnp.bfloat16)


def feed_kernel(own_hidden_ref, other_hidden_ref, inner_ref, outer_ref, own_ref, other_ref, active_ref, slope_ref, total_ref):
    hidden = jnp.concatenate([own_hidden_ref[...], other_hidden_ref[...]], 0)
    step = 256
    for start in range(0, inner_ref.shape[1], step):
        columns = slice(start, start + step)
        upper = dot_plain(hidden, inner_ref[:, columns])
        chance = 0.5 * (1.0 + lax.erf(upper * (0.5**0.5)))
        active = (upper * chance).astype(jnp.bfloat16)
        active_ref[:, columns] = active
        slope_ref[:, columns] = chance + upper * (jnp.exp(-0.5 * upper * upper) * 0.3989422804014327)
        part = dot_cols(active, outer_ref[:, columns])
        if start:
            total_ref[...] += part
        else:
            total_ref[...] = part
    half = own_ref.shape[0]
    own_ref[...] = total_ref[:half, :]
    other_ref[...] = total_ref[half:, :].astype(jnp.bfloat16)


def second_norm_kernel(
    hidden_ref, own_ref, came_ref, gain_ref, shift_ref, teacher_ref, valid_ref, count_own_ref, count_came_ref,
    grad_ref, low_ref, stats_ref, result_ref, *, token_total
):
    valid = jnp.broadcast_to(valid_ref[...].astype(jnp.float32), (PAIR, valid_ref.shape[1])).T[:, :1]
    factor = token_total / (count_own_ref[0:1, 0:1] + count_came_ref[0:1, 0:1])
    total = hidden_ref[...] + (own_ref[...] + came_ref[...].astype(jnp.float32))
    normed, scale = normed_rows(total)
    gain = gain_ref[...]
    result = normed * gain + shift_ref[...]
    result_ref[...] = result.astype(jnp.bfloat16)
    errors = (result - teacher_ref[...].astype(jnp.float32)) * valid
    grads = errors * factor
    grad = norm_back(grads, normed, scale, gain)
    grad_ref[...] = grad
    low_ref[...] = grad.astype(jnp.bfloat16)
    stats_ref[...] = jnp.zeros_like(stats_ref)
    stats_ref[2:3, :] = jnp.sum(grads * normed, axis=0, keepdims=True)
    stats_ref[3:4, :] = jnp.sum(grads, axis=0, keepdims=True)
    squares = jnp.sum(jnp.sum(errors * errors, axis=0, keepdims=True), axis=1, keepdims=True)
    stats_ref[4:5, :] = jnp.broadcast_to(squares, (1, stats_ref.shape[1]))


def feed_back_kernel(own_grad_ref, other_grad_ref, slope_ref, inner_ref, outer_ref, upper_ref, own_ref, other_ref, total_ref):
    grads = jnp.concatenate([own_grad_ref[...], other_grad_ref[...]], 0)
    step = 256
    for start in range(0, inner_ref.shape[1], step):
        columns = slice(start, start + step)
        upper = (dot_plain(grads, outer_ref[:, columns]) * slope_ref[:, columns]).astype(jnp.bfloat16)
        upper_ref[:, columns] = upper
        part = dot_cols(upper, inner_ref[:, columns])
        if start:
            total_ref[...] += part
        else:
            total_ref[...] = part
    half = own_ref.shape[0]
    own_ref[...] = total_ref[:half, :]
    other_ref[...] = total_ref[half:, :].astype(jnp.bfloat16)


def first_back_kernel(
    grad_ref, own_ref, came_ref, sum_ref, gain_ref, other_stats_ref, out_ref, low_ref, stats_ref
):
    grads = grad_ref[...] + (own_ref[...] + came_ref[...].astype(jnp.float32))
    normed, scale = normed_rows(sum_ref[...])
    grad = norm_back(grads, normed, scale, gain_ref[...])
    out_ref[...] = grad
    low_ref[...] = grad.astype(jnp.bfloat16)
    stats_ref[...] = other_stats_ref[...]
    stats_ref[0:1, :] = jnp.sum(grads * normed, axis=0, keepdims=True)
    stats_ref[1:2, :] = jnp.sum(grads, axis=0, keepdims=True)


def write_blocks(owner_ref, made_ref, column, width, out_ref, out_column, masks, far_count, rows):
    for slot, mask in enumerate(masks):
        for far in range(far_count):
            start = pl.multiple_of(owner_ref[mask * far_count + far] * rows, rows)
            out_ref[slot * far_count + far, :, out_column : out_column + width] = made_ref[
                pl.ds(start, rows), column : column + width
            ].astype(out_ref.dtype)


def wide_kernel(
    owner_ref, own_grad_ref, other_grad_ref, active_ref, own_hidden_ref, other_hidden_ref, upper_ref, *refs,
    groups, far_count, rows, step
):
    outs, made_ref = refs[:-1], refs[-1]
    grads = jnp.concatenate([own_grad_ref[...], other_grad_ref[...]], 0)
    hidden = jnp.concatenate([own_hidden_ref[...], other_hidden_ref[...]], 0)
    width = active_ref.shape[1]
    third_width = 2 * width // 3
    for start in range(0, 2 * width, step):
        if start < width:
            made_ref[...] = dot_rows(grads, active_ref[:, start : start + step])
        else:
            made_ref[...] = dot_rows(hidden, upper_ref[:, start - width : start - width + step])
        third = start // third_width
        for at, masks in enumerate(groups[third]):
            write_blocks(
                owner_ref, made_ref, 0, step, outs[third * len(groups[third]) + at], start % third_width,
                masks, far_count, rows
            )


def wide_gradients(owner, own_grad, other_grad, active, own_hidden, other_hidden, upper, groups):
    blocks = owner.shape[0]
    far_count, rows = blocks // 8, own_grad.shape[1] // blocks
    width = active.shape[1]
    third_width = 2 * width // 3
    if rows % 16:
        made = jnp.concatenate(
            [
                dot_rows(jnp.concatenate([own_grad, other_grad], 0), active),
                dot_rows(jnp.concatenate([own_hidden, other_hidden], 0), upper),
            ],
            1,
        )
        outs = []
        for third, group in enumerate(groups):
            columns = made[:, third * third_width : (third + 1) * third_width]
            for at, masks in enumerate(group):
                outs.append(placed_blocks(columns, owner, masks).astype(jnp.bfloat16 if at else jnp.float32))
        return outs
    step = 512
    outs = []
    for group in groups:
        for at, masks in enumerate(group):
            outs.append(
                shaped((len(masks) * far_count, rows, third_width), jnp.bfloat16 if at else jnp.float32)
            )
    kernel = functools.partial(wide_kernel, groups=groups, far_count=far_count, rows=rows, step=step)
    return local_call(
        kernel, outs, [own_grad, other_grad, active, own_hidden, other_hidden, upper], [owner],
        [pltpu.VMEM((own_grad.shape[1], step), jnp.float32)],
        flops=8 * own_grad.size * width, spare=12,
    )


def narrow_kernel(
    own_ref, other_ref, kv_grad_ref, query_grad_ref, own_grad_ref, other_grad_ref, low_ref, made_ref
):
    half, near = own_ref.shape[0], own_grad_ref.shape[0]
    width = query_grad_ref.shape[1]
    made_ref[:, :width] = dot_rows(own_ref[:near, :], query_grad_ref[:near, :]) + dot_rows(
        other_ref[:near, :], query_grad_ref[near:, :]
    )
    made_ref[:, width : 2 * width] = dot_rows(own_grad_ref[...], low_ref[:near, :]) + dot_rows(
        other_grad_ref[...], low_ref[near:, :]
    )
    made_ref[:, 2 * width :] = dot_rows(own_ref[...], kv_grad_ref[:half, :])
    made_ref[:, 2 * width :] += dot_rows(other_ref[...], kv_grad_ref[half:, :])


def narrow_gradients(own, other, kv_grad, query_grad, own_grad, other_grad, low):
    width = query_grad.shape[1]
    return local_call(
        narrow_kernel, [shaped((own.shape[1], 4 * width))],
        [own, other, kv_grad, query_grad, own_grad, other_grad, low],
        flops=4 * own.size * 2 * width + 8 * own_grad.size * width, spare=12,
    )[0]


def token_other_kernel(kv_grad_ref, query_grad_ref, kv_weight_ref, query_weight_ref, out_ref):
    near, half = query_grad_ref.shape[0] // 2, kv_grad_ref.shape[0] // 2
    for start in range(0, half, near):
        total = dot_cols(kv_grad_ref[half + start : half + start + near, :], kv_weight_ref[...])
        if start == 0:
            total += dot_cols(query_grad_ref[near:, :], query_weight_ref[...])
        out_ref[start : start + near, :] = total.astype(jnp.bfloat16)


def token_other(kv_grad, query_grad, kv_weight, query_weight):
    return local_call(
        token_other_kernel, [shaped((kv_grad.shape[0] // 2, kv_weight.shape[0]), jnp.bfloat16)],
        [kv_grad, query_grad, kv_weight, query_weight],
        flops=kv_grad.size * kv_weight.shape[0], spare=12,
    )[0]


def small_kernel(own_ref, came_ref, out_ref):
    lines = own_ref[...] + came_ref[...]
    out_ref[...] = jnp.concatenate([lines, jnp.zeros((PAIR - lines.shape[0], lines.shape[1]), jnp.float32)], 0).T


def token_own_kernel(
    owner_ref, kv_grad_ref, query_grad_ref, kv_weight_ref, query_weight_ref, came_ref, made_ref, small_ref, *outs,
    masks, rows, placed
):
    near = query_grad_ref.shape[0] // 2
    half, columns = outs[0].shape[0], outs[0].shape[2]
    slot_rows = made_ref.shape[1] if placed else made_ref.shape[0] // (2 * half)
    for mask in range(2 * half):
        lines = slice(mask * near, (mask + 1) * near)
        total = dot_cols(kv_grad_ref[lines, :], kv_weight_ref[...]) + came_ref[lines, :].astype(jnp.float32)
        if mask == 0:
            total += dot_cols(query_grad_ref[:near, :], query_weight_ref[...])
        for third, order in enumerate(masks):
            slot = order.index(mask)
            out_ref = outs[2 * third + slot // half]
            at = slot % half
            out_ref[at, :near, :] = total[:, third * columns : (third + 1) * columns].astype(out_ref.dtype)
            for side in range(2):
                base = near + side * slot_rows
                part = slice((2 * third + side) * columns, (2 * third + side + 1) * columns)
                if placed:
                    out_ref[at, base : base + slot_rows, :] = made_ref[mask, :, part].astype(out_ref.dtype)
                    continue
                for far in range(slot_rows // rows):
                    start = pl.multiple_of(owner_ref[mask * (slot_rows // rows) + far] * rows, rows)
                    out_ref[at, base + far * rows : base + (far + 1) * rows, :] = made_ref[
                        pl.ds(start, rows), part
                    ].astype(out_ref.dtype)
            if third == 0:
                if placed:
                    small = small_ref[mask]
                else:
                    far_count = slot_rows // rows
                    small = jnp.concatenate(
                        [
                            small_ref[pl.ds(pl.multiple_of(owner_ref[mask * far_count + far] * rows, rows), rows), :]
                            for far in range(far_count)
                        ],
                        0,
                    )
                small = jnp.concatenate([small[: slot_rows // 2], small[slot_rows // 2 :]], 1)
                if slot >= half:
                    small = in_pieces(small)
                out_ref[at, near + 2 * slot_rows :, :] = small.astype(out_ref.dtype)


def token_own(owner, kv_grad, query_grad, kv_weight, query_weight, came, made, small, masks):
    near = query_grad.shape[0] // 2
    half = came.shape[0] // near // 2
    blocks, features = owner.shape[0], made.shape[0]
    rows, slot_rows = features // blocks, features // (2 * half)
    columns = kv_weight.shape[0] // 3
    placed = rows % 16 != 0
    if placed:
        made, small = (
            placed_blocks(one, owner, tuple(range(2 * half))).reshape(2 * half, slot_rows, one.shape[1])
            for one in (made, small)
        )
    outs = []
    for third in range(len(masks)):
        shape = (half, near + 2 * slot_rows + (slot_rows // 2 if third == 0 else 0), columns)
        outs += [shaped(shape), shaped(shape, jnp.bfloat16)]
    outs = local_call(
        functools.partial(token_own_kernel, masks=masks, rows=rows, placed=placed), outs,
        [kv_grad, query_grad, kv_weight, query_weight, came, made, small], [owner],
        flops=2 * came.shape[0] * kv_weight.size, spare=12,
    )
    return list(outs[::2]), list(outs[1::2])


def last_kernel(grad_ref, *refs):
    token_ref, made_ref = refs[-1], refs[6]
    near, columns = grad_ref.shape[0], refs[0].shape[2]
    slot_rows = made_ref.shape[0]
    width = 6 * columns
    for third in range(3):
        plain = near + 2 * slot_rows
        total = refs[2 * third][0, :plain] + refs[2 * third + 1][0, :plain].astype(jnp.float32)
        if third == 0:
            small = refs[0][0, plain:] + from_pieces(refs[1][0, plain:].astype(jnp.float32))
            made_ref[: slot_rows // 2, width:] = small[:, :PAIR]
            made_ref[slot_rows // 2 :, width:] = small[:, PAIR:]
        part = slice(third * columns, (third + 1) * columns)
        token_ref[:, part] = grad_ref[:, part] + total[:near]
        for side in range(2):
            at = (2 * third + side) * columns
            made_ref[:, at : at + columns] = total[near + side * slot_rows : near + (side + 1) * slot_rows]
    if len(refs) > 8:
        send_ref = refs[7]
        half = slot_rows // 2
        send_ref[:, :width] = made_ref[half:, :width].astype(jnp.bfloat16)
        send_ref[:, width:] = in_pieces(made_ref[half:, width:]).astype(jnp.bfloat16)


def end_kernel(made_ref, came_ref, query_ref, key_ref, value_ref, output_ref, small_ref):
    rows, width = query_ref.shape
    total = made_ref[:rows, : 4 * width] + came_ref[:, : 4 * width].astype(jnp.float32)
    query_ref[...] = total[:, :width]
    output_ref[...] = total[:, width : 2 * width]
    for at in range(0, width, PAIR):
        first = 2 * width + 2 * at
        key_ref[:, at : at + PAIR] = total[:, first : first + PAIR]
        value_ref[:, at : at + PAIR] = total[:, first + PAIR : first + 2 * PAIR]
    small_ref[...] = made_ref[:rows, 4 * width :] + from_pieces(came_ref[:, 4 * width :].astype(jnp.float32))


def wide_end_kernel(*refs):
    out_ref = refs[6]
    columns = refs[0].shape[2]
    for third in range(3):
        out_ref[:, third * columns : (third + 1) * columns] = refs[2 * third][0] + refs[2 * third + 1][0].astype(
            jnp.float32
        )
    if len(refs) > 7:
        refs[7][...] = out_ref[out_ref.shape[0] // 2 :, :].astype(jnp.bfloat16)


def wide_out_kernel(made_ref, came_ref, outer_ref, inner_ref):
    rows, width = outer_ref.shape
    outer_ref[...] = made_ref[:rows, :width] + came_ref[:, :width].astype(jnp.float32)
    inner_ref[...] = made_ref[:rows, width:] + came_ref[:, width:].astype(jnp.float32)


def tie(first, second):
    leaves, tree = jax.tree.flatten(second)
    tied = lax.optimization_barrier(tuple(leaves) + (first,))
    return jax.tree.unflatten(tree, tied[:-1])


def shards(
    tokens,
    query_weight,
    key_weight,
    value_weight,
    output_weight,
    inner_weight,
    outer_weight,
    attn_gain,
    attn_shift,
    ffn_gain,
    ffn_shift,
    teacher,
    segments,
    random_blocks,
    valid_tokens,
):
    devices = lax.axis_size("dp")
    dp_index = lax.axis_index("dp")
    core = lax.axis_index("tensor")
    rows, width = tokens.shape
    length = 2 * rows
    span = segments.shape[1] // length
    near_bits = span.bit_length() - 1
    far_bits = tuple(range(near_bits, devices.bit_length() - 1))
    place, far_place = dp_index % span, dp_index // span
    far_count = devices // span
    each = width // devices
    slot_rows = far_count * each
    head_width = query_weight.shape[1]
    wide = inner_weight.shape[1]
    masks = jnp.arange(span, dtype=jnp.int32)
    fars = jnp.arange(far_count, dtype=jnp.int32)
    owner = ((fars[None, :] ^ far_place) * span + (masks[:, None] ^ place)).reshape(-1)

    def far_gather(block):
        held = block[None]
        for bit in far_bits:
            held = jnp.concatenate([held, swap_mask(held, 1 << bit)], 0)
        return held.reshape(slot_rows, block.shape[1])

    def step(held, at):
        return [swap_mask(one, 1 << bits[at]) for one, bits in zip(held, ROUTES)]

    def both(held, came):
        return [one for pair in zip(held, came) for one in pair]

    def messages(lines):
        return [shaped((one, third), jnp.bfloat16) for one in lines]

    third = width // 3
    cut = 3 * wide // 4
    tail = packed_rows(slot_rows, head_width)
    rest = (cut, cut, 2 * (wide - cut) + head_width + PAIR)
    cuts = (0, cut, 2 * cut, 2 * cut + rest[2])
    sizes = [packed_rows(slot_rows, one) for one in rest]
    valid_row = valid_tokens.reshape(1, rows)
    first, second = fetching_call(
        functools.partial(weight_start_kernel, cut=cut),
        [shaped((each, 3 * head_width), jnp.bfloat16), shaped((each, cuts[3]), jnp.bfloat16)],
        [query_weight, key_weight, value_weight, inner_weight, outer_weight, output_weight, valid_row],
    )
    held = list(
        fetching_call(token_start_kernel, [shaped((rows, third), jnp.bfloat16)] * 3, [tie(first, tokens)])
    )
    came = step(held, 0)
    first_held, second_held = far_gather(first), far_gather(second)
    held = local_call(
        functools.partial(first_pack_kernel, slot_rows=slot_rows), messages([2 * rows + tail] * 3),
        held + came + [first_held],
    )
    came = step(held, 1)
    held = local_call(
        functools.partial(second_pack_kernel, rows=2 * rows, slot_rows=slot_rows, cuts=cuts),
        messages([4 * rows + 2 * tail + size for size in sizes]), both(held, came) + [second_held],
    )
    came = step(held, 2)
    segment_all = lax.dynamic_index_in_dim(segments, far_place, 0, keepdims=False)
    tables = attention_tables(random_blocks, segment_all, place, core, span, length // BLOCK)
    tables, owner, came = lax.optimization_barrier((tables, owner, came))
    sent_masks = [tuple(slot_masks(bits[:2])) for bits in ROUTES]
    came_masks = [tuple(mask ^ (1 << bits[2]) for mask in sent) for sent, bits in zip(sent_masks, ROUTES)]
    own, *held = local_call(
        functools.partial(third_pack_kernel, masks=tuple(both(sent_masks, came_masks)), rows=rows, tail=2 * tail),
        [shaped((span * rows, width), jnp.bfloat16)] + messages([4 * tail + 2 * size for size in sizes]),
        both(held, came),
    )
    came = step(held, 0)
    other = swap_core(own)
    late = local_call(
        functools.partial(fourth_pack_kernel, skip=4 * tail), messages([4 * size for size in sizes]),
        both(held, came),
    )
    late_came = step(late, 1)

    held, came = tie(late[0], (held, came))
    plan = []
    for bits, units in zip(
        ROUTES,
        [((0, 0, head_width),)]
        + [tuple((1, 2 * at + shift, PAIR) for at in range(0, head_width, PAIR)) for shift in (0, PAIR)],
    ):
        sent = tuple(slot_masks((bits[1], bits[2])))
        plan += [(sent, units_of(units)), (tuple(mask ^ (1 << bits[0]) for mask in sent), units_of(units))]
    full_query, full_kv = place_packed(
        owner, both(held, came), tuple(plan), (head_width, 2 * head_width), each
    )
    own_query, own_kv = local_call(
        token_kernel, [shaped((rows, head_width), jnp.bfloat16), shaped((span * rows, 2 * head_width), jnp.bfloat16)],
        [own, full_query, full_kv], flops=4 * own.size * head_width, spare=12,
    )
    mixed, mass, queries, kv = attend(tables, own_query, own_kv, other, full_query, full_kv)

    late, late_came = tie(mixed, (late, late_came))
    plan = []
    for bits, units in zip(
        ROUTES,
        (
            ((0, 0, cut),),
            ((1, 0, cut),),
            ((0, cut, wide - cut), (1, cut, wide - cut), (2, 0, head_width), (3, 0, PAIR)),
        ),
    ):
        sent = tuple(slot_masks((bits[2], bits[0])))
        plan += [(sent, units_of(units)), (tuple(mask ^ (1 << bits[1]) for mask in sent), units_of(units))]
    full_inner, full_outer, full_output, counts = place_packed(
        owner, both(late, late_came), tuple(plan), (wide, wide, head_width, PAIR), each
    )

    half_shape, low_shape = shaped((rows, width)), shaped((rows, width), jnp.bfloat16)
    gain_one, shift_one, gain_two, shift_two = (
        one.reshape(1, width) for one in (attn_gain, attn_shift, ffn_gain, ffn_shift)
    )
    count_shape = shaped((8, PAIR))
    part_own, part_other, attended, count_own = local_call(
        functools.partial(project_kernel, each=each),
        [half_shape, low_shape, shaped(mixed.shape, jnp.bfloat16), count_shape], [mixed, full_output, counts],
        flops=2 * mixed.size * width,
    )
    count_came = swap_core(count_own)
    first_sum, hidden, hidden_own = local_call(
        first_norm_kernel, [half_shape, half_shape, low_shape],
        [tokens, part_own, swap_core(part_other), gain_one, shift_one],
    )
    hidden_other = swap_core(hidden_own)
    part_own, part_other, active, slope = local_call(
        feed_kernel,
        [half_shape, low_shape, shaped((length, wide), jnp.bfloat16), shaped((length, wide))],
        [hidden_own, hidden_other, full_inner, full_outer],
        scratch=[pltpu.VMEM((length, width), jnp.float32)],
        flops=4 * length * width * wide, transcendentals=2 * length * wide, spare=12,
    )
    token_total = devices * lax.axis_size("tensor") * rows
    grad_second, grad_ffn_own, stats_two, result = local_call(
        functools.partial(second_norm_kernel, token_total=token_total),
        [half_shape, low_shape, shaped((8, width)), low_shape],
        [hidden, part_own, swap_core(part_other), gain_two, shift_two, teacher, valid_row, count_own, count_came],
        free=1,
    )
    grad_ffn_other = swap_core(grad_ffn_own)
    upper_grad, part_own, part_other = local_call(
        feed_back_kernel, [shaped((length, wide), jnp.bfloat16), half_shape, low_shape],
        [grad_ffn_own, grad_ffn_other, slope, full_inner, full_outer],
        scratch=[pltpu.VMEM((length, width), jnp.float32)],
        flops=4 * length * width * wide, spare=12,
    )
    part_came = swap_core(part_other)
    scatter_masks = tuple(tuple(slot_masks(bits[::-1])) for bits in ROUTES)
    groups = tuple((one[: span // 2], one[span // 2 :]) for one in scatter_masks)
    outs = wide_gradients(
        owner, grad_ffn_own, grad_ffn_other, active, hidden_own, hidden_other, upper_grad, groups
    )
    outs = [one.reshape(span // 2, slot_rows, one.shape[2]) for one in outs]
    wide_keep, wide_came = outs[::2], step(outs[1::2], 0)
    part_came = tie(outs[0], part_came)
    grad_first, grad_attn_own, stats_one = local_call(
        first_back_kernel, [half_shape, low_shape, shaped((8, width))],
        [grad_second, part_own, part_came, first_sum, gain_one, stats_two],
    )
    grad_attn_other = swap_core(grad_attn_own)
    stats_came = swap_core(stats_one)
    query_grad, kv_grad = attend_back(
        tables, queries, kv, mixed, mass, grad_attn_own, grad_attn_other, full_output
    )

    def folded(keep, came):
        return fold(keep, [[one] for one in came])

    small = local_call(small_kernel, [shaped((width, PAIR))], [stats_one, tie(query_grad, stats_came)])[0]
    wide_keep, wide_send = folded(wide_keep, tie(small, wide_came))
    wide_came = step(wide_send, 1)
    token_sent = token_other(tie(wide_keep[0], kv_grad), query_grad, full_kv, full_query)
    token_came = swap_core(token_sent)
    made = narrow_gradients(
        own, other, tie(token_sent, kv_grad), query_grad, grad_attn_own, grad_attn_other, attended
    )
    wide_keep, wide_send = folded(wide_keep, tie(made, wide_came))
    wide_came = step(wide_send, 2)
    keep, send = token_own(
        owner, kv_grad, query_grad, full_kv, full_query, tie(wide_keep[0], token_came), made, small, scatter_masks
    )
    came = step(send, 0)
    far_send = [shaped((each, 2 * wide), jnp.bfloat16)] if far_count == 2 else []
    wide_sum, *wide_send = local_call(
        wide_end_kernel, [shaped((slot_rows, 2 * wide))] + far_send, both(wide_keep, tie(keep[0], wide_came))
    )
    plain = rows + 2 * slot_rows
    keep, send = fold(keep, [[one] for one in tie(wide_sum, came)], plain)
    came = step(send, 1)

    def far_scatter(total, after=None, dtype=jnp.bfloat16):
        total = total.reshape(far_count, each, total.shape[1])
        for bit in far_bits[::-1]:
            half = total.shape[0] // 2
            came = swap_mask(total[half:].astype(dtype), 1 << bit)
            if after is not None:
                came, total = tie(after, (came, total))
            total = total[:half] + came.astype(jnp.float32)
        return total[0]

    keep, send = fold(keep, [[one] for one in came], plain)
    came = step(send, 2)
    made_shape = shaped((slot_rows, 4 * head_width + PAIR))
    send_shape = [shaped((each, 4 * head_width + PAIR), jnp.bfloat16)] if far_count == 2 else []
    *made, grad_tokens = local_call(
        last_kernel, [made_shape] + send_shape + [half_shape], [grad_first] + both(keep, came), free=1
    )
    made, send = made[0], made[1:]
    if far_count == 2:
        weight_shape = shaped((each, head_width))
        part_query, part_key, part_value, part_output, small = local_call(
            end_kernel, [weight_shape] * 4 + [shaped((each, PAIR))], [made, swap_mask(send[0], 1 << far_bits[0])],
            free=5,
        )
    else:
        narrow_sum = far_scatter(made[:, : 4 * head_width])
        small = far_scatter(made[:, 4 * head_width :], None, jnp.float32)
        part_query, part_output = narrow_sum[:, :head_width], narrow_sum[:, head_width : 2 * head_width]
        kv_sum = narrow_sum[:, 2 * head_width :].reshape(each, head_width // PAIR, 2, PAIR)
        part_key, part_value = (kv_sum[:, :, one].reshape(each, head_width) for one in range(2))
    if far_count == 2:
        wide_came = swap_mask(wide_send[0], 1 << far_bits[0])
        part_outer, part_inner = local_call(
            wide_out_kernel, [shaped((each, wide))] * 2, [wide_sum, tie(grad_tokens, wide_came)], free=2
        )
    else:
        wide_sum = far_scatter(wide_sum, grad_tokens)
        part_outer, part_inner = wide_sum[:, :wide], wide_sum[:, wide:]
    loss_value = small[0, 4] / (2.0 * width * (count_own[0, 0] + count_came[0, 0]))
    half = each // 2
    mine = jnp.where(core == 0, small[:half], small[half:])
    return (
        result,
        loss_value,
        grad_tokens,
        part_query,
        part_key,
        part_value,
        part_output,
        part_inner,
        part_outer,
        mine[:, 0],
        mine[:, 1],
        mine[:, 2],
        mine[:, 3],
    )


def solution(mesh):
    both = P(("dp", "tensor"))
    rows_spec = P(("dp", "tensor"), None)
    weight_spec = P("dp", "tensor")
    in_specs = (rows_spec,) + (weight_spec,) * 6 + (P(),) * 4
    in_specs += (rows_spec, P(), P("tensor", None, None), both)
    out_specs = (rows_spec, P(), rows_spec) + (weight_spec,) * 6 + (both,) * 4
    return jax.shard_map(shards, mesh=mesh, in_specs=in_specs, out_specs=out_specs, check_vma=False)
```

profile of v0, /device:TPU:0, one launch (start us, length us, event | category | flops | bytes accessed | tf_op | source)
XLA Modules:
  0.0 241.4 jit_solution(7830541617687536599)
XLA Ops:
  1.9 4.1 %collective-permute-start.3 = (bf16[1,48,1152]{2,1,0:T(8,128)(2,1)S(1)}, bf16[1,48,1152]{2,1,0:T(8,128)(2,1)S(1)}, u32[]{:S(2)}, u32[]{:S(2)}) collective-permute-start(bf16[1,48,1152]{2,1,0:T(8,128)(2,1)S(1)} %bitcast.51), channel_id=1, source_target_pairs={{0,16},{2,18},{4,20},{6,22},{8,24},{10,26},{12,28},{14,30},{16,0},... | collective-permute-start | bytes 331784 | tf_op jit(solution)/shard_map/ppermute | solution.py:23
  19.3 9.4 %collective-permute-done.7 = bf16[1,48,3584]{2,1,0:T(8,128)(2,1)S(1)} collective-permute-done((bf16[1,48,3584]{2,1,0:T(8,128)(2,1)S(1)}, bf16[1,48,3584]{2,1,0:T(8,128)(2,1)S(1)}, u32[]{:S(2)}, u32[]{:S(2)}) %collective-permute-start.7) | collective-permute-done | bytes 344096 | tf_op jit(solution)/shard_map/ppermute | solution.py:23
  28.8 2.8 %collective-permute-done.5.refs_3_ = bf16[656,256]{1,0:T(8,128)(2,1)S(1)} collective-permute-done((bf16[656,256]{1,0:T(8,128)(2,1)S(1)}, bf16[656,256]{1,0:T(8,128)(2,1)S(1)}, u32[]{:S(2)}, u32[]{:S(2)}) %collective-permute-start.5) | collective-permute-done | bytes 335904 | tf_op jit(solution)/shard_map/ppermute | solution.py:23
  37.0 17.0 %collective-permute-done.8.refs_1_ = bf16[1744,256]{1,0:T(8,128)(2,1)} collective-permute-done((bf16[1744,256]{1,0:T(8,128)(2,1)S(1)}, bf16[1744,256]{1,0:T(8,128)(2,1)}, u32[]{:S(2)}, u32[]{:S(2)}) %collective-permute-start.8) | collective-permute-done | bytes 892960 | tf_op jit(solution)/shard_map/ppermute | solution.py:23
  60.6 16.5 %collective-permute-done.11.refs_1_ = bf16[1440,256]{1,0:T(8,128)(2,1)S(1)} collective-permute-done((bf16[1440,256]{1,0:T(8,128)(2,1)S(1)}, bf16[1440,256]{1,0:T(8,128)(2,1)S(1)}, u32[]{:S(2)}, u32[]{:S(2)}) %collective-permute-start.11) | collective-permute-done | bytes 737312 | tf_op jit(solution)/shard_map/ppermute | solution.py:23
  81.6 2.8 %shard_map.253 = (bf16[256,384]{1,0:T(8,128)(2,1)S(1)}, bf16[2048,768]{1,0:T(8,128)(2,1)S(1)}) custom-call(bf16[2048,768]{1,0:T(8,128)(2,1)S(1)} %get-tuple-element.170.x_ref.own_ref, bf16[768,384]{1,0:T(8,128)(2,1)S(1)} %get-tuple-element.182.query_weight_ref, bf16[768,768]{1,0:T(8,128)(2,1)S(1)} %get-tuple-element.183.kv_weight_ref), custom_call_target="tpu_custom_call" | custom-call | flops 1000 | bytes 1000 | tf_op jit(solution)/shard_map/pallas_call | solution.py:70
  84.4 9.4 %shard_map.254 = (f32[512,384]{1,0:T(8,128)S(1)}, f32[24,8,128]{2,1,0:T(8,128)S(1)}, bf16[512,384]{1,0:T(8,128)(2,1)S(1)}, bf16[4096,768]{1,0:T(8,128)(2,1)S(1)}) custom-call(s32[501]{0:T(512)S(1)} %pad_add_fusion.numbers_ref, f32[8,128]{1,0:T(8,128)S(1)} %pad_maximum_fusion.3.query_side_ref, f32[4096,128]{1,0:T(8,128)S(1)} %broadcast_in_dim.143.key_side_ref, ...), custom_call_target="tpu_custom_call" | custom-call | flops 1000 | bytes 1000 | tf_op jit(solution)/shard_map/pallas_call | solution.py:70
  93.8 5.6 %collective-permute-done.15.refs_1_ = bf16[1728,256]{1,0:T(8,128)(2,1)S(1)} collective-permute-done((bf16[1728,256]{1,0:T(8,128)(2,1)S(1)}, bf16[1728,256]{1,0:T(8,128)(2,1)S(1)}, u32[]{:S(2)}, u32[]{:S(2)}) %collective-permute-start.15) | collective-permute-done | bytes 884768 | tf_op jit(solution)/shard_map/ppermute | solution.py:23
  106.1 3.2 %shard_map.258 = (f32[256,768]{1,0:T(8,128)S(1)}, bf16[256,768]{1,0:T(8,128)(2,1)S(1)}, bf16[512,1536]{1,0:T(8,128)(2,1)S(1)}, f32[512,1536]{1,0:T(8,128)S(1)}) custom-call(bf16[256,768]{1,0:T(8,128)(2,1)S(1)} %get-tuple-element.200.own_hidden_ref, bf16[256,768]{1,0:T(8,128)(2,1)S(1)} %collective-permute-done.19.other_hidden_ref, ...), custom_call_target="tpu_custom_call" | custom-call | flops 1000 | bytes 1000 | tf_op jit(solution)/shard_map/pallas_call | solution.py:70
  114.3 3.0 %shard_map.260 = (bf16[512,1536]{1,0:T(8,128)(2,1)S(1)}, f32[256,768]{1,0:T(8,128)S(1)}, bf16[256,768]{1,0:T(8,128)(2,1)S(1)}) custom-call(bf16[256,768]{1,0:T(8,128)(2,1)S(1)} %get-tuple-element.208.own_grad_ref, bf16[256,768]{1,0:T(8,128)(2,1)S(1)} %collective-permute-done.22.other_grad_ref, f32[512,1536]{1,0:T(8,128)S(1)} %get-tuple-element.209.slope_ref, ...), custom_call_target="tpu_custom_call" | custom-call | flops 1000 | bytes 1000 | tf_op jit(solution)/shard_map/pallas_call | solution.py:70
  117.5 3.5 %shard_map.261 = (f32[8,48,1024]{2,1,0:T(8,128)S(1)}, bf16[8,48,1024]{2,1,0:T(8,128)(2,1)S(1)}, f32[8,48,1024]{2,1,0:T(8,128)S(1)}, bf16[8,48,1024]{2,1,0:T(8,12...) custom-call(s32[16]{0:T(128)S(1)} %add.233.owner_ref, ...), custom_call_target="tpu_custom_call" | custom-call | flops 1000 | bytes 1000 | tf_op jit(solution)/shard_map/pallas_call | solution.py:70
  127.0 22.3 %shard_map.263 = (bf16[512,384]{1,0:T(8,128)(2,1)S(1)}, bf16[4096,768]{1,0:T(8,128)(2,1)S(1)}) custom-call(s32[501]{0:T(512)S(1)} %pad_add_fusion.numbers_ref, f32[8,128]{1,0:T(8,128)S(1)} %pad_maximum_fusion.3.query_side_ref, f32[4096,128]{1,0:T(8,128)S(1)} %broadcast_in_dim.143.key_side_ref, bf16[512,384]{1,0:T(8,128)(2,1)S(1)} %get-tuple-element.219.q_ref, ...), custom_call_target="tpu_custom_call" | custom-call | flops 1000 | bytes 1000 | tf_op jit(solution)/shard_map/pallas_call | solution.py:70
  150.0 2.8 %shard_map.266 = bf16[2048,768]{1,0:T(8,128)(2,1)S(1)} custom-call(bf16[4096,768]{1,0:T(8,128)(2,1)S(1)} %get-tuple-element.240.kv_grad_ref, bf16[512,384]{1,0:T(8,128)(2,1)S(1)} %get-tuple-element.224.query_grad_ref, bf16[768,768]{1,0:T(8,128)(2,1)S(1)} %get-tuple-element.183.kv_weight_ref, bf16[768,384]{1,0:T(8,128)(2,1)S(1)} %get-tuple-element.182.query_weight_ref), custom_call_target="tpu_custom_call" | custom-call | flops 1000 | bytes 1000 | tf_op jit(solution)/shard_map/pallas_call | solution.py:70
  155.7 5.9 %shard_map.267.made_ref = f32[768,1536]{1,0:T(8,128)S(1)} custom-call(bf16[2048,768]{1,0:T(8,128)(2,1)S(1)} %get-tuple-element.170.x_ref.own_ref, bf16[2048,768]{1,0:T(8,128)(2,1)S(1)} %collective-permute-done.14.other_ref, bf16[4096,768]{1,0:T(8,128)(2,1)S(1)} %get-tuple-element.240.kv_grad_ref, bf16[512,384]{1,0:T(8,128)(2,1)S(1)} %get-tuple-element.224.query_grad_ref, ...), custom_call_target="tpu_custom_call" | custom-call | flops 1000 | bytes 1000 | tf_op jit(solution)/shard_map/pallas_call | solution.py:70
  161.6 3.5 %collective-permute-done.30.refs_1_ = bf16[2,96,1024]{2,1,0:T(8,128)(2,1)S(1)} collective-permute-done((bf16[2,96,1024]{2,1,0:T(8,128)(2,1)S(1)}, bf16[2,96,1024]{2,1,0:T(8,128)(2,1)S(1)}, u32[]{:S(2)}, u32[]{:S(2)}) %collective-permute-start.30) | collective-permute-done | bytes 393248 | tf_op jit(solution)/shard_map/ppermute | solution.py:23
  166.4 3.5 %shard_map.269 = (f32[4,496,256]{2,1,0:T(8,128)S(1)}, bf16[4,496,256]{2,1,0:T(8,128)(2,1)S(1)}, f32[4,448,256]{2,1,0:T(8,128)S(1)}, bf16[4,448,256]{2,1,0:T(8,12...) custom-call(s32[16]{0:T(128)S(1)} %add.233.owner_ref, ...), custom_call_target="tpu_custom_call" | custom-call | flops 1000 | bytes 1000 | tf_op jit(solution)/shard_map/pallas_call | solution.py:70
  174.8 21.7 %collective-permute-done.36.refs_1_ = bf16[1,96,1024]{2,1,0:T(8,128)(2,1)S(1)} collective-permute-done((bf16[1,96,1024]{2,1,0:T(8,128)(2,1)S(1)}, bf16[1,96,1024]{2,1,0:T(8,128)(2,1)S(1)}, u32[]{:S(2)}, u32[]{:S(2)}) %collective-permute-start.36) | collective-permute-done | bytes 196640 | tf_op jit(solution)/shard_map/ppermute | solution.py:23
  197.6 4.6 %collective-permute-done.38.refs_5_ = bf16[1,96,1024]{2,1,0:T(8,128)(2,1)S(1)} collective-permute-done((bf16[1,96,1024]{2,1,0:T(8,128)(2,1)S(1)}, bf16[1,96,1024]{2,1,0:T(8,128)(2,1)S(1)}, u32[]{:S(2)}, u32[]{:S(2)}) %collective-permute-start.38) | collective-permute-done | bytes 196640 | tf_op jit(solution)/shard_map/ppermute | solution.py:23
  207.2 5.9 %collective-permute-done.40.refs_3_ = bf16[2,448,256]{2,1,0:T(8,128)(2,1)S(1)} collective-permute-done((bf16[2,448,256]{2,1,0:T(8,128)(2,1)S(1)}, bf16[2,448,256]{2,1,0:T(8,128)(2,1)S(1)}, u32[]{:S(2)}, u32[]{:S(2)}) %collective-permute-start.40) | collective-permute-done | bytes 458784 | tf_op jit(solution)/shard_map/ppermute | solution.py:23
  213.1 2.2 collective-permute-done.41.refs_5_
  215.8 2.1 collective-permute-start.43
  218.3 5.4 %collective-permute-start.46 = (bf16[48,3072]{1,0:T(8,128)(2,1)S(1)}, bf16[48,3072]{1,0:T(8,128)(2,1)S(1)}, u32[]{:S(2)}, u32[]{:S(2)}) collective-permute-start(bf16[48,3072]{1,0:T(8,128)(2,1)S(1)} %get-tuple-element.287), channel_id=1, source_target_pairs={{0,16},{2,18},{4,20},{6,22},{8,24},{10,26},{12,28},{14,30},{16,0},... | collective-permute-start | bytes 884744 | tf_op jit(solution)/shard_map/ppermute | solution.py:23
  225.1 5.1 %collective-permute-start.45 = (bf16[48,1664]{1,0:T(8,128)(2,1)S(1)}, bf16[48,1664]{1,0:T(8,128)(2,1)S(1)}, u32[]{:S(2)}, u32[]{:S(2)}) collective-permute-start(bf16[48,1664]{1,0:T(8,128)(2,1)S(1)} %get-tuple-element.280), channel_id=1, source_target_pairs={{0,16},{2,18},{4,20},{6,22},{8,24},{10,26},{12,28},{14,30},{16,0},... | collective-permute-start | bytes 479240 | tf_op jit(solution)/shard_map/ppermute | solution.py:23
  232.5 3.2 %collective-permute-done.46.came_ref = bf16[48,3072]{1,0:T(8,128)(2,1)S(1)} collective-permute-done((bf16[48,3072]{1,0:T(8,128)(2,1)S(1)}, bf16[48,3072]{1,0:T(8,128)(2,1)S(1)}, u32[]{:S(2)}, u32[]{:S(2)}) %collective-permute-start.46) | collective-permute-done | bytes 294944 | tf_op jit(solution)/shard_map/ppermute | solution.py:23
  (180 shorter events, 71.4 us)
Async XLA Ops:
  1.9 14.8 %collective-permute-start.3 = (bf16[1,48,1152]{2,1,0:T(8,128)(2,1)S(1)}, bf16[1,48,1152]{2,1,0:T(8,128)(2,1)S(1)}, u32[]{:S(2)}, u32[]{:S(2)}) collective-permute-start(bf16[1,48,1152]{2,1,0:T(8,128)(2,1)S(1)} %bitcast.51), channel_id=1, source_target_pairs={{0,16},{2,18},{4,20},{6,22},{8,24},{10,26},{12,28},{14,30},{16,0},... | collective-permute-start | bytes 331784 | tf_op jit(solution)/shard_map/ppermute | solution.py:23
  11.7 17.0 %collective-permute-start.7 = (bf16[1,48,3584]{2,1,0:T(8,128)(2,1)S(1)}, bf16[1,48,3584]{2,1,0:T(8,128)(2,1)S(1)}, u32[]{:S(2)}, u32[]{:S(2)}) collective-permute-start(bf16[1,48,3584]{2,1,0:T(8,128)(2,1)S(1)} %bitcast.49), channel_id=1, source_target_pairs={{0,16},{2,18},{4,20},{6,22},{8,24},{10,26},{12,28},{14,30},{16,0},... | collective-permute-start | bytes 1032200 | tf_op jit(solution)/shard_map/ppermute | solution.py:23
  17.4 14.2 %collective-permute-start.5 = (bf16[656,256]{1,0:T(8,128)(2,1)S(1)}, bf16[656,256]{1,0:T(8,128)(2,1)S(1)}, u32[]{:S(2)}, u32[]{:S(2)}) collective-permute-start(bf16[656,256]{1,0:T(8,128)(2,1)S(1)} %get-tuple-element.158.refs_2_), channel_id=1, source_target_pairs={{0,8},{2,10},{4,12},{6,14},{8,0},{10,2},{12,4},{14,6},{16,24},{18,... | collective-permute-start | bytes 1007624 | tf_op jit(solution)/shard_map/ppermute | solution.py:23
  32.7 21.6 %collective-permute-start.10 = (bf16[1792,256]{1,0:T(8,128)(2,1)S(1)}, bf16[1792,256]{1,0:T(8,128)(2,1)S(1)}, u32[]{:S(2)}, u32[]{:S(2)}) collective-permute-start(bf16[1792,256]{1,0:T(8,128)(2,1)S(1)} %get-tuple-element.163.refs_4_), channel_id=1, source_target_pairs={{0,4},{2,6},{4,0},{6,2},{8,12},{10,14},{12,8},{14,10},{16,20},{18,... | collective-permute-start | bytes 2752520 | tf_op jit(solution)/shard_map/ppermute | solution.py:23
  35.2 18.8 %collective-permute-start.8 = (bf16[1744,256]{1,0:T(8,128)(2,1)S(1)}, bf16[1744,256]{1,0:T(8,128)(2,1)}, u32[]{:S(2)}, u32[]{:S(2)}) collective-permute-start(bf16[1744,256]{1,0:T(8,128)(2,1)S(1)} %get-tuple-element.161.refs_0_), channel_id=1, source_target_pairs={{0,8},{2,10},{4,12},{6,14},{8,0},{10,2},{12,4},{14,6},{16,24},{18,... | collective-permute-start | bytes 2678792 | tf_op jit(solution)/shard_map/ppermute | solution.py:23
  35.2 19.1 %collective-permute-start.9 = (bf16[1744,256]{1,0:T(8,128)(2,1)}, bf16[1744,256]{1,0:T(8,128)(2,1)}, u32[]{:S(2)}, u32[]{:S(2)}) collective-permute-start(bf16[1744,256]{1,0:T(8,128)(2,1)} %copy-done.1), channel_id=1, source_target_pairs={{0,2},{2,0},{4,6},{6,4},{8,10},{10,8},{12,14},{14,12},{16,18},{18,... | collective-permute-start | bytes 2678792 | tf_op jit(solution)/shard_map/ppermute | solution.py:23
  56.7 27.7 %collective-permute-start.14 = (bf16[2048,768]{1,0:T(8,128)(2,1)S(1)}, bf16[2048,768]{1,0:T(8,128)(2,1)S(1)}, u32[]{:S(2)}, u32[]{:S(2)}) collective-permute-start(bf16[2048,768]{1,0:T(8,128)(2,1)S(1)} %get-tuple-element.170.x_ref.own_ref), channel_id=1, source_target_pairs={{0,1},{1,0},{2,3},{3,2},{4,5},{5,4},{6,7},{7,6},{8,9},{9,8},{10,11... | collective-permute-start | bytes 9437192 | tf_op jit(solution)/shard_map/ppermute | solution.py:27
  56.8 20.8 %collective-permute-start.13 = (bf16[1536,256]{1,0:T(8,128)(2,1)S(1)}, bf16[1536,256]{1,0:T(8,128)(2,1)S(1)}, u32[]{:S(2)}, u32[]{:S(2)}) collective-permute-start(bf16[1536,256]{1,0:T(8,128)(2,1)S(1)} %get-tuple-element.180.refs_4_), channel_id=1, source_target_pairs={{0,8},{2,10},{4,12},{6,14},{8,0},{10,2},{12,4},{14,6},{16,24},{18,... | collective-permute-start | bytes 2359304 | tf_op jit(solution)/shard_map/ppermute | solution.py:23
  58.5 18.6 %collective-permute-start.11 = (bf16[1440,256]{1,0:T(8,128)(2,1)S(1)}, bf16[1440,256]{1,0:T(8,128)(2,1)S(1)}, u32[]{:S(2)}, u32[]{:S(2)}) collective-permute-start(bf16[1440,256]{1,0:T(8,128)(2,1)S(1)} %get-tuple-element.176.refs_0_), channel_id=1, source_target_pairs={{0,2},{2,0},{4,6},{6,4},{8,10},{10,8},{12,14},{14,12},{16,18},{18,... | collective-permute-start | bytes 2211848 | tf_op jit(solution)/shard_map/ppermute | solution.py:23
  59.3 18.3 %collective-permute-start.12 = (bf16[1440,256]{1,0:T(8,128)(2,1)S(1)}, bf16[1440,256]{1,0:T(8,128)(2,1)S(1)}, u32[]{:S(2)}, u32[]{:S(2)}) collective-permute-start(bf16[1440,256]{1,0:T(8,128)(2,1)S(1)} %get-tuple-element.178.refs_2_), channel_id=1, source_target_pairs={{0,4},{2,6},{4,0},{6,2},{8,12},{10,14},{12,8},{14,10},{16,20},{18,... | collective-permute-start | bytes 2211848 | tf_op jit(solution)/shard_map/ppermute | solution.py:23
  77.8 22.7 %collective-permute-start.17 = (bf16[1920,256]{1,0:T(8,128)(2,1)S(1)}, bf16[1920,256]{1,0:T(8,128)(2,1)S(1)}, u32[]{:S(2)}, u32[]{:S(2)}) collective-permute-start(bf16[1920,256]{1,0:T(8,128)(2,1)S(1)} %get-tuple-element.193.refs_4_), channel_id=1, source_target_pairs={{0,2},{2,0},{4,6},{6,4},{8,10},{10,8},{12,14},{14,12},{16,18},{18,... | collective-permute-start | bytes 2949128 | tf_op jit(solution)/shard_map/ppermute | solution.py:23
  79.1 20.3 %collective-permute-start.15 = (bf16[1728,256]{1,0:T(8,128)(2,1)S(1)}, bf16[1728,256]{1,0:T(8,128)(2,1)S(1)}, u32[]{:S(2)}, u32[]{:S(2)}) collective-permute-start(bf16[1728,256]{1,0:T(8,128)(2,1)S(1)} %get-tuple-element.189.refs_0_), channel_id=1, source_target_pairs={{0,4},{2,6},{4,0},{6,2},{8,12},{10,14},{12,8},{14,10},{16,20},{18,... | collective-permute-start | bytes 2654216 | tf_op jit(solution)/shard_map/ppermute | solution.py:23
  79.6 20.2 %collective-permute-start.16 = (bf16[1728,256]{1,0:T(8,128)(2,1)S(1)}, bf16[1728,256]{1,0:T(8,128)(2,1)S(1)}, u32[]{:S(2)}, u32[]{:S(2)}) collective-permute-start(bf16[1728,256]{1,0:T(8,128)(2,1)S(1)} %get-tuple-element.191.refs_2_), channel_id=1, source_target_pairs={{0,8},{2,10},{4,12},{6,14},{8,0},{10,2},{12,4},{14,6},{16,24},{18,... | collective-permute-start | bytes 2654216 | tf_op jit(solution)/shard_map/ppermute | solution.py:23
  121.0 28.5 %collective-permute-start.25 = (bf16[4,96,1024]{2,1,0:T(8,128)(2,1)S(1)}, bf16[4,96,1024]{2,1,0:T(8,128)(2,1)S(1)}, u32[]{:S(2)}, u32[]{:S(2)}) collective-permute-start(bf16[4,96,1024]{2,1,0:T(8,128)(2,1)S(1)} %bitcast.57), channel_id=1, source_target_pairs={{0,2},{2,0},{4,6},{6,4},{8,10},{10,8},{12,14},{14,12},{16,18},{18,... | collective-permute-start | bytes 2359304 | tf_op jit(solution)/shard_map/ppermute | solution.py:23
  122.3 27.2 %collective-permute-start.26 = (bf16[4,96,1024]{2,1,0:T(8,128)(2,1)S(1)}, bf16[4,96,1024]{2,1,0:T(8,128)(2,1)S(1)}, u32[]{:S(2)}, u32[]{:S(2)}) collective-permute-start(bf16[4,96,1024]{2,1,0:T(8,128)(2,1)S(1)} %bitcast.56), channel_id=1, source_target_pairs={{0,4},{2,6},{4,0},{6,2},{8,12},{10,14},{12,8},{14,10},{16,20},{18,... | collective-permute-start | bytes 2359304 | tf_op jit(solution)/shard_map/ppermute | solution.py:23
  122.9 26.6 %collective-permute-start.27 = (bf16[4,96,1024]{2,1,0:T(8,128)(2,1)S(1)}, bf16[4,96,1024]{2,1,0:T(8,128)(2,1)S(1)}, u32[]{:S(2)}, u32[]{:S(2)}) collective-permute-start(bf16[4,96,1024]{2,1,0:T(8,128)(2,1)S(1)} %bitcast.55), channel_id=1, source_target_pairs={{0,8},{2,10},{4,12},{6,14},{8,0},{10,2},{12,4},{14,6},{16,24},{18,... | collective-permute-start | bytes 2359304 | tf_op jit(solution)/shard_map/ppermute | solution.py:23
  125.3 24.0 %collective-permute-start.28 = (f32[8,768]{1,0:T(8,128)S(1)}, f32[8,768]{1,0:T(8,128)S(1)}, u32[]{:S(2)}, u32[]{:S(2)}) collective-permute-start(f32[8,768]{1,0:T(8,128)S(1)} %get-tuple-element.228.own_ref), channel_id=1, source_target_pairs={{0,1},{1,0},{2,3},{3,2},{4,5},{5,4},{6,7},{7,6},{8,9},{9,8},{10,11... | collective-permute-start | bytes 73736 | tf_op jit(solution)/shard_map/ppermute | solution.py:27
  152.9 13.6 %collective-permute-start.29 = (bf16[2048,768]{1,0:T(8,128)(2,1)S(1)}, bf16[2048,768]{1,0:T(8,128)(2,1)S(1)}, u32[]{:S(2)}, u32[]{:S(2)}) collective-permute-start(bf16[2048,768]{1,0:T(8,128)(2,1)S(1)} %shard_map.266), channel_id=1, source_target_pairs={{0,1},{1,0},{2,3},{3,2},{4,5},{5,4},{6,7},{7,6},{8,9},{9,8},{10,11... | collective-permute-start | bytes 9437192 | tf_op jit(solution)/shard_map/ppermute | solution.py:27
  170.0 32.4 %collective-permute-start.33 = (bf16[4,496,256]{2,1,0:T(8,128)(2,1)S(1)}, bf16[4,496,256]{2,1,0:T(8,128)(2,1)S(1)}, u32[]{:S(2)}, u32[]{:S(2)}) collective-permute-start(bf16[4,496,256]{2,1,0:T(8,128)(2,1)S(1)} %get-tuple-element.250), channel_id=1, source_target_pairs={{0,2},{2,0},{4,6},{6,4},{8,10},{10,8},{12,14},{14,12},{16,18},{18,... | collective-permute-start | bytes 3047432 | tf_op jit(solution)/shard_map/ppermute | solution.py:23
  170.4 32.0 %collective-permute-start.34 = (bf16[4,448,256]{2,1,0:T(8,128)(2,1)S(1)}, bf16[4,448,256]{2,1,0:T(8,128)(2,1)S(1)}, u32[]{:S(2)}, u32[]{:S(2)}) collective-permute-start(bf16[4,448,256]{2,1,0:T(8,128)(2,1)S(1)} %get-tuple-element.251), channel_id=1, source_target_pairs={{0,4},{2,6},{4,0},{6,2},{8,12},{10,14},{12,8},{14,10},{16,20},{18,... | collective-permute-start | bytes 2752520 | tf_op jit(solution)/shard_map/ppermute | solution.py:23
  171.6 30.8 %collective-permute-start.35 = (bf16[4,448,256]{2,1,0:T(8,128)(2,1)S(1)}, bf16[4,448,256]{2,1,0:T(8,128)(2,1)S(1)}, u32[]{:S(2)}, u32[]{:S(2)}) collective-permute-start(bf16[4,448,256]{2,1,0:T(8,128)(2,1)S(1)} %get-tuple-element.252), channel_id=1, source_target_pairs={{0,8},{2,10},{4,12},{6,14},{8,0},{10,2},{12,4},{14,6},{16,24},{18,... | collective-permute-start | bytes 2752520 | tf_op jit(solution)/shard_map/ppermute | solution.py:23
  173.1 23.4 %collective-permute-start.36 = (bf16[1,96,1024]{2,1,0:T(8,128)(2,1)S(1)}, bf16[1,96,1024]{2,1,0:T(8,128)(2,1)S(1)}, u32[]{:S(2)}, u32[]{:S(2)}) collective-permute-start(bf16[1,96,1024]{2,1,0:T(8,128)(2,1)S(1)} %get-tuple-element.253), channel_id=1, source_target_pairs={{0,8},{2,10},{4,12},{6,14},{8,0},{10,2},{12,4},{14,6},{16,24},{18,... | collective-permute-start | bytes 589832 | tf_op jit(solution)/shard_map/ppermute | solution.py:23
  173.6 24.0 %collective-permute-start.37 = (bf16[1,96,1024]{2,1,0:T(8,128)(2,1)S(1)}, bf16[1,96,1024]{2,1,0:T(8,128)(2,1)S(1)}, u32[]{:S(2)}, u32[]{:S(2)}) collective-permute-start(bf16[1,96,1024]{2,1,0:T(8,128)(2,1)S(1)} %get-tuple-element.254), channel_id=1, source_target_pairs={{0,2},{2,0},{4,6},{6,4},{8,10},{10,8},{12,14},{14,12},{16,18},{18,... | collective-permute-start | bytes 589832 | tf_op jit(solution)/shard_map/ppermute | solution.py:23
  218.3 17.3 %collective-permute-start.46 = (bf16[48,3072]{1,0:T(8,128)(2,1)S(1)}, bf16[48,3072]{1,0:T(8,128)(2,1)S(1)}, u32[]{:S(2)}, u32[]{:S(2)}) collective-permute-start(bf16[48,3072]{1,0:T(8,128)(2,1)S(1)} %get-tuple-element.287), channel_id=1, source_target_pairs={{0,16},{2,18},{4,20},{6,22},{8,24},{10,26},{12,28},{14,30},{16,0},... | collective-permute-start | bytes 884744 | tf_op jit(solution)/shard_map/ppermute | solution.py:23
  (32 other events, 215.1 us)
where the time goes:
time: 245 us; the launch traced here: 241 us
  waiting for transfers between devices  104 us (42%)
  Pallas kernels  70.8 us (29%)
  starting transfers between devices  51.5 us (21%)
  local copies, waits for them, and re-layouts  5.86 us (2%)
  between operations  4.51 us (2%)
  other arithmetic  3.87 us (2%)
    ppermute x37, waiting for transfers between devices, swap_mask(): lax.ppermute(block, 'dp', [(one, one ^ mask) for one in range(count)])  96.7 us
    pallas_call x28, Pallas kernels, local_call(): pl.pallas_call(kernel, out_shape=tuple((one if len(outs) - at <= free els...  68.5 us
    ppermute x37, starting transfers between devices, swap_mask(): lax.ppermute(block, 'dp', [(one, one ^ mask) for one in range(count)])  48.5 us
    ppermute x10, waiting for transfers between devices, swap_core(): return lax.ppermute(block, 'tensor', [(0, 1), (1, 0)])  7.26 us
  transfers between devices with their start and end apart: 47, of which 25 were waited for; matrix products, arithmetic and copies ran while one was open for 3% of the time, Pallas kernels for 20%

commit v1 on v0

--- a/solution.py
+++ b/solution.py
@@ -423,22 +423,16 @@
         copy.wait()
 
 
-def weight_start_kernel(*refs, cut):
+def weight_start_kernel(*refs):
     near = refs[9:-1]
     fetched(refs[:7], near, refs[-1])
-    query_ref, key_ref, value_ref, inner_ref, outer_ref, output_ref, valid_ref = near
     first_ref, second_ref = refs[7:9]
-    width = query_ref.shape[1]
-    for at, one in enumerate((query_ref, key_ref, value_ref)):
-        first_ref[:, at * width : (at + 1) * width] = one[...]
-    second_ref[:, :cut] = inner_ref[:, :cut]
-    second_ref[:, cut : 2 * cut] = outer_ref[:, :cut]
-    at = 2 * cut
-    for one, first in ((inner_ref, cut), (outer_ref, cut), (output_ref, 0)):
-        size = one.shape[1] - first
-        second_ref[:, at : at + size] = one[:, first:]
-        at += size
-    count = jnp.sum(valid_ref[...].astype(jnp.float32), axis=1, keepdims=True)
+    for out_ref, sources in ((first_ref, near[:4]), (second_ref, near[4:6])):
+        at = 0
+        for one in sources:
+            out_ref[:, at : at + one.shape[1]] = one[...]
+            at += one.shape[1]
+    count = jnp.sum(near[6][...].astype(jnp.float32), axis=1, keepdims=True)
     second_ref[:, at:] = jnp.broadcast_to(count, (second_ref.shape[0], PAIR)).astype(jnp.bfloat16)
 
 
@@ -577,9 +571,7 @@
         )
 
 
-def project_kernel(mixed_ref, weight_ref, counts_ref, own_ref, other_ref, low_ref, count_ref, *, each):
-    count = jnp.sum(counts_ref[...].astype(jnp.float32), axis=0, keepdims=True) / each
-    count_ref[...] = jnp.broadcast_to(count, count_ref.shape)
+def project_kernel(mixed_ref, weight_ref, own_ref, other_ref, low_ref):
     low = mixed_ref[...].astype(jnp.bfloat16)
     low_ref[...] = low
     total = dot_cols(low, weight_ref[...])
@@ -611,7 +603,12 @@
     low_ref[...] = hidden.astype(jnp.bfloat16)
 
 
-def feed_kernel(own_hidden_ref, other_hidden_ref, inner_ref, outer_ref, own_ref, other_ref, active_ref, slope_ref, total_ref):
+def feed_kernel(
+    own_hidden_ref, other_hidden_ref, inner_ref, outer_ref, counts_ref,
+    own_ref, other_ref, active_ref, slope_ref, count_ref, total_ref, *, each
+):
+    count = jnp.sum(counts_ref[...].astype(jnp.float32), axis=0, keepdims=True) / each
+    count_ref[...] = jnp.broadcast_to(count, count_ref.shape)
     hidden = jnp.concatenate([own_hidden_ref[...], other_hidden_ref[...]], 0)
     step = 256
     for start in range(0, inner_ref.shape[1], step):
@@ -901,15 +898,49 @@
     small_ref[...] = made_ref[:rows, 4 * width :] + from_pieces(came_ref[:, 4 * width :].astype(jnp.float32))
 
 
-def wide_end_kernel(*refs):
-    out_ref = refs[6]
-    columns = refs[0].shape[2]
+def merge_kernel(*refs, riders):
+    keeps, cames, sends, kept, messages = (refs[at : at + 3] for at in range(0, 15, 3))
+    for third, rider in enumerate(riders):
+        kept[third][...] = keeps[third][0] + cames[third][0].astype(jnp.float32)
+        later = (keeps[third][1] + cames[third][1].astype(jnp.float32)).astype(jnp.bfloat16)
+        slots, lines, columns = sends[rider].shape
+        for slot in range(slots):
+            messages[rider][slot * lines : (slot + 1) * lines, :] = sends[rider][slot]
+        base, rows = slots * lines, later.shape[0]
+        for chunk in range(later.shape[1] // columns):
+            messages[rider][base + chunk * rows : base + (chunk + 1) * rows, :] = later[
+                :, chunk * columns : (chunk + 1) * columns
+            ]
+
+
+def part_kernel(*refs, riders, plain):
+    keeps, cames, kept = refs[:3], refs[3:6], refs[6:9]
+    outs, wide_ref = refs[9:15], refs[15]
     for third in range(3):
-        out_ref[:, third * columns : (third + 1) * columns] = refs[2 * third][0] + refs[2 * third + 1][0].astype(
-            jnp.float32
-        )
-    if len(refs) > 7:
-        refs[7][...] = out_ref[out_ref.shape[0] // 2 :, :].astype(jnp.bfloat16)
+        keep_ref, came_ref = keeps[third], cames[third]
+        slots, lines, _ = keep_ref.shape
+        most = min(plain, lines)
+        for slot in range(slots):
+            side, at = slot // (slots // 2), slot % (slots // 2)
+            out_ref, base = outs[2 * third + side], slot * lines
+            total = keep_ref[slot, :most] + came_ref[base : base + most, :].astype(jnp.float32)
+            out_ref[at, :most] = total.astype(out_ref.dtype)
+            if most < lines:
+                total = keep_ref[slot, most:] + from_pieces(
+                    came_ref[base + most : base + lines, :].astype(jnp.float32)
+                )
+                out_ref[at, most:] = (in_pieces(total) if side else total).astype(out_ref.dtype)
+    for third, rider in enumerate(riders):
+        slots, lines, columns = keeps[rider].shape
+        rows, width = kept[third].shape
+        for chunk in range(width // columns):
+            part = slice(chunk * columns, (chunk + 1) * columns)
+            base = slots * lines + chunk * rows
+            wide_ref[:, third * width + chunk * columns : third * width + (chunk + 1) * columns] = kept[third][
+                :, part
+            ] + cames[rider][base : base + rows, :].astype(jnp.float32)
+    if len(refs) > 16:
+        refs[16][...] = wide_ref[wide_ref.shape[0] // 2 :, :].astype(jnp.bfloat16)
 
 
 def wide_out_kernel(made_ref, came_ref, outer_ref, inner_ref):
@@ -975,16 +1006,14 @@
         return [shaped((one, third), jnp.bfloat16) for one in lines]
 
     third = width // 3
-    cut = 3 * wide // 4
-    tail = packed_rows(slot_rows, head_width)
-    rest = (cut, cut, 2 * (wide - cut) + head_width + PAIR)
-    cuts = (0, cut, 2 * cut, 2 * cut + rest[2])
-    sizes = [packed_rows(slot_rows, one) for one in rest]
+    tail = packed_rows(slot_rows, 4 * head_width // 3)
+    cuts = (0, 2 * wide // 3, 4 * wide // 3, 2 * wide + PAIR)
+    sizes = [packed_rows(slot_rows, last - first) for first, last in zip(cuts, cuts[1:])]
     valid_row = valid_tokens.reshape(1, rows)
     first, second = fetching_call(
-        functools.partial(weight_start_kernel, cut=cut),
-        [shaped((each, 3 * head_width), jnp.bfloat16), shaped((each, cuts[3]), jnp.bfloat16)],
-        [query_weight, key_weight, value_weight, inner_weight, outer_weight, output_weight, valid_row],
+        weight_start_kernel,
+        [shaped((each, 4 * head_width), jnp.bfloat16), shaped((each, cuts[3]), jnp.bfloat16)],
+        [query_weight, key_weight, value_weight, output_weight, inner_weight, outer_weight, valid_row],
     )
     held = list(
         fetching_call(token_start_kernel, [shaped((rows, third), jnp.bfloat16)] * 3, [tie(first, tokens)])
@@ -1020,16 +1049,18 @@
     late_came = step(late, 1)
 
     held, came = tie(late[0], (held, came))
+    units = units_of(
+        ((0, 0, head_width),)
+        + tuple((1, 2 * at + shift, PAIR) for shift in (0, PAIR) for at in range(0, head_width, PAIR))
+        + ((2, 0, head_width),)
+    )
     plan = []
-    for bits, units in zip(
-        ROUTES,
-        [((0, 0, head_width),)]
-        + [tuple((1, 2 * at + shift, PAIR) for at in range(0, head_width, PAIR)) for shift in (0, PAIR)],
-    ):
+    for at, bits in enumerate(ROUTES):
+        part = units[at * len(units) // 3 : (at + 1) * len(units) // 3]
         sent = tuple(slot_masks((bits[1], bits[2])))
-        plan += [(sent, units_of(units)), (tuple(mask ^ (1 << bits[0]) for mask in sent), units_of(units))]
-    full_query, full_kv = place_packed(
-        owner, both(held, came), tuple(plan), (head_width, 2 * head_width), each
+        plan += [(sent, part), (tuple(mask ^ (1 << bits[0]) for mask in sent), part)]
+    full_query, full_kv, full_output = place_packed(
+        owner, both(held, came), tuple(plan), (head_width, 2 * head_width, head_width), each
     )
     own_query, own_kv = local_call(
         token_kernel, [shaped((rows, head_width), jnp.bfloat16), shaped((span * rows, 2 * head_width), jnp.bfloat16)],
@@ -1037,45 +1068,38 @@
     )
     mixed, mass, queries, kv = attend(tables, own_query, own_kv, other, full_query, full_kv)
 
-    late, late_came = tie(mixed, (late, late_came))
-    plan = []
-    for bits, units in zip(
-        ROUTES,
-        (
-            ((0, 0, cut),),
-            ((1, 0, cut),),
-            ((0, cut, wide - cut), (1, cut, wide - cut), (2, 0, head_width), (3, 0, PAIR)),
-        ),
-    ):
-        sent = tuple(slot_masks((bits[2], bits[0])))
-        plan += [(sent, units_of(units)), (tuple(mask ^ (1 << bits[1]) for mask in sent), units_of(units))]
-    full_inner, full_outer, full_output, counts = place_packed(
-        owner, both(late, late_came), tuple(plan), (wide, wide, head_width, PAIR), each
-    )
-
     half_shape, low_shape = shaped((rows, width)), shaped((rows, width), jnp.bfloat16)
     gain_one, shift_one, gain_two, shift_two = (
         one.reshape(1, width) for one in (attn_gain, attn_shift, ffn_gain, ffn_shift)
     )
-    count_shape = shaped((8, PAIR))
-    part_own, part_other, attended, count_own = local_call(
-        functools.partial(project_kernel, each=each),
-        [half_shape, low_shape, shaped(mixed.shape, jnp.bfloat16), count_shape], [mixed, full_output, counts],
+    part_own, part_other, attended = local_call(
+        project_kernel, [half_shape, low_shape, shaped(mixed.shape, jnp.bfloat16)], [mixed, full_output],
         flops=2 * mixed.size * width,
     )
-    count_came = swap_core(count_own)
+    part_came, late, late_came = lax.optimization_barrier((swap_core(part_other), late, late_came))
     first_sum, hidden, hidden_own = local_call(
         first_norm_kernel, [half_shape, half_shape, low_shape],
-        [tokens, part_own, swap_core(part_other), gain_one, shift_one],
+        [tokens, part_own, part_came, gain_one, shift_one],
     )
     hidden_other = swap_core(hidden_own)
-    part_own, part_other, active, slope = local_call(
-        feed_kernel,
-        [half_shape, low_shape, shaped((length, wide), jnp.bfloat16), shaped((length, wide))],
-        [hidden_own, hidden_other, full_inner, full_outer],
+    late, late_came = tie(hidden_own, (late, late_came))
+    units = units_of(((0, 0, wide), (1, 0, wide), (2, 0, PAIR)))
+    plan = []
+    for at, bits in enumerate(ROUTES):
+        part = units[cuts[at] // PAIR : cuts[at + 1] // PAIR]
+        sent = tuple(slot_masks((bits[2], bits[0])))
+        plan += [(sent, part), (tuple(mask ^ (1 << bits[1]) for mask in sent), part)]
+    full_inner, full_outer, counts = place_packed(
+        owner, both(late, late_came), tuple(plan), (wide, wide, PAIR), each
+    )
+    part_own, part_other, active, slope, count_own = local_call(
+        functools.partial(feed_kernel, each=each),
+        [half_shape, low_shape, shaped((length, wide), jnp.bfloat16), shaped((length, wide)), shaped((8, PAIR))],
+        [hidden_own, hidden_other, full_inner, full_outer, counts],
         scratch=[pltpu.VMEM((length, width), jnp.float32)],
         flops=4 * length * width * wide, transcendentals=2 * length * wide, spare=12,
     )
+    count_came = swap_core(count_own)
     token_total = devices * lax.axis_size("tensor") * rows
     grad_second, grad_ffn_own, stats_two, result = local_call(
         functools.partial(second_norm_kernel, token_total=token_total),
@@ -1120,32 +1144,49 @@
     made = narrow_gradients(
         own, other, tie(token_sent, kv_grad), query_grad, grad_attn_own, grad_attn_other, attended
     )
-    wide_keep, wide_send = folded(wide_keep, tie(made, wide_came))
-    wide_came = step(wide_send, 2)
     keep, send = token_own(
-        owner, kv_grad, query_grad, full_kv, full_query, tie(wide_keep[0], token_came), made, small, scatter_masks
-    )
-    came = step(send, 0)
+        owner, kv_grad, query_grad, full_kv, full_query, tie(made, token_came), made, small, scatter_masks
+    )
+    riders = tuple([bits[0] for bits in ROUTES].index(bits[2]) for bits in ROUTES)
+    columns = width // 3
+    ride = slot_rows * wide_keep[0].shape[2] // columns
+    lengths = [one.shape[0] * one.shape[1] + ride for one in send]
+    outs = local_call(
+        functools.partial(merge_kernel, riders=riders),
+        [shaped(one.shape[1:]) for one in wide_keep] + [shaped((one, columns), jnp.bfloat16) for one in lengths],
+        wide_keep + tie(keep[0], wide_came) + send,
+    )
+    wide_keep, came = outs[:3], step(outs[3:], 0)
+    plain = rows + 2 * slot_rows
+    halves = []
+    for one in keep:
+        half = (one.shape[0] // 2,) + one.shape[1:]
+        halves += [shaped(half), shaped(half, jnp.bfloat16)]
     far_send = [shaped((each, 2 * wide), jnp.bfloat16)] if far_count == 2 else []
-    wide_sum, *wide_send = local_call(
-        wide_end_kernel, [shaped((slot_rows, 2 * wide))] + far_send, both(wide_keep, tie(keep[0], wide_came))
-    )
-    plain = rows + 2 * slot_rows
-    keep, send = fold(keep, [[one] for one in tie(wide_sum, came)], plain)
+    outs = local_call(
+        functools.partial(part_kernel, riders=riders, plain=plain),
+        halves + [shaped((slot_rows, 2 * wide))] + far_send, keep + came + list(wide_keep),
+    )
+    keep, send, wide_sum, wide_send = list(outs[:6:2]), list(outs[1:6:2]), outs[6], outs[7:]
     came = step(send, 1)
 
-    def far_scatter(total, after=None, dtype=jnp.bfloat16):
+    def far_scatter(total, dtype=jnp.bfloat16):
         total = total.reshape(far_count, each, total.shape[1])
         for bit in far_bits[::-1]:
             half = total.shape[0] // 2
-            came = swap_mask(total[half:].astype(dtype), 1 << bit)
-            if after is not None:
-                came, total = tie(after, (came, total))
-            total = total[:half] + came.astype(jnp.float32)
+            total = total[:half] + swap_mask(total[half:].astype(dtype), 1 << bit).astype(jnp.float32)
         return total[0]
 
     keep, send = fold(keep, [[one] for one in came], plain)
     came = step(send, 2)
+    if far_count == 2:
+        part_outer, part_inner = local_call(
+            wide_out_kernel, [shaped((each, wide))] * 2, [wide_sum, swap_mask(wide_send[0], 1 << far_bits[0])], free=2
+        )
+    else:
+        wide_sum = far_scatter(wide_sum)
+        part_outer, part_inner = wide_sum[:, :wide], wide_sum[:, wide:]
+    came = tie(part_outer, came)
     made_shape = shaped((slot_rows, 4 * head_width + PAIR))
     send_shape = [shaped((each, 4 * head_width + PAIR), jnp.bfloat16)] if far_count == 2 else []
     *made, grad_tokens = local_call(
@@ -1160,18 +1201,10 @@
         )
     else:
         narrow_sum = far_scatter(made[:, : 4 * head_width])
-        small = far_scatter(made[:, 4 * head_width :], None, jnp.float32)
+        small = far_scatter(made[:, 4 * head_width :], jnp.float32)
         part_query, part_output = narrow_sum[:, :head_width], narrow_sum[:, head_width : 2 * head_width]
         kv_sum = narrow_sum[:, 2 * head_width :].reshape(each, head_width // PAIR, 2, PAIR)
         part_key, part_value = (kv_sum[:, :, one].reshape(each, head_width) for one in range(2))
-    if far_count == 2:
-        wide_came = swap_mask(wide_send[0], 1 << far_bits[0])
-        part_outer, part_inner = local_call(
-            wide_out_kernel, [shaped((each, wide))] * 2, [wide_sum, tie(grad_tokens, wide_came)], free=2
-        )
-    else:
-        wide_sum = far_scatter(wide_sum, grad_tokens)
-        part_outer, part_inner = wide_sum[:, :wide], wide_sum[:, wide:]
     loss_value = small[0, 4] / (2.0 * width * (count_own[0, 0] + count_came[0, 0]))
     half = each // 2
     mine = jnp.where(core == 0, small[:half], small[half:])

time: 245 us -> 241 us (0.984)
  waiting for transfers between devices: 104 us -> 94.8 us
  starting transfers between devices: 51.5 us -> 55.1 us
  Pallas kernels: 70.8 us -> 74.1 us
    ppermute x37 -> x34, waiting for transfers between devices: 96.7 us -> 90 us  [swap_mask(): lax.ppermute(block, 'dp', [(one, one ^ mask) for one in range(count)])]
    ppermute x37 -> x34, starting transfers between devices: 48.5 us -> 52.3 us  [swap_mask(): lax.ppermute(block, 'dp', [(one, one ^ mask) for one in range(count)])]
    pallas_call x28 -> x27, Pallas kernels: 68.5 us -> 71.8 us  [local_call(): pl.pallas_call(kernel, out_shape=tuple((one if len(outs) - at <= free els...]
  transfers between devices with their start and end apart: 47 -> 44, of which waited for: 25 -> 22; matrix products, arithmetic and copies ran while one was open for 3% -> 3% of each run, Pallas kernels for 20% -> 23%
where the time goes in v1:
time: 241 us; the launch traced here: 238 us
  waiting for transfers between devices  94.8 us (39%)
  Pallas kernels  74.1 us (31%)
  starting transfers between devices  55.1 us (23%)
  local copies, waits for them, and re-layouts  4.94 us (2%)
  between operations  4.49 us (2%)
  other arithmetic  3.8 us (2%)
    ppermute x34, waiting for transfers between devices, swap_mask(): lax.ppermute(block, 'dp', [(one, one ^ mask) for one in range(count)])  90 us
    pallas_call x27, Pallas kernels, local_call(): pl.pallas_call(kernel, out_shape=tuple((one if len(outs) - at <= free els...  71.8 us
    ppermute x34, starting transfers between devices, swap_mask(): lax.ppermute(block, 'dp', [(one, one ^ mask) for one in range(count)])  52.3 us
    ppermute x10, waiting for transfers between devices, swap_core(): return lax.ppermute(block, 'tensor', [(0, 1), (1, 0)])  4.84 us
  transfers between devices with their start and end apart: 44, of which 22 were waited for; matrix products, arithmetic and copies ran while one was open for 3% of the time, Pallas kernels for 23%

profile of v1, /device:TPU:0, one launch (start us, length us, event | category | flops | bytes accessed | tf_op | source)
XLA Modules:
  0.0 238.1 jit_solution(7603686108171345348)
XLA Ops:
  1.9 4.1 %collective-permute-start.3 = (bf16[1,48,1536]{2,1,0:T(8,128)(2,1)S(1)}, bf16[1,48,1536]{2,1,0:T(8,128)(2,1)S(1)}, u32[]{:S(2)}, u32[]{:S(2)}) collective-permute-start(bf16[1,48,1536]{2,1,0:T(8,128)(2,1)S(1)} %bitcast.51), channel_id=1, source_target_pairs={{0,16},{2,18},{4,20},{6,22},{8,24},{10,26},{12,28},{14,30},{16,0},... | collective-permute-start | bytes 442376 | tf_op jit(solution)/shard_map/ppermute | solution.py:23
  18.8 5.2 %collective-permute-start.6 = (bf16[704,256]{1,0:T(8,128)(2,1)S(1)}, bf16[704,256]{1,0:T(8,128)(2,1)S(1)}, u32[]{:S(2)}, u32[]{:S(2)}) collective-permute-start(bf16[704,256]{1,0:T(8,128)(2,1)S(1)} %get-tuple-element.162.refs_4_), channel_id=1, source_target_pairs={{0,2},{2,0},{4,6},{6,4},{8,10},{10,8},{12,14},{14,12},{16,18},{18,... | collective-permute-start | bytes 1081352 | tf_op jit(solution)/shard_map/ppermute | solution.py:23
  24.0 3.1 %collective-permute-done.7 = bf16[1,48,3200]{2,1,0:T(8,128)(2,1)S(1)} collective-permute-done((bf16[1,48,3200]{2,1,0:T(8,128)(2,1)S(1)}, bf16[1,48,3200]{2,1,0:T(8,128)(2,1)S(1)}, u32[]{:S(2)}, u32[]{:S(2)}) %collective-permute-start.7) | collective-permute-done | bytes 307232 | tf_op jit(solution)/shard_map/ppermute | solution.py:23
  27.2 5.9 %collective-permute-done.5.refs_3_ = bf16[704,256]{1,0:T(8,128)(2,1)S(1)} collective-permute-done((bf16[704,256]{1,0:T(8,128)(2,1)S(1)}, bf16[704,256]{1,0:T(8,128)(2,1)S(1)}, u32[]{:S(2)}, u32[]{:S(2)}) %collective-permute-start.5) | collective-permute-done | bytes 360480 | tf_op jit(solution)/shard_map/ppermute | solution.py:23
  38.8 17.3 %collective-permute-done.8.refs_1_ = bf16[1792,256]{1,0:T(8,128)(2,1)} collective-permute-done((bf16[1792,256]{1,0:T(8,128)(2,1)S(1)}, bf16[1792,256]{1,0:T(8,128)(2,1)}, u32[]{:S(2)}, u32[]{:S(2)}) %collective-permute-start.8) | collective-permute-done | bytes 917536 | tf_op jit(solution)/shard_map/ppermute | solution.py:23
  57.0 2.1 shard_map.250
  62.5 18.1 %collective-permute-done.11.refs_1_ = bf16[1536,256]{1,0:T(8,128)(2,1)S(1)} collective-permute-done((bf16[1536,256]{1,0:T(8,128)(2,1)S(1)}, bf16[1536,256]{1,0:T(8,128)(2,1)S(1)}, u32[]{:S(2)}, u32[]{:S(2)}) %collective-permute-start.11) | collective-permute-done | bytes 786464 | tf_op jit(solution)/shard_map/ppermute | solution.py:23
  84.8 2.8 %shard_map.253 = (bf16[256,384]{1,0:T(8,128)(2,1)S(1)}, bf16[2048,768]{1,0:T(8,128)(2,1)S(1)}) custom-call(bf16[2048,768]{1,0:T(8,128)(2,1)S(1)} %get-tuple-element.173.x_ref.own_ref, bf16[768,384]{1,0:T(8,128)(2,1)S(1)} %get-tuple-element.185.query_weight_ref, bf16[768,768]{1,0:T(8,128)(2,1)S(1)} %get-tuple-element.186.kv_weight_ref), custom_call_target="tpu_custom_call" | custom-call | flops 1000 | bytes 1000 | tf_op jit(solution)/shard_map/pallas_call | solution.py:70
  87.6 10.2 %shard_map.254 = (f32[512,384]{1,0:T(8,128)S(1)}, f32[24,8,128]{2,1,0:T(8,128)S(1)}, bf16[512,384]{1,0:T(8,128)(2,1)S(1)}, bf16[4096,768]{1,0:T(8,128)(2,1)S(1)}) custom-call(s32[501]{0:T(512)S(1)} %pad_add_fusion.numbers_ref, f32[8,128]{1,0:T(8,128)S(1)} %pad_maximum_fusion.3.query_side_ref, f32[4096,128]{1,0:T(8,128)S(1)} %broadcast_in_dim.143.key_side_ref, ...), custom_call_target="tpu_custom_call" | custom-call | flops 1000 | bytes 1000 | tf_op jit(solution)/shard_map/pallas_call | solution.py:70
  98.5 2.2 collective-permute-done.16.refs_1_
  104.5 3.3 %shard_map.258 = (f32[256,768]{1,0:T(8,128)S(1)}, bf16[256,768]{1,0:T(8,128)(2,1)S(1)}, bf16[512,1536]{1,0:T(8,128)(2,1)S(1)}, f32[512,1536]{1,0:T(8,128)S(1)}, f32[8,128]{1,0:T(8,128)S(1)}) custom-call(bf16[256,768]{1,0:T(8,128)(2,1)S(1)} %get-tuple-element.197.own_hidden_ref, bf16[256,768]{1,0:T(8,128)(2,1)S(1)} %collective-permute-done.19.other_hidden_ref, ...), custom_call_target="tpu_custom_call" | custom-call | flops 1000 | bytes 1000 | tf_op jit(solution)/shard_map/pallas_call | solution.py:70
  112.8 3.1 %shard_map.260 = (bf16[512,1536]{1,0:T(8,128)(2,1)S(1)}, f32[256,768]{1,0:T(8,128)S(1)}, bf16[256,768]{1,0:T(8,128)(2,1)S(1)}) custom-call(bf16[256,768]{1,0:T(8,128)(2,1)S(1)} %get-tuple-element.218.own_grad_ref, bf16[256,768]{1,0:T(8,128)(2,1)S(1)} %collective-permute-done.22.other_grad_ref, f32[512,1536]{1,0:T(8,128)S(1)} %get-tuple-element.219.slope_ref, ...), custom_call_target="tpu_custom_call" | custom-call | flops 1000 | bytes 1000 | tf_op jit(solution)/shard_map/pallas_call | solution.py:70
  116.1 3.5 %shard_map.261 = (f32[8,48,1024]{2,1,0:T(8,128)S(1)}, bf16[8,48,1024]{2,1,0:T(8,128)(2,1)S(1)}, f32[8,48,1024]{2,1,0:T(8,128)S(1)}, bf16[8,48,1024]{2,1,0:T(8,12...) custom-call(s32[16]{0:T(128)S(1)} %add.233.owner_ref, ...), custom_call_target="tpu_custom_call" | custom-call | flops 1000 | bytes 1000 | tf_op jit(solution)/shard_map/pallas_call | solution.py:70
  124.6 23.2 %shard_map.263 = (bf16[512,384]{1,0:T(8,128)(2,1)S(1)}, bf16[4096,768]{1,0:T(8,128)(2,1)S(1)}) custom-call(s32[501]{0:T(512)S(1)} %pad_add_fusion.numbers_ref, f32[8,128]{1,0:T(8,128)S(1)} %pad_maximum_fusion.3.query_side_ref, f32[4096,128]{1,0:T(8,128)S(1)} %broadcast_in_dim.143.key_side_ref, bf16[512,384]{1,0:T(8,128)(2,1)S(1)} %get-tuple-element.229.q_ref, ...), custom_call_target="tpu_custom_call" | custom-call | flops 1000 | bytes 1000 | tf_op jit(solution)/shard_map/pallas_call | solution.py:70
  148.4 2.8 %shard_map.266 = bf16[2048,768]{1,0:T(8,128)(2,1)S(1)} custom-call(bf16[4096,768]{1,0:T(8,128)(2,1)S(1)} %get-tuple-element.247.kv_grad_ref, bf16[512,384]{1,0:T(8,128)(2,1)S(1)} %get-tuple-element.234.query_grad_ref, bf16[768,768]{1,0:T(8,128)(2,1)S(1)} %get-tuple-element.186.kv_weight_ref, bf16[768,384]{1,0:T(8,128)(2,1)S(1)} %get-tuple-element.185.query_weight_ref), custom_call_target="tpu_custom_call" | custom-call | flops 1000 | bytes 1000 | tf_op jit(solution)/shard_map/pallas_call | solution.py:70
  154.1 5.9 %shard_map.267.made_ref = f32[768,1536]{1,0:T(8,128)S(1)} custom-call(bf16[2048,768]{1,0:T(8,128)(2,1)S(1)} %get-tuple-element.173.x_ref.own_ref, bf16[2048,768]{1,0:T(8,128)(2,1)S(1)} %collective-permute-done.14.other_ref, bf16[4096,768]{1,0:T(8,128)(2,1)S(1)} %get-tuple-element.247.kv_grad_ref, bf16[512,384]{1,0:T(8,128)(2,1)S(1)} %get-tuple-element.234.query_grad_ref, ...), custom_call_target="tpu_custom_call" | custom-call | flops 1000 | bytes 1000 | tf_op jit(solution)/shard_map/pallas_call | solution.py:70
  160.0 3.7 %shard_map.268 = (f32[4,496,256]{2,1,0:T(8,128)S(1)}, bf16[4,496,256]{2,1,0:T(8,128)(2,1)S(1)}, f32[4,448,256]{2,1,0:T(8,128)S(1)}, bf16[4,448,256]{2,1,0:T(8,12...) custom-call(s32[16]{0:T(128)S(1)} %add.233.owner_ref, ...), custom_call_target="tpu_custom_call" | custom-call | flops 1000 | bytes 1000 | tf_op jit(solution)/shard_map/pallas_call | solution.py:70
  166.6 2.0 collective-permute-start.35
  168.6 22.5 %collective-permute-done.34.refs_4_ = bf16[2176,256]{1,0:T(8,128)(2,1)S(1)} collective-permute-done((bf16[2176,256]{1,0:T(8,128)(2,1)S(1)}, bf16[2176,256]{1,0:T(8,128)(2,1)S(1)}, u32[]{:S(2)}, u32[]{:S(2)}) %collective-permute-start.34) | collective-permute-done | bytes 1114144 | tf_op jit(solution)/shard_map/ppermute | solution.py:23
  197.5 6.9 %collective-permute-start.42 = (bf16[48,3072]{1,0:T(8,128)(2,1)S(1)}, bf16[48,3072]{1,0:T(8,128)(2,1)S(1)}, u32[]{:S(2)}, u32[]{:S(2)}) collective-permute-start(bf16[48,3072]{1,0:T(8,128)(2,1)S(1)} %get-tuple-element.281), channel_id=1, source_target_pairs={{0,16},{2,18},{4,20},{6,22},{8,24},{10,26},{12,28},{14,30},{16,0},... | collective-permute-start | bytes 884744 | tf_op jit(solution)/shard_map/ppermute | solution.py:23
  204.4 9.3 %collective-permute-done.37.refs_3_ = bf16[2,448,256]{2,1,0:T(8,128)(2,1)S(1)} collective-permute-done((bf16[2,448,256]{2,1,0:T(8,128)(2,1)S(1)}, bf16[2,448,256]{2,1,0:T(8,128)(2,1)S(1)}, u32[]{:S(2)}, u32[]{:S(2)}) %collective-permute-start.37) | collective-permute-done | bytes 458784 | tf_op jit(solution)/shard_map/ppermute | solution.py:23
  216.5 3.8 %collective-permute-done.40.refs_3_ = bf16[1,448,256]{2,1,0:T(8,128)(2,1)S(1)} collective-permute-done((bf16[1,448,256]{2,1,0:T(8,128)(2,1)S(1)}, bf16[1,448,256]{2,1,0:T(8,128)(2,1)S(1)}, u32[]{:S(2)}, u32[]{:S(2)}) %collective-permute-start.40) | collective-permute-done | bytes 229408 | tf_op jit(solution)/shard_map/ppermute | solution.py:23
  222.5 7.2 %collective-permute-start.43 = (bf16[48,1664]{1,0:T(8,128)(2,1)S(1)}, bf16[48,1664]{1,0:T(8,128)(2,1)S(1)}, u32[]{:S(2)}, u32[]{:S(2)}) collective-permute-start(bf16[48,1664]{1,0:T(8,128)(2,1)S(1)} %get-tuple-element.289), channel_id=1, source_target_pairs={{0,16},{2,18},{4,20},{6,22},{8,24},{10,26},{12,28},{14,30},{16,0},... | collective-permute-start | bytes 479240 | tf_op jit(solution)/shard_map/ppermute | solution.py:23
  231.9 2.2 collective-permute-done.43.came_ref
  (169 shorter events, 63.3 us)
Async XLA Ops:
  1.9 14.8 %collective-permute-start.3 = (bf16[1,48,1536]{2,1,0:T(8,128)(2,1)S(1)}, bf16[1,48,1536]{2,1,0:T(8,128)(2,1)S(1)}, u32[]{:S(2)}, u32[]{:S(2)}) collective-permute-start(bf16[1,48,1536]{2,1,0:T(8,128)(2,1)S(1)} %bitcast.51), channel_id=1, source_target_pairs={{0,16},{2,18},{4,20},{6,22},{8,24},{10,26},{12,28},{14,30},{16,0},... | collective-permute-start | bytes 442376 | tf_op jit(solution)/shard_map/ppermute | solution.py:23
  11.7 15.4 %collective-permute-start.7 = (bf16[1,48,3200]{2,1,0:T(8,128)(2,1)S(1)}, bf16[1,48,3200]{2,1,0:T(8,128)(2,1)S(1)}, u32[]{:S(2)}, u32[]{:S(2)}) collective-permute-start(bf16[1,48,3200]{2,1,0:T(8,128)(2,1)S(1)} %bitcast.49), channel_id=1, source_target_pairs={{0,16},{2,18},{4,20},{6,22},{8,24},{10,26},{12,28},{14,30},{16,0},... | collective-permute-start | bytes 921608 | tf_op jit(solution)/shard_map/ppermute | solution.py:23
  18.0 15.1 %collective-permute-start.5 = (bf16[704,256]{1,0:T(8,128)(2,1)S(1)}, bf16[704,256]{1,0:T(8,128)(2,1)S(1)}, u32[]{:S(2)}, u32[]{:S(2)}) collective-permute-start(bf16[704,256]{1,0:T(8,128)(2,1)S(1)} %get-tuple-element.161.refs_2_), channel_id=1, source_target_pairs={{0,8},{2,10},{4,12},{6,14},{8,0},{10,2},{12,4},{14,6},{16,24},{18,... | collective-permute-start | bytes 1081352 | tf_op jit(solution)/shard_map/ppermute | solution.py:23
  34.2 22.1 %collective-permute-start.10 = (bf16[1840,256]{1,0:T(8,128)(2,1)S(1)}, bf16[1840,256]{1,0:T(8,128)(2,1)S(1)}, u32[]{:S(2)}, u32[]{:S(2)}) collective-permute-start(bf16[1840,256]{1,0:T(8,128)(2,1)S(1)} %get-tuple-element.166.refs_4_), channel_id=1, source_target_pairs={{0,4},{2,6},{4,0},{6,2},{8,12},{10,14},{12,8},{14,10},{16,20},{18,... | collective-permute-start | bytes 2826248 | tf_op jit(solution)/shard_map/ppermute | solution.py:23
  35.4 20.8 %collective-permute-start.8 = (bf16[1792,256]{1,0:T(8,128)(2,1)S(1)}, bf16[1792,256]{1,0:T(8,128)(2,1)}, u32[]{:S(2)}, u32[]{:S(2)}) collective-permute-start(bf16[1792,256]{1,0:T(8,128)(2,1)S(1)} %get-tuple-element.164.refs_0_), channel_id=1, source_target_pairs={{0,8},{2,10},{4,12},{6,14},{8,0},{10,2},{12,4},{14,6},{16,24},{18,... | collective-permute-start | bytes 2752520 | tf_op jit(solution)/shard_map/ppermute | solution.py:23
  35.4 21.0 %collective-permute-start.9 = (bf16[1792,256]{1,0:T(8,128)(2,1)}, bf16[1792,256]{1,0:T(8,128)(2,1)}, u32[]{:S(2)}, u32[]{:S(2)}) collective-permute-start(bf16[1792,256]{1,0:T(8,128)(2,1)} %get-tuple-element.165.refs_2_), channel_id=1, source_target_pairs={{0,2},{2,0},{4,6},{6,4},{8,10},{10,8},{12,14},{14,12},{16,18},{18,... | collective-permute-start | bytes 2752520 | tf_op jit(solution)/shard_map/ppermute | solution.py:23
  59.1 28.5 %collective-permute-start.14 = (bf16[2048,768]{1,0:T(8,128)(2,1)S(1)}, bf16[2048,768]{1,0:T(8,128)(2,1)S(1)}, u32[]{:S(2)}, u32[]{:S(2)}) collective-permute-start(bf16[2048,768]{1,0:T(8,128)(2,1)S(1)} %get-tuple-element.173.x_ref.own_ref), channel_id=1, source_target_pairs={{0,1},{1,0},{2,3},{3,2},{4,5},{5,4},{6,7},{7,6},{8,9},{9,8},{10,11... | collective-permute-start | bytes 9437192 | tf_op jit(solution)/shard_map/ppermute | solution.py:27
  59.2 22.4 %collective-permute-start.13 = (bf16[1632,256]{1,0:T(8,128)(2,1)S(1)}, bf16[1632,256]{1,0:T(8,128)(2,1)S(1)}, u32[]{:S(2)}, u32[]{:S(2)}) collective-permute-start(bf16[1632,256]{1,0:T(8,128)(2,1)S(1)} %get-tuple-element.183.refs_4_), channel_id=1, source_target_pairs={{0,8},{2,10},{4,12},{6,14},{8,0},{10,2},{12,4},{14,6},{16,24},{18,... | collective-permute-start | bytes 2506760 | tf_op jit(solution)/shard_map/ppermute | solution.py:23
  61.0 19.6 %collective-permute-start.11 = (bf16[1536,256]{1,0:T(8,128)(2,1)S(1)}, bf16[1536,256]{1,0:T(8,128)(2,1)S(1)}, u32[]{:S(2)}, u32[]{:S(2)}) collective-permute-start(bf16[1536,256]{1,0:T(8,128)(2,1)S(1)} %get-tuple-element.179.refs_0_), channel_id=1, source_target_pairs={{0,2},{2,0},{4,6},{6,4},{8,10},{10,8},{12,14},{14,12},{16,18},{18,... | collective-permute-start | bytes 2359304 | tf_op jit(solution)/shard_map/ppermute | solution.py:23
  62.2 19.3 %collective-permute-start.12 = (bf16[1536,256]{1,0:T(8,128)(2,1)S(1)}, bf16[1536,256]{1,0:T(8,128)(2,1)S(1)}, u32[]{:S(2)}, u32[]{:S(2)}) collective-permute-start(bf16[1536,256]{1,0:T(8,128)(2,1)S(1)} %get-tuple-element.181.refs_2_), channel_id=1, source_target_pairs={{0,4},{2,6},{4,0},{6,2},{8,12},{10,14},{12,8},{14,10},{16,20},{18,... | collective-permute-start | bytes 2359304 | tf_op jit(solution)/shard_map/ppermute | solution.py:23
  81.7 20.6 %collective-permute-start.18 = (bf16[1728,256]{1,0:T(8,128)(2,1)S(1)}, bf16[1728,256]{1,0:T(8,128)(2,1)S(1)}, u32[]{:S(2)}, u32[]{:S(2)}) collective-permute-start(bf16[1728,256]{1,0:T(8,128)(2,1)S(1)} %get-tuple-element.208.refs_4_), channel_id=1, source_target_pairs={{0,2},{2,0},{4,6},{6,4},{8,10},{10,8},{12,14},{14,12},{16,18},{18,... | collective-permute-start | bytes 2654216 | tf_op jit(solution)/shard_map/ppermute | solution.py:23
  82.6 18.2 %collective-permute-start.16 = (bf16[1536,256]{1,0:T(8,128)(2,1)S(1)}, bf16[1536,256]{1,0:T(8,128)(2,1)S(1)}, u32[]{:S(2)}, u32[]{:S(2)}) collective-permute-start(bf16[1536,256]{1,0:T(8,128)(2,1)S(1)} %get-tuple-element.204.refs_0_), channel_id=1, source_target_pairs={{0,4},{2,6},{4,0},{6,2},{8,12},{10,14},{12,8},{14,10},{16,20},{18,... | collective-permute-start | bytes 2359304 | tf_op jit(solution)/shard_map/ppermute | solution.py:23
  83.6 17.9 %collective-permute-start.17 = (bf16[1536,256]{1,0:T(8,128)(2,1)S(1)}, bf16[1536,256]{1,0:T(8,128)(2,1)S(1)}, u32[]{:S(2)}, u32[]{:S(2)}) collective-permute-start(bf16[1536,256]{1,0:T(8,128)(2,1)S(1)} %get-tuple-element.206.refs_2_), channel_id=1, source_target_pairs={{0,8},{2,10},{4,12},{6,14},{8,0},{10,2},{12,4},{14,6},{16,24},{18,... | collective-permute-start | bytes 2359304 | tf_op jit(solution)/shard_map/ppermute | solution.py:23
  119.6 28.4 %collective-permute-start.25 = (bf16[4,96,1024]{2,1,0:T(8,128)(2,1)S(1)}, bf16[4,96,1024]{2,1,0:T(8,128)(2,1)S(1)}, u32[]{:S(2)}, u32[]{:S(2)}) collective-permute-start(bf16[4,96,1024]{2,1,0:T(8,128)(2,1)S(1)} %bitcast.57), channel_id=1, source_target_pairs={{0,2},{2,0},{4,6},{6,4},{8,10},{10,8},{12,14},{14,12},{16,18},{18,... | collective-permute-start | bytes 2359304 | tf_op jit(solution)/shard_map/ppermute | solution.py:23
  120.4 27.6 %collective-permute-start.26 = (bf16[4,96,1024]{2,1,0:T(8,128)(2,1)S(1)}, bf16[4,96,1024]{2,1,0:T(8,128)(2,1)S(1)}, u32[]{:S(2)}, u32[]{:S(2)}) collective-permute-start(bf16[4,96,1024]{2,1,0:T(8,128)(2,1)S(1)} %bitcast.56), channel_id=1, source_target_pairs={{0,4},{2,6},{4,0},{6,2},{8,12},{10,14},{12,8},{14,10},{16,20},{18,... | collective-permute-start | bytes 2359304 | tf_op jit(solution)/shard_map/ppermute | solution.py:23
  121.5 26.5 %collective-permute-start.27 = (bf16[4,96,1024]{2,1,0:T(8,128)(2,1)S(1)}, bf16[4,96,1024]{2,1,0:T(8,128)(2,1)S(1)}, u32[]{:S(2)}, u32[]{:S(2)}) collective-permute-start(bf16[4,96,1024]{2,1,0:T(8,128)(2,1)S(1)} %bitcast.55), channel_id=1, source_target_pairs={{0,8},{2,10},{4,12},{6,14},{8,0},{10,2},{12,4},{14,6},{16,24},{18,... | collective-permute-start | bytes 2359304 | tf_op jit(solution)/shard_map/ppermute | solution.py:23
  122.9 24.9 %collective-permute-start.28 = (f32[8,768]{1,0:T(8,128)S(1)}, f32[8,768]{1,0:T(8,128)S(1)}, u32[]{:S(2)}, u32[]{:S(2)}) collective-permute-start(f32[8,768]{1,0:T(8,128)S(1)} %get-tuple-element.238.own_ref), channel_id=1, source_target_pairs={{0,1},{1,0},{2,3},{3,2},{4,5},{5,4},{6,7},{7,6},{8,9},{9,8},{10,11... | collective-permute-start | bytes 73736 | tf_op jit(solution)/shard_map/ppermute | solution.py:27
  164.4 27.9 %collective-permute-start.33 = (bf16[2368,256]{1,0:T(8,128)(2,1)S(1)}, bf16[2368,256]{1,0:T(8,128)(2,1)S(1)}, u32[]{:S(2)}, u32[]{:S(2)}) collective-permute-start(bf16[2368,256]{1,0:T(8,128)(2,1)S(1)} %get-tuple-element.264), channel_id=1, source_target_pairs={{0,2},{2,0},{4,6},{6,4},{8,10},{10,8},{12,14},{14,12},{16,18},{18,... | collective-permute-start | bytes 3637256 | tf_op jit(solution)/shard_map/ppermute | solution.py:23
  165.4 25.7 %collective-permute-start.34 = (bf16[2176,256]{1,0:T(8,128)(2,1)S(1)}, bf16[2176,256]{1,0:T(8,128)(2,1)S(1)}, u32[]{:S(2)}, u32[]{:S(2)}) collective-permute-start(bf16[2176,256]{1,0:T(8,128)(2,1)S(1)} %get-tuple-element.265), channel_id=1, source_target_pairs={{0,4},{2,6},{4,0},{6,2},{8,12},{10,14},{12,8},{14,10},{16,20},{18,... | collective-permute-start | bytes 3342344 | tf_op jit(solution)/shard_map/ppermute | solution.py:23
  166.6 25.4 %collective-permute-start.35 = (bf16[2176,256]{1,0:T(8,128)(2,1)S(1)}, bf16[2176,256]{1,0:T(8,128)(2,1)S(1)}, u32[]{:S(2)}, u32[]{:S(2)}) collective-permute-start(bf16[2176,256]{1,0:T(8,128)(2,1)S(1)} %get-tuple-element.266), channel_id=1, source_target_pairs={{0,8},{2,10},{4,12},{6,14},{8,0},{10,2},{12,4},{14,6},{16,24},{18,... | collective-permute-start | bytes 3342344 | tf_op jit(solution)/shard_map/ppermute | solution.py:23
  193.3 20.4 %collective-permute-start.36 = (bf16[2,496,256]{2,1,0:T(8,128)(2,1)S(1)}, bf16[2,496,256]{2,1,0:T(8,128)(2,1)S(1)}, u32[]{:S(2)}, u32[]{:S(2)}) collective-permute-start(bf16[2,496,256]{2,1,0:T(8,128)(2,1)S(1)} %get-tuple-element.271), channel_id=1, source_target_pairs={{0,4},{2,6},{4,0},{6,2},{8,12},{10,14},{12,8},{14,10},{16,20},{18,... | collective-permute-start | bytes 1523720 | tf_op jit(solution)/shard_map/ppermute | solution.py:23
  194.6 19.0 %collective-permute-start.37 = (bf16[2,448,256]{2,1,0:T(8,128)(2,1)S(1)}, bf16[2,448,256]{2,1,0:T(8,128)(2,1)S(1)}, u32[]{:S(2)}, u32[]{:S(2)}) collective-permute-start(bf16[2,448,256]{2,1,0:T(8,128)(2,1)S(1)} %get-tuple-element.273), channel_id=1, source_target_pairs={{0,8},{2,10},{4,12},{6,14},{8,0},{10,2},{12,4},{14,6},{16,24},{18,... | collective-permute-start | bytes 1376264 | tf_op jit(solution)/shard_map/ppermute | solution.py:23
  196.4 17.3 %collective-permute-start.38 = (bf16[2,448,256]{2,1,0:T(8,128)(2,1)S(1)}, bf16[2,448,256]{2,1,0:T(8,128)(2,1)S(1)}, u32[]{:S(2)}, u32[]{:S(2)}) collective-permute-start(bf16[2,448,256]{2,1,0:T(8,128)(2,1)S(1)} %get-tuple-element.275), channel_id=1, source_target_pairs={{0,2},{2,0},{4,6},{6,4},{8,10},{10,8},{12,14},{14,12},{16,18},{18,... | collective-permute-start | bytes 1376264 | tf_op jit(solution)/shard_map/ppermute | solution.py:23
  197.5 18.1 %collective-permute-start.42 = (bf16[48,3072]{1,0:T(8,128)(2,1)S(1)}, bf16[48,3072]{1,0:T(8,128)(2,1)S(1)}, u32[]{:S(2)}, u32[]{:S(2)}) collective-permute-start(bf16[48,3072]{1,0:T(8,128)(2,1)S(1)} %get-tuple-element.281), channel_id=1, source_target_pairs={{0,16},{2,18},{4,20},{6,22},{8,24},{10,26},{12,28},{14,30},{16,0},... | collective-permute-start | bytes 884744 | tf_op jit(solution)/shard_map/ppermute | solution.py:23
  (27 other events, 195.3 us)

commit v2 on v1

--- a/solution.py
+++ b/solution.py
@@ -226,10 +226,15 @@
     q_ref[half_rows:, :] = dot_plain(other_ref[:half_rows, :], query_weight_ref[...]).astype(jnp.bfloat16)
     kv_ref[:half_kv, :] = own_kv_ref[...]
     step = 512
-    for start in range(0, half_kv, step):
-        kv_ref[half_kv + start : half_kv + start + step, :] = dot_plain(
-            other_ref[start : start + step, :], kv_weight_ref[...]
+
+    def one_part(at, carry):
+        lines = pl.ds(pl.multiple_of(at * step, step), step)
+        kv_ref[pl.ds(pl.multiple_of(half_kv + at * step, step), step), :] = dot_plain(
+            other_ref[lines, :], kv_weight_ref[...]
         ).astype(jnp.bfloat16)
+        return carry
+
+    lax.fori_loop(0, half_kv // step, one_part, 0)
     low_lanes = lax.broadcasted_iota(jnp.int32, (BLOCK, PAIR), 1) < HEAD
     most = (numbers_ref.shape[0] - 1) // (2 + pairs * SLOTS)
 
@@ -565,10 +570,13 @@
     rows = query_ref.shape[0]
     query_ref[...] = dot_plain(x_ref[:rows, :], query_weight_ref[...]).astype(jnp.bfloat16)
     step = 512
-    for start in range(0, kv_ref.shape[0], step):
-        kv_ref[start : start + step, :] = dot_plain(x_ref[start : start + step, :], kv_weight_ref[...]).astype(
-            jnp.bfloat16
-        )
+
+    def one_part(at, carry):
+        lines = pl.ds(pl.multiple_of(at * step, step), step)
+        kv_ref[lines, :] = dot_plain(x_ref[lines, :], kv_weight_ref[...]).astype(jnp.bfloat16)
+        return carry
+
+    lax.fori_loop(0, kv_ref.shape[0] // step, one_part, 0)
 
 
 def project_kernel(mixed_ref, weight_ref, own_ref, other_ref, low_ref):
@@ -772,11 +780,20 @@
 
 def token_other_kernel(kv_grad_ref, query_grad_ref, kv_weight_ref, query_weight_ref, out_ref):
     near, half = query_grad_ref.shape[0] // 2, kv_grad_ref.shape[0] // 2
-    for start in range(0, half, near):
-        total = dot_cols(kv_grad_ref[half + start : half + start + near, :], kv_weight_ref[...])
-        if start == 0:
-            total += dot_cols(query_grad_ref[near:, :], query_weight_ref[...])
-        out_ref[start : start + near, :] = total.astype(jnp.bfloat16)
+    step = 512
+
+    def one_part(at, carry):
+        lines = pl.ds(pl.multiple_of(half + at * step, step), step)
+        total = dot_cols(kv_grad_ref[lines, :], kv_weight_ref[...])
+        out_ref[pl.ds(pl.multiple_of(at * step, step), step), :] = total.astype(jnp.bfloat16)
+        return carry
+
+    lax.fori_loop(1, half // step, one_part, 0)
+    total = dot_cols(kv_grad_ref[half : half + step, :], kv_weight_ref[...])
+    total = jnp.concatenate(
+        [total[:near] + dot_cols(query_grad_ref[near:, :], query_weight_ref[...]), total[near:]], 0
+    )
+    out_ref[:step, :] = total.astype(jnp.bfloat16)
 
 
 def token_other(kv_grad, query_grad, kv_weight, query_weight):
@@ -886,7 +903,10 @@
         send_ref[:, width:] = in_pieces(made_ref[half:, width:]).astype(jnp.bfloat16)
 
 
-def end_kernel(made_ref, came_ref, query_ref, key_ref, value_ref, output_ref, small_ref):
+def end_kernel(
+    core_ref, made_ref, came_ref, count_own_ref, count_came_ref,
+    query_ref, key_ref, value_ref, output_ref, loss_ref, *norm_refs
+):
     rows, width = query_ref.shape
     total = made_ref[:rows, : 4 * width] + came_ref[:, : 4 * width].astype(jnp.float32)
     query_ref[...] = total[:, :width]
@@ -895,7 +915,14 @@
         first = 2 * width + 2 * at
         key_ref[:, at : at + PAIR] = total[:, first : first + PAIR]
         value_ref[:, at : at + PAIR] = total[:, first + PAIR : first + 2 * PAIR]
-    small_ref[...] = made_ref[:rows, 4 * width :] + from_pieces(came_ref[:, 4 * width :].astype(jnp.float32))
+    small = made_ref[:rows, 4 * width :] + from_pieces(came_ref[:, 4 * width :].astype(jnp.float32))
+    features = 2.0 * rows * core_ref[1].astype(jnp.float32)
+    loss_ref[...] = small[:1, 4:5] / (features * (count_own_ref[0:1, 0:1] + count_came_ref[0:1, 0:1]))
+    lines = jnp.concatenate([small, jnp.zeros((PAIR - rows, PAIR), jnp.float32)], 0).T
+    half = rows // 2
+    mine = jnp.where(core_ref[0] == 0, lines[:, :half], lines[:, half:rows])
+    for at, one_ref in enumerate(norm_refs):
+        one_ref[...] = mine[at : at + 1, :]
 
 
 def merge_kernel(*refs, riders):
@@ -1137,12 +1164,12 @@
         return fold(keep, [[one] for one in came])
 
     small = local_call(small_kernel, [shaped((width, PAIR))], [stats_one, tie(query_grad, stats_came)])[0]
-    wide_keep, wide_send = folded(wide_keep, tie(small, wide_came))
+    token_sent = token_other(tie(small, kv_grad), query_grad, full_kv, full_query)
+    wide_keep, wide_send = folded(wide_keep, tie(token_sent, wide_came))
     wide_came = step(wide_send, 1)
-    token_sent = token_other(tie(wide_keep[0], kv_grad), query_grad, full_kv, full_query)
-    token_came = swap_core(token_sent)
+    token_came = swap_core(tie(wide_keep[0], token_sent))
     made = narrow_gradients(
-        own, other, tie(token_sent, kv_grad), query_grad, grad_attn_own, grad_attn_other, attended
+        own, other, tie(wide_keep[0], kv_grad), query_grad, grad_attn_own, grad_attn_other, attended
     )
     keep, send = token_own(
         owner, kv_grad, query_grad, full_kv, full_query, tie(made, token_came), made, small, scatter_masks
@@ -1193,21 +1220,26 @@
         last_kernel, [made_shape] + send_shape + [half_shape], [grad_first] + both(keep, came), free=1
     )
     made, send = made[0], made[1:]
+    half = each // 2
     if far_count == 2:
         weight_shape = shaped((each, head_width))
-        part_query, part_key, part_value, part_output, small = local_call(
-            end_kernel, [weight_shape] * 4 + [shaped((each, PAIR))], [made, swap_mask(send[0], 1 << far_bits[0])],
-            free=5,
+        outs = local_call(
+            end_kernel, [weight_shape] * 4 + [shaped((1, 1))] + [shaped((1, half))] * 4,
+            [made, swap_mask(send[0], 1 << far_bits[0]), count_own, count_came],
+            [jnp.stack([core, jnp.int32(devices)])], free=9,
         )
+        part_query, part_key, part_value, part_output = outs[:4]
+        loss_value = outs[4].reshape(())
+        norm_parts = [one.reshape(half) for one in outs[5:]]
     else:
         narrow_sum = far_scatter(made[:, : 4 * head_width])
         small = far_scatter(made[:, 4 * head_width :], jnp.float32)
         part_query, part_output = narrow_sum[:, :head_width], narrow_sum[:, head_width : 2 * head_width]
         kv_sum = narrow_sum[:, 2 * head_width :].reshape(each, head_width // PAIR, 2, PAIR)
         part_key, part_value = (kv_sum[:, :, one].reshape(each, head_width) for one in range(2))
-    loss_value = small[0, 4] / (2.0 * width * (count_own[0, 0] + count_came[0, 0]))
-    half = each // 2
-    mine = jnp.where(core == 0, small[:half], small[half:])
+        loss_value = small[0, 4] / (2.0 * width * (count_own[0, 0] + count_came[0, 0]))
+        mine = jnp.where(core == 0, small[:half], small[half:])
+        norm_parts = [mine[:, at] for at in range(4)]
     return (
         result,
         loss_value,
@@ -1218,10 +1250,7 @@
         part_output,
         part_inner,
         part_outer,
-        mine[:, 0],
-        mine[:, 1],
-        mine[:, 2],
-        mine[:, 3],
+        *norm_parts,
     )
 
 

time: 241 us -> 225 us (0.934)
  Pallas kernels: 74.1 us -> 65.2 us
  waiting for transfers between devices: 94.8 us -> 99.2 us
  starting transfers between devices: 55.1 us -> 51.4 us
  between operations: 4.49 us -> 1.22 us
    pallas_call x27, Pallas kernels: 71.8 us -> 63 us  [local_call(): pl.pallas_call(kernel, out_shape=tuple((one if len(outs) - at <= free els...]
    ppermute x34, waiting for transfers between devices: 90 us -> 94.4 us  [swap_mask(): lax.ppermute(block, 'dp', [(one, one ^ mask) for one in range(count)])]
    ppermute x34, starting transfers between devices: 52.3 us -> 49.5 us  [swap_mask(): lax.ppermute(block, 'dp', [(one, one ^ mask) for one in range(count)])]
  transfers between devices with their start and end apart: 44 -> 44, of which waited for: 22 -> 21; matrix products, arithmetic and copies ran while one was open for 3% -> 3% of each run, Pallas kernels for 23% -> 21%
where the time goes in v2:
time: 225 us; the launch traced here: 224 us
  waiting for transfers between devices  99.2 us (44%)
  Pallas kernels  65.2 us (29%)
  starting transfers between devices  51.4 us (23%)
  other arithmetic  3.87 us (2%)
  local copies, waits for them, and re-layouts  2.6 us (1%)
    ppermute x34, waiting for transfers between devices, swap_mask(): lax.ppermute(block, 'dp', [(one, one ^ mask) for one in range(count)])  94.4 us
    pallas_call x27, Pallas kernels, local_call(): pl.pallas_call(kernel, out_shape=tuple((one if len(outs) - at <= free els...  63 us
    ppermute x34, starting transfers between devices, swap_mask(): lax.ppermute(block, 'dp', [(one, one ^ mask) for one in range(count)])  49.5 us
    ppermute x10, waiting for transfers between devices, swap_core(): return lax.ppermute(block, 'tensor', [(0, 1), (1, 0)])  4.84 us
  transfers between devices with their start and end apart: 44, of which 21 were waited for; matrix products, arithmetic and copies ran while one was open for 3% of the time, Pallas kernels for 21%

profile of v2, /device:TPU:0, one launch (start us, length us, event | category | flops | bytes accessed | tf_op | source)
XLA Modules:
  0.0 224.5 jit_solution(4290978479494546569)
XLA Ops:
  1.9 4.1 %collective-permute-start.3 = (bf16[1,48,1536]{2,1,0:T(8,128)(2,1)S(1)}, bf16[1,48,1536]{2,1,0:T(8,128)(2,1)S(1)}, u32[]{:S(2)}, u32[]{:S(2)}) collective-permute-start(bf16[1,48,1536]{2,1,0:T(8,128)(2,1)S(1)} %bitcast.56), channel_id=1, source_target_pairs={{0,16},{2,18},{4,20},{6,22},{8,24},{10,26},{12,28},{14,30},{16,0},... | collective-permute-start | bytes 442376 | tf_op jit(solution)/shard_map/ppermute | solution.py:23
  18.8 5.2 %collective-permute-start.6 = (bf16[704,256]{1,0:T(8,128)(2,1)S(1)}, bf16[704,256]{1,0:T(8,128)(2,1)S(1)}, u32[]{:S(2)}, u32[]{:S(2)}) collective-permute-start(bf16[704,256]{1,0:T(8,128)(2,1)S(1)} %get-tuple-element.167.refs_4_), channel_id=1, source_target_pairs={{0,2},{2,0},{4,6},{6,4},{8,10},{10,8},{12,14},{14,12},{16,18},{18,... | collective-permute-start | bytes 1081352 | tf_op jit(solution)/shard_map/ppermute | solution.py:23
  24.0 3.1 %collective-permute-done.7 = bf16[1,48,3200]{2,1,0:T(8,128)(2,1)S(1)} collective-permute-done((bf16[1,48,3200]{2,1,0:T(8,128)(2,1)S(1)}, bf16[1,48,3200]{2,1,0:T(8,128)(2,1)S(1)}, u32[]{:S(2)}, u32[]{:S(2)}) %collective-permute-start.7) | collective-permute-done | bytes 307232 | tf_op jit(solution)/shard_map/ppermute | solution.py:23
  27.2 5.9 %collective-permute-done.5.refs_3_ = bf16[704,256]{1,0:T(8,128)(2,1)S(1)} collective-permute-done((bf16[704,256]{1,0:T(8,128)(2,1)S(1)}, bf16[704,256]{1,0:T(8,128)(2,1)S(1)}, u32[]{:S(2)}, u32[]{:S(2)}) %collective-permute-start.5) | collective-permute-done | bytes 360480 | tf_op jit(solution)/shard_map/ppermute | solution.py:23
  38.8 17.3 %collective-permute-done.8.refs_1_ = bf16[1792,256]{1,0:T(8,128)(2,1)} collective-permute-done((bf16[1792,256]{1,0:T(8,128)(2,1)S(1)}, bf16[1792,256]{1,0:T(8,128)(2,1)}, u32[]{:S(2)}, u32[]{:S(2)}) %collective-permute-start.8) | collective-permute-done | bytes 917536 | tf_op jit(solution)/shard_map/ppermute | solution.py:23
  57.0 2.1 shard_map.250
  62.5 18.1 %collective-permute-done.11.refs_1_ = bf16[1536,256]{1,0:T(8,128)(2,1)S(1)} collective-permute-done((bf16[1536,256]{1,0:T(8,128)(2,1)S(1)}, bf16[1536,256]{1,0:T(8,128)(2,1)S(1)}, u32[]{:S(2)}, u32[]{:S(2)}) %collective-permute-start.11) | collective-permute-done | bytes 786464 | tf_op jit(solution)/shard_map/ppermute | solution.py:23
  84.8 3.5 %shard_map.253 = (bf16[256,384]{1,0:T(8,128)(2,1)S(1)}, bf16[2048,768]{1,0:T(8,128)(2,1)S(1)}) custom-call(bf16[2048,768]{1,0:T(8,128)(2,1)S(1)} %get-tuple-element.178.x_ref.own_ref, bf16[768,384]{1,0:T(8,128)(2,1)S(1)} %get-tuple-element.190.query_weight_ref, bf16[768,768]{1,0:T(8,128)(2,1)S(1)} %get-tuple-element.191.kv_weight_ref), custom_call_target="tpu_custom_call" | custom-call | flops 1000 | bytes 1000 | tf_op jit(solution)/shard_map/pallas_call | solution.py:70
  88.3 10.2 %shard_map.254 = (f32[512,384]{1,0:T(8,128)S(1)}, f32[24,8,128]{2,1,0:T(8,128)S(1)}, bf16[512,384]{1,0:T(8,128)(2,1)S(1)}, bf16[4096,768]{1,0:T(8,128)(2,1)S(1)}) custom-call(s32[501]{0:T(512)S(1)} %pad_add_fusion.numbers_ref, f32[8,128]{1,0:T(8,128)S(1)} %pad_maximum_fusion.3.query_side_ref, f32[4096,128]{1,0:T(8,128)S(1)} %broadcast_in_dim.143.key_side_ref, ...), custom_call_target="tpu_custom_call" | custom-call | flops 1000 | bytes 1000 | tf_op jit(solution)/shard_map/pallas_call | solution.py:70
  104.5 3.3 %shard_map.258 = (f32[256,768]{1,0:T(8,128)S(1)}, bf16[256,768]{1,0:T(8,128)(2,1)S(1)}, bf16[512,1536]{1,0:T(8,128)(2,1)S(1)}, f32[512,1536]{1,0:T(8,128)S(1)}, f32[8,128]{1,0:T(8,128)S(1)}) custom-call(bf16[256,768]{1,0:T(8,128)(2,1)S(1)} %get-tuple-element.202.own_hidden_ref, bf16[256,768]{1,0:T(8,128)(2,1)S(1)} %collective-permute-done.19.other_hidden_ref, ...), custom_call_target="tpu_custom_call" | custom-call | flops 1000 | bytes 1000 | tf_op jit(solution)/shard_map/pallas_call | solution.py:70
  112.8 3.1 %shard_map.260 = (bf16[512,1536]{1,0:T(8,128)(2,1)S(1)}, f32[256,768]{1,0:T(8,128)S(1)}, bf16[256,768]{1,0:T(8,128)(2,1)S(1)}) custom-call(bf16[256,768]{1,0:T(8,128)(2,1)S(1)} %get-tuple-element.223.own_grad_ref, bf16[256,768]{1,0:T(8,128)(2,1)S(1)} %collective-permute-done.22.other_grad_ref, f32[512,1536]{1,0:T(8,128)S(1)} %get-tuple-element.224.slope_ref, ...), custom_call_target="tpu_custom_call" | custom-call | flops 1000 | bytes 1000 | tf_op jit(solution)/shard_map/pallas_call | solution.py:70
  116.1 4.4 %shard_map.261 = (f32[8,48,1024]{2,1,0:T(8,128)S(1)}, bf16[8,48,1024]{2,1,0:T(8,128)(2,1)}, f32[8,48,1024]{2,1,0:T(8,128)S(1)}, bf16[8,48,1024]{2,1,0:T(8,128)(2...) custom-call(s32[16]{0:T(128)S(1)} %add.229.owner_ref, ...), custom_call_target="tpu_custom_call" | custom-call | flops 1000 | bytes 1000 | tf_op jit(solution)/shard_map/pallas_call | solution.py:70
  122.3 1.9 collective-permute-start.28
  126.7 11.5 %shard_map.263 = (bf16[512,384]{1,0:T(8,128)(2,1)S(1)}, bf16[4096,768]{1,0:T(8,128)(2,1)S(1)}) custom-call(s32[501]{0:T(512)S(1)} %pad_add_fusion.numbers_ref, f32[8,128]{1,0:T(8,128)S(1)} %pad_maximum_fusion.3.query_side_ref, f32[4096,128]{1,0:T(8,128)S(1)} %broadcast_in_dim.143.key_side_ref, bf16[512,384]{1,0:T(8,128)(2,1)S(1)} %get-tuple-element.234.q_ref, ...), custom_call_target="tpu_custom_call" | custom-call | flops 1000 | bytes 1000 | tf_op jit(solution)/shard_map/pallas_call | solution.py:70
  138.3 3.4 %shard_map.265 = bf16[2048,768]{1,0:T(8,128)(2,1)S(1)} custom-call(bf16[4096,768]{1,0:T(8,128)(2,1)S(1)} %get-tuple-element.253.kv_grad_ref, bf16[512,384]{1,0:T(8,128)(2,1)S(1)} %get-tuple-element.239.query_grad_ref, bf16[768,768]{1,0:T(8,128)(2,1)S(1)} %get-tuple-element.191.kv_weight_ref, bf16[768,384]{1,0:T(8,128)(2,1)S(1)} %get-tuple-element.190.query_weight_ref), custom_call_target="tpu_custom_call" | custom-call | flops 1000 | bytes 1000 | tf_op jit(solution)/shard_map/pallas_call | solution.py:70
  144.6 1.9 collective-permute-start.32
  146.5 5.9 %shard_map.267.made_ref = f32[768,1536]{1,0:T(8,128)S(1)} custom-call(bf16[2048,768]{1,0:T(8,128)(2,1)S(1)} %get-tuple-element.178.x_ref.own_ref, bf16[2048,768]{1,0:T(8,128)(2,1)S(1)} %collective-permute-done.14.other_ref, bf16[4096,768]{1,0:T(8,128)(2,1)S(1)} %get-tuple-element.253.kv_grad_ref, bf16[512,384]{1,0:T(8,128)(2,1)S(1)} %get-tuple-element.239.query_grad_ref, ...), custom_call_target="tpu_custom_call" | custom-call | flops 1000 | bytes 1000 | tf_op jit(solution)/shard_map/pallas_call | solution.py:70
  152.5 3.7 %shard_map.268 = (f32[4,496,256]{2,1,0:T(8,128)S(1)}, bf16[4,496,256]{2,1,0:T(8,128)(2,1)S(1)}, f32[4,448,256]{2,1,0:T(8,128)S(1)}, bf16[4,448,256]{2,1,0:T(8,12...) custom-call(s32[16]{0:T(128)S(1)} %add.229.owner_ref, ...), custom_call_target="tpu_custom_call" | custom-call | flops 1000 | bytes 1000 | tf_op jit(solution)/shard_map/pallas_call | solution.py:70
  158.6 24.5 %collective-permute-done.34.refs_4_ = bf16[2176,256]{1,0:T(8,128)(2,1)S(1)} collective-permute-done((bf16[2176,256]{1,0:T(8,128)(2,1)S(1)}, bf16[2176,256]{1,0:T(8,128)(2,1)S(1)}, u32[]{:S(2)}, u32[]{:S(2)}) %collective-permute-start.34) | collective-permute-done | bytes 1114144 | tf_op jit(solution)/shard_map/ppermute | solution.py:23
  187.8 5.5 %collective-permute-start.42 = (bf16[48,3072]{1,0:T(8,128)(2,1)S(1)}, bf16[48,3072]{1,0:T(8,128)(2,1)S(1)}, u32[]{:S(2)}, u32[]{:S(2)}) collective-permute-start(bf16[48,3072]{1,0:T(8,128)(2,1)S(1)} %get-tuple-element.287), channel_id=1, source_target_pairs={{0,16},{2,18},{4,20},{6,22},{8,24},{10,26},{12,28},{14,30},{16,0},... | collective-permute-start | bytes 884744 | tf_op jit(solution)/shard_map/ppermute | solution.py:23
  193.3 10.1 %collective-permute-done.37.refs_3_ = bf16[2,448,256]{2,1,0:T(8,128)(2,1)S(1)} collective-permute-done((bf16[2,448,256]{2,1,0:T(8,128)(2,1)S(1)}, bf16[2,448,256]{2,1,0:T(8,128)(2,1)S(1)}, u32[]{:S(2)}, u32[]{:S(2)}) %collective-permute-start.37) | collective-permute-done | bytes 458784 | tf_op jit(solution)/shard_map/ppermute | solution.py:23
  206.6 3.4 %collective-permute-done.40.refs_3_ = bf16[1,448,256]{2,1,0:T(8,128)(2,1)S(1)} collective-permute-done((bf16[1,448,256]{2,1,0:T(8,128)(2,1)S(1)}, bf16[1,448,256]{2,1,0:T(8,128)(2,1)S(1)}, u32[]{:S(2)}, u32[]{:S(2)}) %collective-permute-start.40) | collective-permute-done | bytes 229408 | tf_op jit(solution)/shard_map/ppermute | solution.py:23
  212.5 6.1 %collective-permute-start.43 = (bf16[48,1664]{1,0:T(8,128)(2,1)S(1)}, bf16[48,1664]{1,0:T(8,128)(2,1)S(1)}, u32[]{:S(2)}, u32[]{:S(2)}) collective-permute-start(bf16[48,1664]{1,0:T(8,128)(2,1)S(1)} %get-tuple-element.295), channel_id=1, source_target_pairs={{0,16},{2,18},{4,20},{6,22},{8,24},{10,26},{12,28},{14,30},{16,0},... | collective-permute-start | bytes 479240 | tf_op jit(solution)/shard_map/ppermute | solution.py:23
  218.6 4.4 %collective-permute-done.43.came_ref = bf16[48,1664]{1,0:T(8,128)(2,1)S(1)} collective-permute-done((bf16[48,1664]{1,0:T(8,128)(2,1)S(1)}, bf16[48,1664]{1,0:T(8,128)(2,1)S(1)}, u32[]{:S(2)}, u32[]{:S(2)}) %collective-permute-start.43) | collective-permute-done | bytes 159776 | tf_op jit(solution)/shard_map/ppermute | solution.py:23
  (165 shorter events, 60.6 us)
Async XLA Ops:
  1.9 14.8 %collective-permute-start.3 = (bf16[1,48,1536]{2,1,0:T(8,128)(2,1)S(1)}, bf16[1,48,1536]{2,1,0:T(8,128)(2,1)S(1)}, u32[]{:S(2)}, u32[]{:S(2)}) collective-permute-start(bf16[1,48,1536]{2,1,0:T(8,128)(2,1)S(1)} %bitcast.56), channel_id=1, source_target_pairs={{0,16},{2,18},{4,20},{6,22},{8,24},{10,26},{12,28},{14,30},{16,0},... | collective-permute-start | bytes 442376 | tf_op jit(solution)/shard_map/ppermute | solution.py:23
  11.7 15.4 %collective-permute-start.7 = (bf16[1,48,3200]{2,1,0:T(8,128)(2,1)S(1)}, bf16[1,48,3200]{2,1,0:T(8,128)(2,1)S(1)}, u32[]{:S(2)}, u32[]{:S(2)}) collective-permute-start(bf16[1,48,3200]{2,1,0:T(8,128)(2,1)S(1)} %bitcast.54), channel_id=1, source_target_pairs={{0,16},{2,18},{4,20},{6,22},{8,24},{10,26},{12,28},{14,30},{16,0},... | collective-permute-start | bytes 921608 | tf_op jit(solution)/shard_map/ppermute | solution.py:23
  18.0 15.1 %collective-permute-start.5 = (bf16[704,256]{1,0:T(8,128)(2,1)S(1)}, bf16[704,256]{1,0:T(8,128)(2,1)S(1)}, u32[]{:S(2)}, u32[]{:S(2)}) collective-permute-start(bf16[704,256]{1,0:T(8,128)(2,1)S(1)} %get-tuple-element.166.refs_2_), channel_id=1, source_target_pairs={{0,8},{2,10},{4,12},{6,14},{8,0},{10,2},{12,4},{14,6},{16,24},{18,... | collective-permute-start | bytes 1081352 | tf_op jit(solution)/shard_map/ppermute | solution.py:23
  18.8 14.4 %collective-permute-start.6 = (bf16[704,256]{1,0:T(8,128)(2,1)S(1)}, bf16[704,256]{1,0:T(8,128)(2,1)S(1)}, u32[]{:S(2)}, u32[]{:S(2)}) collective-permute-start(bf16[704,256]{1,0:T(8,128)(2,1)S(1)} %get-tuple-element.167.refs_4_), channel_id=1, source_target_pairs={{0,2},{2,0},{4,6},{6,4},{8,10},{10,8},{12,14},{14,12},{16,18},{18,... | collective-permute-start | bytes 1081352 | tf_op jit(solution)/shard_map/ppermute | solution.py:23
  34.3 22.1 %collective-permute-start.10 = (bf16[1840,256]{1,0:T(8,128)(2,1)S(1)}, bf16[1840,256]{1,0:T(8,128)(2,1)S(1)}, u32[]{:S(2)}, u32[]{:S(2)}) collective-permute-start(bf16[1840,256]{1,0:T(8,128)(2,1)S(1)} %get-tuple-element.171.refs_4_), channel_id=1, source_target_pairs={{0,4},{2,6},{4,0},{6,2},{8,12},{10,14},{12,8},{14,10},{16,20},{18,... | collective-permute-start | bytes 2826248 | tf_op jit(solution)/shard_map/ppermute | solution.py:23
  35.4 20.8 %collective-permute-start.8 = (bf16[1792,256]{1,0:T(8,128)(2,1)S(1)}, bf16[1792,256]{1,0:T(8,128)(2,1)}, u32[]{:S(2)}, u32[]{:S(2)}) collective-permute-start(bf16[1792,256]{1,0:T(8,128)(2,1)S(1)} %get-tuple-element.169.refs_0_), channel_id=1, source_target_pairs={{0,8},{2,10},{4,12},{6,14},{8,0},{10,2},{12,4},{14,6},{16,24},{18,... | collective-permute-start | bytes 2752520 | tf_op jit(solution)/shard_map/ppermute | solution.py:23
  35.4 21.0 %collective-permute-start.9 = (bf16[1792,256]{1,0:T(8,128)(2,1)}, bf16[1792,256]{1,0:T(8,128)(2,1)}, u32[]{:S(2)}, u32[]{:S(2)}) collective-permute-start(bf16[1792,256]{1,0:T(8,128)(2,1)} %get-tuple-element.170.refs_2_), channel_id=1, source_target_pairs={{0,2},{2,0},{4,6},{6,4},{8,10},{10,8},{12,14},{14,12},{16,18},{18,... | collective-permute-start | bytes 2752520 | tf_op jit(solution)/shard_map/ppermute | solution.py:23
  59.1 29.2 %collective-permute-start.14 = (bf16[2048,768]{1,0:T(8,128)(2,1)S(1)}, bf16[2048,768]{1,0:T(8,128)(2,1)S(1)}, u32[]{:S(2)}, u32[]{:S(2)}) collective-permute-start(bf16[2048,768]{1,0:T(8,128)(2,1)S(1)} %get-tuple-element.178.x_ref.own_ref), channel_id=1, source_target_pairs={{0,1},{1,0},{2,3},{3,2},{4,5},{5,4},{6,7},{7,6},{8,9},{9,8},{10,11... | collective-permute-start | bytes 9437192 | tf_op jit(solution)/shard_map/ppermute | solution.py:27
  59.2 22.4 %collective-permute-start.13 = (bf16[1632,256]{1,0:T(8,128)(2,1)S(1)}, bf16[1632,256]{1,0:T(8,128)(2,1)S(1)}, u32[]{:S(2)}, u32[]{:S(2)}) collective-permute-start(bf16[1632,256]{1,0:T(8,128)(2,1)S(1)} %get-tuple-element.188.refs_4_), channel_id=1, source_target_pairs={{0,8},{2,10},{4,12},{6,14},{8,0},{10,2},{12,4},{14,6},{16,24},{18,... | collective-permute-start | bytes 2506760 | tf_op jit(solution)/shard_map/ppermute | solution.py:23
  61.0 19.6 %collective-permute-start.11 = (bf16[1536,256]{1,0:T(8,128)(2,1)S(1)}, bf16[1536,256]{1,0:T(8,128)(2,1)S(1)}, u32[]{:S(2)}, u32[]{:S(2)}) collective-permute-start(bf16[1536,256]{1,0:T(8,128)(2,1)S(1)} %get-tuple-element.184.refs_0_), channel_id=1, source_target_pairs={{0,2},{2,0},{4,6},{6,4},{8,10},{10,8},{12,14},{14,12},{16,18},{18,... | collective-permute-start | bytes 2359304 | tf_op jit(solution)/shard_map/ppermute | solution.py:23
  62.2 19.3 %collective-permute-start.12 = (bf16[1536,256]{1,0:T(8,128)(2,1)S(1)}, bf16[1536,256]{1,0:T(8,128)(2,1)S(1)}, u32[]{:S(2)}, u32[]{:S(2)}) collective-permute-start(bf16[1536,256]{1,0:T(8,128)(2,1)S(1)} %get-tuple-element.186.refs_2_), channel_id=1, source_target_pairs={{0,4},{2,6},{4,0},{6,2},{8,12},{10,14},{12,8},{14,10},{16,20},{18,... | collective-permute-start | bytes 2359304 | tf_op jit(solution)/shard_map/ppermute | solution.py:23
  81.7 20.6 %collective-permute-start.18 = (bf16[1728,256]{1,0:T(8,128)(2,1)S(1)}, bf16[1728,256]{1,0:T(8,128)(2,1)S(1)}, u32[]{:S(2)}, u32[]{:S(2)}) collective-permute-start(bf16[1728,256]{1,0:T(8,128)(2,1)S(1)} %get-tuple-element.213.refs_4_), channel_id=1, source_target_pairs={{0,2},{2,0},{4,6},{6,4},{8,10},{10,8},{12,14},{14,12},{16,18},{18,... | collective-permute-start | bytes 2654216 | tf_op jit(solution)/shard_map/ppermute | solution.py:23
  82.6 18.2 %collective-permute-start.16 = (bf16[1536,256]{1,0:T(8,128)(2,1)S(1)}, bf16[1536,256]{1,0:T(8,128)(2,1)S(1)}, u32[]{:S(2)}, u32[]{:S(2)}) collective-permute-start(bf16[1536,256]{1,0:T(8,128)(2,1)S(1)} %get-tuple-element.209.refs_0_), channel_id=1, source_target_pairs={{0,4},{2,6},{4,0},{6,2},{8,12},{10,14},{12,8},{14,10},{16,20},{18,... | collective-permute-start | bytes 2359304 | tf_op jit(solution)/shard_map/ppermute | solution.py:23
  83.6 17.9 %collective-permute-start.17 = (bf16[1536,256]{1,0:T(8,128)(2,1)S(1)}, bf16[1536,256]{1,0:T(8,128)(2,1)S(1)}, u32[]{:S(2)}, u32[]{:S(2)}) collective-permute-start(bf16[1536,256]{1,0:T(8,128)(2,1)S(1)} %get-tuple-element.211.refs_2_), channel_id=1, source_target_pairs={{0,8},{2,10},{4,12},{6,14},{8,0},{10,2},{12,4},{14,6},{16,24},{18,... | collective-permute-start | bytes 2359304 | tf_op jit(solution)/shard_map/ppermute | solution.py:23
  120.5 21.3 %collective-permute-start.26 = (bf16[4,96,1024]{2,1,0:T(8,128)(2,1)}, bf16[4,96,1024]{2,1,0:T(8,128)(2,1)S(1)}, u32[]{:S(2)}, u32[]{:S(2)}) collective-permute-start(bf16[4,96,1024]{2,1,0:T(8,128)(2,1)} %bitcast.20), channel_id=1, source_target_pairs={{0,2},{2,0},{4,6},{6,4},{8,10},{10,8},{12,14},{14,12},{16,18},{18,... | collective-permute-start | bytes 2359304 | tf_op jit(solution)/shard_map/ppermute | solution.py:23
  121.3 20.5 %collective-permute-start.27 = (bf16[4,96,1024]{2,1,0:T(8,128)(2,1)S(1)}, bf16[4,96,1024]{2,1,0:T(8,128)(2,1)S(1)}, u32[]{:S(2)}, u32[]{:S(2)}) collective-permute-start(bf16[4,96,1024]{2,1,0:T(8,128)(2,1)S(1)} %bitcast.61), channel_id=1, source_target_pairs={{0,4},{2,6},{4,0},{6,2},{8,12},{10,14},{12,8},{14,10},{16,20},{18,... | collective-permute-start | bytes 2359304 | tf_op jit(solution)/shard_map/ppermute | solution.py:23
  122.3 19.5 %collective-permute-start.28 = (bf16[4,96,1024]{2,1,0:T(8,128)(2,1)S(1)}, bf16[4,96,1024]{2,1,0:T(8,128)(2,1)S(1)}, u32[]{:S(2)}, u32[]{:S(2)}) collective-permute-start(bf16[4,96,1024]{2,1,0:T(8,128)(2,1)S(1)} %bitcast.60), channel_id=1, source_target_pairs={{0,8},{2,10},{4,12},{6,14},{8,0},{10,2},{12,4},{14,6},{16,24},{18,... | collective-permute-start | bytes 2359304 | tf_op jit(solution)/shard_map/ppermute | solution.py:23
  156.6 28.3 %collective-permute-start.33 = (bf16[2368,256]{1,0:T(8,128)(2,1)S(1)}, bf16[2368,256]{1,0:T(8,128)(2,1)S(1)}, u32[]{:S(2)}, u32[]{:S(2)}) collective-permute-start(bf16[2368,256]{1,0:T(8,128)(2,1)S(1)} %get-tuple-element.270), channel_id=1, source_target_pairs={{0,2},{2,0},{4,6},{6,4},{8,10},{10,8},{12,14},{14,12},{16,18},{18,... | collective-permute-start | bytes 3637256 | tf_op jit(solution)/shard_map/ppermute | solution.py:23
  157.9 25.2 %collective-permute-start.34 = (bf16[2176,256]{1,0:T(8,128)(2,1)S(1)}, bf16[2176,256]{1,0:T(8,128)(2,1)S(1)}, u32[]{:S(2)}, u32[]{:S(2)}) collective-permute-start(bf16[2176,256]{1,0:T(8,128)(2,1)S(1)} %get-tuple-element.271), channel_id=1, source_target_pairs={{0,4},{2,6},{4,0},{6,2},{8,12},{10,14},{12,8},{14,10},{16,20},{18,... | collective-permute-start | bytes 3342344 | tf_op jit(solution)/shard_map/ppermute | solution.py:23
  158.2 25.5 %collective-permute-start.35 = (bf16[2176,256]{1,0:T(8,128)(2,1)S(1)}, bf16[2176,256]{1,0:T(8,128)(2,1)S(1)}, u32[]{:S(2)}, u32[]{:S(2)}) collective-permute-start(bf16[2176,256]{1,0:T(8,128)(2,1)S(1)} %get-tuple-element.272), channel_id=1, source_target_pairs={{0,8},{2,10},{4,12},{6,14},{8,0},{10,2},{12,4},{14,6},{16,24},{18,... | collective-permute-start | bytes 3342344 | tf_op jit(solution)/shard_map/ppermute | solution.py:23
  185.8 17.6 %collective-permute-start.36 = (bf16[2,496,256]{2,1,0:T(8,128)(2,1)S(1)}, bf16[2,496,256]{2,1,0:T(8,128)(2,1)S(1)}, u32[]{:S(2)}, u32[]{:S(2)}) collective-permute-start(bf16[2,496,256]{2,1,0:T(8,128)(2,1)S(1)} %get-tuple-element.277), channel_id=1, source_target_pairs={{0,4},{2,6},{4,0},{6,2},{8,12},{10,14},{12,8},{14,10},{16,20},{18,... | collective-permute-start | bytes 1523720 | tf_op jit(solution)/shard_map/ppermute | solution.py:23
  186.2 17.3 %collective-permute-start.37 = (bf16[2,448,256]{2,1,0:T(8,128)(2,1)S(1)}, bf16[2,448,256]{2,1,0:T(8,128)(2,1)S(1)}, u32[]{:S(2)}, u32[]{:S(2)}) collective-permute-start(bf16[2,448,256]{2,1,0:T(8,128)(2,1)S(1)} %get-tuple-element.279), channel_id=1, source_target_pairs={{0,8},{2,10},{4,12},{6,14},{8,0},{10,2},{12,4},{14,6},{16,24},{18,... | collective-permute-start | bytes 1376264 | tf_op jit(solution)/shard_map/ppermute | solution.py:23
  186.7 16.7 %collective-permute-start.38 = (bf16[2,448,256]{2,1,0:T(8,128)(2,1)S(1)}, bf16[2,448,256]{2,1,0:T(8,128)(2,1)S(1)}, u32[]{:S(2)}, u32[]{:S(2)}) collective-permute-start(bf16[2,448,256]{2,1,0:T(8,128)(2,1)S(1)} %get-tuple-element.281), channel_id=1, source_target_pairs={{0,2},{2,0},{4,6},{6,4},{8,10},{10,8},{12,14},{14,12},{16,18},{18,... | collective-permute-start | bytes 1376264 | tf_op jit(solution)/shard_map/ppermute | solution.py:23
  187.8 17.9 %collective-permute-start.42 = (bf16[48,3072]{1,0:T(8,128)(2,1)S(1)}, bf16[48,3072]{1,0:T(8,128)(2,1)S(1)}, u32[]{:S(2)}, u32[]{:S(2)}) collective-permute-start(bf16[48,3072]{1,0:T(8,128)(2,1)S(1)} %get-tuple-element.287), channel_id=1, source_target_pairs={{0,16},{2,18},{4,20},{6,22},{8,24},{10,26},{12,28},{14,30},{16,0},... | collective-permute-start | bytes 884744 | tf_op jit(solution)/shard_map/ppermute | solution.py:23
  (27 other events, 200.8 us)

commit v3 on v2

--- a/solution.py
+++ b/solution.py
@@ -428,10 +428,13 @@
         copy.wait()
 
 
-def weight_start_kernel(*refs):
-    near = refs[9:-1]
-    fetched(refs[:7], near, refs[-1])
-    first_ref, second_ref = refs[7:9]
+def start_kernel(*refs):
+    near = refs[13:-1]
+    fetched(refs[:8], near, refs[-1])
+    first_ref, second_ref, thirds = refs[8], refs[9], refs[10:13]
+    columns = thirds[0].shape[1]
+    for at in range(3):
+        thirds[at][...] = near[7][:, at * columns : (at + 1) * columns]
     for out_ref, sources in ((first_ref, near[:4]), (second_ref, near[4:6])):
         at = 0
         for one in sources:
@@ -439,14 +442,6 @@
             at += one.shape[1]
     count = jnp.sum(near[6][...].astype(jnp.float32), axis=1, keepdims=True)
     second_ref[:, at:] = jnp.broadcast_to(count, (second_ref.shape[0], PAIR)).astype(jnp.bfloat16)
-
-
-def token_start_kernel(tokens_ref, *refs):
-    near_ref, arrived = refs[3:]
-    fetched([tokens_ref], [near_ref], arrived)
-    columns = refs[0].shape[1]
-    for at in range(3):
-        refs[at][...] = near_ref[:, at * columns : (at + 1) * columns]
 
 
 def fetching_call(kernel, outs, sources):
@@ -483,17 +478,21 @@
         put_packed(out_ref, 2 * (rows + tail), second_ref, cuts[at], cuts[at + 1] - cuts[at], slot_rows)
 
 
-def third_pack_kernel(*refs, masks, rows, tail):
+def place_tokens_kernel(*refs, masks, rows):
     out_ref = refs[6]
     columns = refs[0].shape[1]
+    for at, group in enumerate(masks):
+        third = at // 2
+        for slot, mask in enumerate(group):
+            out_ref[mask * rows : (mask + 1) * rows, third * columns : (third + 1) * columns] = refs[at][
+                slot * rows : (slot + 1) * rows, :
+            ]
+
+
+def third_pack_kernel(*refs, tokens, tail):
     for at in range(3):
-        tokens = len(masks[2 * at]) * rows
         for side in range(2):
-            piece, target = refs[2 * at + side], refs[7 + at]
-            for slot, mask in enumerate(masks[2 * at + side]):
-                out_ref[mask * rows : (mask + 1) * rows, at * columns : (at + 1) * columns] = piece[
-                    slot * rows : (slot + 1) * rows, :
-                ]
+            piece, target = refs[2 * at + side], refs[6 + at]
             target[side * tail : (side + 1) * tail, :] = piece[tokens : tokens + tail, :]
             rest = piece.shape[0] - tokens - tail
             base = 2 * tail + side * rest
@@ -778,29 +777,35 @@
     )[0]
 
 
+def turn_kernel(*refs):
+    half = len(refs) // 2
+    for source_ref, out_ref in zip(refs[:half], refs[half:]):
+        out_ref[...] = source_ref[...].astype(jnp.float32).T.astype(jnp.bfloat16)
+
+
 def token_other_kernel(kv_grad_ref, query_grad_ref, kv_weight_ref, query_weight_ref, out_ref):
     near, half = query_grad_ref.shape[0] // 2, kv_grad_ref.shape[0] // 2
     step = 512
 
     def one_part(at, carry):
         lines = pl.ds(pl.multiple_of(half + at * step, step), step)
-        total = dot_cols(kv_grad_ref[lines, :], kv_weight_ref[...])
+        total = dot_plain(kv_grad_ref[lines, :], kv_weight_ref[...])
         out_ref[pl.ds(pl.multiple_of(at * step, step), step), :] = total.astype(jnp.bfloat16)
         return carry
 
     lax.fori_loop(1, half // step, one_part, 0)
-    total = dot_cols(kv_grad_ref[half : half + step, :], kv_weight_ref[...])
+    total = dot_plain(kv_grad_ref[half : half + step, :], kv_weight_ref[...])
     total = jnp.concatenate(
-        [total[:near] + dot_cols(query_grad_ref[near:, :], query_weight_ref[...]), total[near:]], 0
+        [total[:near] + dot_plain(query_grad_ref[near:, :], query_weight_ref[...]), total[near:]], 0
     )
     out_ref[:step, :] = total.astype(jnp.bfloat16)
 
 
 def token_other(kv_grad, query_grad, kv_weight, query_weight):
     return local_call(
-        token_other_kernel, [shaped((kv_grad.shape[0] // 2, kv_weight.shape[0]), jnp.bfloat16)],
+        token_other_kernel, [shaped((kv_grad.shape[0] // 2, kv_weight.shape[1]), jnp.bfloat16)],
         [kv_grad, query_grad, kv_weight, query_weight],
-        flops=kv_grad.size * kv_weight.shape[0], spare=12,
+        flops=kv_grad.size * kv_weight.shape[1], spare=12,
     )[0]
 
 
@@ -818,9 +823,9 @@
     slot_rows = made_ref.shape[1] if placed else made_ref.shape[0] // (2 * half)
     for mask in range(2 * half):
         lines = slice(mask * near, (mask + 1) * near)
-        total = dot_cols(kv_grad_ref[lines, :], kv_weight_ref[...]) + came_ref[lines, :].astype(jnp.float32)
+        total = dot_plain(kv_grad_ref[lines, :], kv_weight_ref[...]) + came_ref[lines, :].astype(jnp.float32)
         if mask == 0:
-            total += dot_cols(query_grad_ref[:near, :], query_weight_ref[...])
+            total += dot_plain(query_grad_ref[:near, :], query_weight_ref[...])
         for third, order in enumerate(masks):
             slot = order.index(mask)
             out_ref = outs[2 * third + slot // half]
@@ -860,7 +865,7 @@
     half = came.shape[0] // near // 2
     blocks, features = owner.shape[0], made.shape[0]
     rows, slot_rows = features // blocks, features // (2 * half)
-    columns = kv_weight.shape[0] // 3
+    columns = kv_weight.shape[1] // 3
     placed = rows % 16 != 0
     if placed:
         made, small = (
@@ -879,28 +884,33 @@
     return list(outs[::2]), list(outs[1::2])
 
 
-def last_kernel(grad_ref, *refs):
-    token_ref, made_ref = refs[-1], refs[6]
-    near, columns = grad_ref.shape[0], refs[0].shape[2]
+def narrow_last_kernel(*refs, near):
+    made_ref = refs[6]
+    columns = refs[0].shape[2]
     slot_rows = made_ref.shape[0]
-    width = 6 * columns
+    width, plain = 6 * columns, near + 2 * slot_rows
     for third in range(3):
-        plain = near + 2 * slot_rows
-        total = refs[2 * third][0, :plain] + refs[2 * third + 1][0, :plain].astype(jnp.float32)
-        if third == 0:
-            small = refs[0][0, plain:] + from_pieces(refs[1][0, plain:].astype(jnp.float32))
-            made_ref[: slot_rows // 2, width:] = small[:, :PAIR]
-            made_ref[slot_rows // 2 :, width:] = small[:, PAIR:]
-        part = slice(third * columns, (third + 1) * columns)
-        token_ref[:, part] = grad_ref[:, part] + total[:near]
+        total = refs[2 * third][0, near:plain] + refs[2 * third + 1][0, near:plain].astype(jnp.float32)
         for side in range(2):
             at = (2 * third + side) * columns
-            made_ref[:, at : at + columns] = total[near + side * slot_rows : near + (side + 1) * slot_rows]
-    if len(refs) > 8:
-        send_ref = refs[7]
+            made_ref[:, at : at + columns] = total[side * slot_rows : (side + 1) * slot_rows]
+    small = refs[0][0, plain:] + from_pieces(refs[1][0, plain:].astype(jnp.float32))
+    made_ref[: slot_rows // 2, width:] = small[:, :PAIR]
+    made_ref[slot_rows // 2 :, width:] = small[:, PAIR:]
+    if len(refs) > 7:
         half = slot_rows // 2
-        send_ref[:, :width] = made_ref[half:, :width].astype(jnp.bfloat16)
-        send_ref[:, width:] = in_pieces(made_ref[half:, width:]).astype(jnp.bfloat16)
+        refs[7][:, :width] = made_ref[half:, :width].astype(jnp.bfloat16)
+        refs[7][:, width:] = in_pieces(made_ref[half:, width:]).astype(jnp.bfloat16)
+
+
+def token_end_kernel(grad_ref, *refs):
+    out_ref = refs[-1]
+    near, columns = grad_ref.shape[0], refs[0].shape[2]
+    for third in range(3):
+        part = slice(third * columns, (third + 1) * columns)
+        out_ref[:, part] = grad_ref[:, part] + (
+            refs[2 * third][0, :near] + refs[2 * third + 1][0, :near].astype(jnp.float32)
+        )
 
 
 def end_kernel(
@@ -940,9 +950,8 @@
             ]
 
 
-def part_kernel(*refs, riders, plain):
-    keeps, cames, kept = refs[:3], refs[3:6], refs[6:9]
-    outs, wide_ref = refs[9:15], refs[15]
+def part_kernel(*refs, plain):
+    keeps, cames, outs = refs[:3], refs[3:6], refs[6:12]
     for third in range(3):
         keep_ref, came_ref = keeps[third], cames[third]
         slots, lines, _ = keep_ref.shape
@@ -957,17 +966,21 @@
                     came_ref[base + most : base + lines, :].astype(jnp.float32)
                 )
                 out_ref[at, most:] = (in_pieces(total) if side else total).astype(out_ref.dtype)
+
+
+def wide_end_kernel(*refs, riders, lengths):
+    cames, kept, wide_ref = refs[:3], refs[3:6], refs[6]
     for third, rider in enumerate(riders):
-        slots, lines, columns = keeps[rider].shape
         rows, width = kept[third].shape
+        columns = cames[rider].shape[1]
         for chunk in range(width // columns):
             part = slice(chunk * columns, (chunk + 1) * columns)
-            base = slots * lines + chunk * rows
+            base = lengths[rider] + chunk * rows
             wide_ref[:, third * width + chunk * columns : third * width + (chunk + 1) * columns] = kept[third][
                 :, part
             ] + cames[rider][base : base + rows, :].astype(jnp.float32)
-    if len(refs) > 16:
-        refs[16][...] = wide_ref[wide_ref.shape[0] // 2 :, :].astype(jnp.bfloat16)
+    if len(refs) > 7:
+        refs[7][...] = wide_ref[wide_ref.shape[0] // 2 :, :].astype(jnp.bfloat16)
 
 
 def wide_out_kernel(made_ref, came_ref, outer_ref, inner_ref):
@@ -1037,13 +1050,11 @@
     cuts = (0, 2 * wide // 3, 4 * wide // 3, 2 * wide + PAIR)
     sizes = [packed_rows(slot_rows, last - first) for first, last in zip(cuts, cuts[1:])]
     valid_row = valid_tokens.reshape(1, rows)
-    first, second = fetching_call(
-        weight_start_kernel,
-        [shaped((each, 4 * head_width), jnp.bfloat16), shaped((each, cuts[3]), jnp.bfloat16)],
-        [query_weight, key_weight, value_weight, output_weight, inner_weight, outer_weight, valid_row],
-    )
-    held = list(
-        fetching_call(token_start_kernel, [shaped((rows, third), jnp.bfloat16)] * 3, [tie(first, tokens)])
+    first, second, *held = fetching_call(
+        start_kernel,
+        [shaped((each, 4 * head_width), jnp.bfloat16), shaped((each, cuts[3]), jnp.bfloat16)]
+        + [shaped((rows, third), jnp.bfloat16)] * 3,
+        [query_weight, key_weight, value_weight, output_weight, inner_weight, outer_weight, valid_row, tokens],
     )
     came = step(held, 0)
     first_held, second_held = far_gather(first), far_gather(second)
@@ -1062,12 +1073,16 @@
     tables, owner, came = lax.optimization_barrier((tables, owner, came))
     sent_masks = [tuple(slot_masks(bits[:2])) for bits in ROUTES]
     came_masks = [tuple(mask ^ (1 << bits[2]) for mask in sent) for sent, bits in zip(sent_masks, ROUTES)]
-    own, *held = local_call(
-        functools.partial(third_pack_kernel, masks=tuple(both(sent_masks, came_masks)), rows=rows, tail=2 * tail),
-        [shaped((span * rows, width), jnp.bfloat16)] + messages([4 * tail + 2 * size for size in sizes]),
-        both(held, came),
+    arrived = both(held, came)
+    held = local_call(
+        functools.partial(third_pack_kernel, tokens=4 * rows, tail=2 * tail),
+        messages([4 * tail + 2 * size for size in sizes]), arrived,
     )
     came = step(held, 0)
+    own = local_call(
+        functools.partial(place_tokens_kernel, masks=tuple(both(sent_masks, came_masks)), rows=rows),
+        [shaped((span * rows, width), jnp.bfloat16)], [tie(held[0], arrived[0])] + arrived[1:],
+    )[0]
     other = swap_core(own)
     late = local_call(
         functools.partial(fourth_pack_kernel, skip=4 * tail), messages([4 * size for size in sizes]),
@@ -1103,7 +1118,12 @@
         project_kernel, [half_shape, low_shape, shaped(mixed.shape, jnp.bfloat16)], [mixed, full_output],
         flops=2 * mixed.size * width,
     )
-    part_came, late, late_came = lax.optimization_barrier((swap_core(part_other), late, late_came))
+    turned = local_call(
+        turn_kernel, [shaped(one.shape[::-1], jnp.bfloat16) for one in (full_query, full_kv)],
+        [tie(part_own, full_query), full_kv],
+    )
+    part_came, late, late_came, turned = lax.optimization_barrier((swap_core(part_other), late, late_came, turned))
+    turned_query, turned_kv = turned
     first_sum, hidden, hidden_own = local_call(
         first_norm_kernel, [half_shape, half_shape, low_shape],
         [tokens, part_own, part_came, gain_one, shift_one],
@@ -1164,7 +1184,7 @@
         return fold(keep, [[one] for one in came])
 
     small = local_call(small_kernel, [shaped((width, PAIR))], [stats_one, tie(query_grad, stats_came)])[0]
-    token_sent = token_other(tie(small, kv_grad), query_grad, full_kv, full_query)
+    token_sent = token_other(tie(small, kv_grad), query_grad, turned_kv, turned_query)
     wide_keep, wide_send = folded(wide_keep, tie(token_sent, wide_came))
     wide_came = step(wide_send, 1)
     token_came = swap_core(tie(wide_keep[0], token_sent))
@@ -1172,7 +1192,7 @@
         own, other, tie(wide_keep[0], kv_grad), query_grad, grad_attn_own, grad_attn_other, attended
     )
     keep, send = token_own(
-        owner, kv_grad, query_grad, full_kv, full_query, tie(made, token_came), made, small, scatter_masks
+        owner, kv_grad, query_grad, turned_kv, turned_query, tie(made, token_came), made, small, scatter_masks
     )
     riders = tuple([bits[0] for bits in ROUTES].index(bits[2]) for bits in ROUTES)
     columns = width // 3
@@ -1190,12 +1210,14 @@
         half = (one.shape[0] // 2,) + one.shape[1:]
         halves += [shaped(half), shaped(half, jnp.bfloat16)]
     far_send = [shaped((each, 2 * wide), jnp.bfloat16)] if far_count == 2 else []
-    outs = local_call(
-        functools.partial(part_kernel, riders=riders, plain=plain),
-        halves + [shaped((slot_rows, 2 * wide))] + far_send, keep + came + list(wide_keep),
-    )
-    keep, send, wide_sum, wide_send = list(outs[:6:2]), list(outs[1:6:2]), outs[6], outs[7:]
+    cames = came
+    outs = local_call(functools.partial(part_kernel, plain=plain), halves, keep + cames)
+    keep, send = list(outs[::2]), list(outs[1::2])
     came = step(send, 1)
+    wide_sum, *wide_send = local_call(
+        functools.partial(wide_end_kernel, riders=riders, lengths=tuple(one - ride for one in lengths)),
+        [shaped((slot_rows, 2 * wide))] + far_send, [tie(keep[0], cames[0])] + list(cames[1:]) + list(wide_keep),
+    )
 
     def far_scatter(total, dtype=jnp.bfloat16):
         total = total.reshape(far_count, each, total.shape[1])
@@ -1216,16 +1238,19 @@
     came = tie(part_outer, came)
     made_shape = shaped((slot_rows, 4 * head_width + PAIR))
     send_shape = [shaped((each, 4 * head_width + PAIR), jnp.bfloat16)] if far_count == 2 else []
-    *made, grad_tokens = local_call(
-        last_kernel, [made_shape] + send_shape + [half_shape], [grad_first] + both(keep, came), free=1
-    )
-    made, send = made[0], made[1:]
+    arrived = both(keep, came)
+    made, *send = local_call(
+        functools.partial(narrow_last_kernel, near=rows), [made_shape] + send_shape, arrived
+    )
+    grad_tokens = local_call(
+        token_end_kernel, [half_shape], [grad_first, tie(made, arrived[0])] + arrived[1:], free=1
+    )[0]
     half = each // 2
     if far_count == 2:
         weight_shape = shaped((each, head_width))
         outs = local_call(
             end_kernel, [weight_shape] * 4 + [shaped((1, 1))] + [shaped((1, half))] * 4,
-            [made, swap_mask(send[0], 1 << far_bits[0]), count_own, count_came],
+            [made, tie(grad_tokens, swap_mask(send[0], 1 << far_bits[0])), count_own, count_came],
             [jnp.stack([core, jnp.int32(devices)])], free=9,
         )
         part_query, part_key, part_value, part_output = outs[:4]

time: 225 us -> 221 us (0.982)
  starting transfers between devices: 51.4 us -> 45.8 us
  Pallas kernels: 65.2 us -> 68.1 us
    ppermute x34, starting transfers between devices: 49.5 us -> 44 us  [swap_mask(): lax.ppermute(block, 'dp', [(one, one ^ mask) for one in range(count)])]
    pallas_call x27 -> x31, Pallas kernels: 63 us -> 66.7 us  [local_call(): pl.pallas_call(kernel, out_shape=tuple((one if len(outs) - at <= free els...]
  transfers between devices with their start and end apart: 44 -> 44, of which waited for: 21 -> 21; matrix products, arithmetic and copies ran while one was open for 3% -> 3% of each run, Pallas kernels for 21% -> 23%
where the time goes in v3:
time: 221 us
  waiting for transfers between devices  98.1 us (44%)
  Pallas kernels  68.1 us (31%)
  starting transfers between devices  45.8 us (21%)
  other arithmetic  3.88 us (2%)
  local copies, waits for them, and re-layouts  2.6 us (1%)
    ppermute x34, waiting for transfers between devices, swap_mask(): lax.ppermute(block, 'dp', [(one, one ^ mask) for one in range(count)])  93.3 us
    pallas_call x31, Pallas kernels, local_call(): pl.pallas_call(kernel, out_shape=tuple((one if len(outs) - at <= free els...  66.7 us
    ppermute x34, starting transfers between devices, swap_mask(): lax.ppermute(block, 'dp', [(one, one ^ mask) for one in range(count)])  44 us
    ppermute x10, waiting for transfers between devices, swap_core(): return lax.ppermute(block, 'tensor', [(0, 1), (1, 0)])  4.84 us
  transfers between devices with their start and end apart: 44, of which 21 were waited for; matrix products, arithmetic and copies ran while one was open for 3% of the time, Pallas kernels for 23%

profile of v3, /device:TPU:0, one launch (start us, length us, event | category | flops | bytes accessed | tf_op | source)
XLA Modules:
  0.0 220.6 jit_solution(10426695082492135728)
XLA Ops:
  2.1 3.0 %collective-permute-start = (bf16[256,256]{1,0:T(8,128)(2,1)S(1)}, bf16[256,256]{1,0:T(8,128)(2,1)S(1)}, u32[]{:S(2)}, u32[]{:S(2)}) collective-permute-start(bf16[256,256]{1,0:T(8,128)(2,1)S(1)} %get-tuple-element.166.refs_0_), channel_id=1, source_target_pairs={{0,2},{2,0},{4,6},{6,4},{8,10},{10,8},{12,14},{14,12},{16,18},{18,... | collective-permute-start | bytes 393224 | tf_op jit(solution)/shard_map/ppermute | solution.py:23
  8.2 2.6 %collective-permute-start.3 = (bf16[1,48,1536]{2,1,0:T(8,128)(2,1)S(1)}, bf16[1,48,1536]{2,1,0:T(8,128)(2,1)S(1)}, u32[]{:S(2)}, u32[]{:S(2)}) collective-permute-start(bf16[1,48,1536]{2,1,0:T(8,128)(2,1)S(1)} %bitcast.56), channel_id=1, source_target_pairs={{0,16},{2,18},{4,20},{6,22},{8,24},{10,26},{12,28},{14,30},{16,0},... | collective-permute-start | bytes 442376 | tf_op jit(solution)/shard_map/ppermute | solution.py:23
  15.8 9.3 %collective-permute-done.3 = bf16[1,48,1536]{2,1,0:T(8,128)(2,1)S(1)} collective-permute-done((bf16[1,48,1536]{2,1,0:T(8,128)(2,1)S(1)}, bf16[1,48,1536]{2,1,0:T(8,128)(2,1)S(1)}, u32[]{:S(2)}, u32[]{:S(2)}) %collective-permute-start.3) | collective-permute-done | bytes 147488 | tf_op jit(solution)/shard_map/ppermute | solution.py:23
  26.3 4.0 %collective-permute-done.7 = bf16[1,48,3200]{2,1,0:T(8,128)(2,1)S(1)} collective-permute-done((bf16[1,48,3200]{2,1,0:T(8,128)(2,1)S(1)}, bf16[1,48,3200]{2,1,0:T(8,128)(2,1)S(1)}, u32[]{:S(2)}, u32[]{:S(2)}) %collective-permute-start.7) | collective-permute-done | bytes 307232 | tf_op jit(solution)/shard_map/ppermute | solution.py:23
  30.4 2.3 %collective-permute-done.4.refs_1_ = bf16[704,256]{1,0:T(8,128)(2,1)S(1)} collective-permute-done((bf16[704,256]{1,0:T(8,128)(2,1)S(1)}, bf16[704,256]{1,0:T(8,128)(2,1)S(1)}, u32[]{:S(2)}, u32[]{:S(2)}) %collective-permute-start.4) | collective-permute-done | bytes 360480 | tf_op jit(solution)/shard_map/ppermute | solution.py:23
  32.7 2.7 %collective-permute-done.5.refs_3_ = bf16[704,256]{1,0:T(8,128)(2,1)S(1)} collective-permute-done((bf16[704,256]{1,0:T(8,128)(2,1)S(1)}, bf16[704,256]{1,0:T(8,128)(2,1)S(1)}, u32[]{:S(2)}, u32[]{:S(2)}) %collective-permute-start.5) | collective-permute-done | bytes 360480 | tf_op jit(solution)/shard_map/ppermute | solution.py:23
  37.4 2.5 %collective-permute-start.10 = (bf16[1840,256]{1,0:T(8,128)(2,1)S(1)}, bf16[1840,256]{1,0:T(8,128)(2,1)S(1)}, u32[]{:S(2)}, u32[]{:S(2)}) collective-permute-start(bf16[1840,256]{1,0:T(8,128)(2,1)S(1)} %get-tuple-element.176.refs_4_), channel_id=1, source_target_pairs={{0,4},{2,6},{4,0},{6,2},{8,12},{10,14},{12,8},{14,10},{16,20},{18,... | collective-permute-start | bytes 2826248 | tf_op jit(solution)/shard_map/ppermute | solution.py:23
  42.1 11.8 %collective-permute-done.8.refs_1_ = bf16[1792,256]{1,0:T(8,128)(2,1)} collective-permute-done((bf16[1792,256]{1,0:T(8,128)(2,1)S(1)}, bf16[1792,256]{1,0:T(8,128)(2,1)}, u32[]{:S(2)}, u32[]{:S(2)}) %collective-permute-start.8) | collective-permute-done | bytes 917536 | tf_op jit(solution)/shard_map/ppermute | solution.py:23
  61.7 17.6 %collective-permute-done.11.refs_1_ = bf16[1536,256]{1,0:T(8,128)(2,1)S(1)} collective-permute-done((bf16[1536,256]{1,0:T(8,128)(2,1)S(1)}, bf16[1536,256]{1,0:T(8,128)(2,1)S(1)}, u32[]{:S(2)}, u32[]{:S(2)}) %collective-permute-start.11) | collective-permute-done | bytes 786464 | tf_op jit(solution)/shard_map/ppermute | solution.py:23
  83.9 3.5 %shard_map.253 = (bf16[256,384]{1,0:T(8,128)(2,1)S(1)}, bf16[2048,768]{1,0:T(8,128)(2,1)S(1)}) custom-call(bf16[2048,768]{1,0:T(8,128)(2,1)S(1)} %shard_map.250.x_ref.own_ref, bf16[768,384]{1,0:T(8,128)(2,1)S(1)} %get-tuple-element.205.query_weight_ref.refs_0_, bf16[768,768]{1,0:T(8,128)(2,1)S(1)} %get-tuple-element.196.kv_weight_ref.refs_1_), custom_call_target="tpu_custom_call" | custom-call | flops 1000 | bytes 1000 | tf_op jit(solution)/shard_map/pallas_call | solution.py:70
  87.4 10.8 %shard_map.254 = (f32[512,384]{1,0:T(8,128)S(1)}, f32[24,8,128]{2,1,0:T(8,128)S(1)}, bf16[512,384]{1,0:T(8,128)(2,1)S(1)}, bf16[4096,768]{1,0:T(8,128)(2,1)S(1)}) custom-call(s32[501]{0:T(512)S(1)} %pad_add_fusion.numbers_ref, f32[8,128]{1,0:T(8,128)S(1)} %pad_maximum_fusion.3.query_side_ref, f32[4096,128]{1,0:T(8,128)S(1)} %broadcast_in_dim.143.key_side_ref, ...), custom_call_target="tpu_custom_call" | custom-call | flops 1000 | bytes 1000 | tf_op jit(solution)/shard_map/pallas_call | solution.py:70
  103.3 3.3 %shard_map.259 = (f32[256,768]{1,0:T(8,128)S(1)}, bf16[256,768]{1,0:T(8,128)(2,1)S(1)}, bf16[512,1536]{1,0:T(8,128)(2,1)S(1)}, f32[512,1536]{1,0:T(8,128)S(1)}, f32[8,128]{1,0:T(8,128)S(1)}) custom-call(bf16[256,768]{1,0:T(8,128)(2,1)S(1)} %get-tuple-element.210.own_hidden_ref, bf16[256,768]{1,0:T(8,128)(2,1)S(1)} %collective-permute-done.19.other_hidden_ref, ...), custom_call_target="tpu_custom_call" | custom-call | flops 1000 | bytes 1000 | tf_op jit(solution)/shard_map/pallas_call | solution.py:70
  111.5 3.1 %shard_map.261 = (bf16[512,1536]{1,0:T(8,128)(2,1)S(1)}, f32[256,768]{1,0:T(8,128)S(1)}, bf16[256,768]{1,0:T(8,128)(2,1)S(1)}) custom-call(bf16[256,768]{1,0:T(8,128)(2,1)S(1)} %get-tuple-element.234.own_grad_ref, bf16[256,768]{1,0:T(8,128)(2,1)S(1)} %collective-permute-done.22.other_grad_ref, f32[512,1536]{1,0:T(8,128)S(1)} %get-tuple-element.235.slope_ref, ...), custom_call_target="tpu_custom_call" | custom-call | flops 1000 | bytes 1000 | tf_op jit(solution)/shard_map/pallas_call | solution.py:70
  114.8 4.5 %shard_map.262 = (f32[8,48,1024]{2,1,0:T(8,128)S(1)}, bf16[8,48,1024]{2,1,0:T(8,128)(2,1)}, f32[8,48,1024]{2,1,0:T(8,128)S(1)}, bf16[8,48,1024]{2,1,0:T(8,128)(2...) custom-call(s32[16]{0:T(128)S(1)} %add.229.owner_ref, ...), custom_call_target="tpu_custom_call" | custom-call | flops 1000 | bytes 1000 | tf_op jit(solution)/shard_map/pallas_call | solution.py:70
  124.9 12.4 %shard_map.264 = (bf16[512,384]{1,0:T(8,128)(2,1)S(1)}, bf16[4096,768]{1,0:T(8,128)(2,1)S(1)}) custom-call(s32[501]{0:T(512)S(1)} %pad_add_fusion.numbers_ref, f32[8,128]{1,0:T(8,128)S(1)} %pad_maximum_fusion.3.query_side_ref, f32[4096,128]{1,0:T(8,128)S(1)} %broadcast_in_dim.143.key_side_ref, bf16[512,384]{1,0:T(8,128)(2,1)S(1)} %get-tuple-element.230.q_ref, ...), custom_call_target="tpu_custom_call" | custom-call | flops 1000 | bytes 1000 | tf_op jit(solution)/shard_map/pallas_call | solution.py:70
  137.5 3.3 %shard_map.266 = bf16[2048,768]{1,0:T(8,128)(2,1)S(1)} custom-call(bf16[4096,768]{1,0:T(8,128)(2,1)S(1)} %get-tuple-element.262.kv_grad_ref, bf16[512,384]{1,0:T(8,128)(2,1)S(1)} %get-tuple-element.246.query_grad_ref, bf16[768,768]{1,0:T(8,128)(2,1)S(1)} %get-tuple-element.247.kv_weight_ref, bf16[384,768]{1,0:T(8,128)(2,1)S(1)} %get-tuple-element.248.query_weight_ref), custom_call_target="tpu_custom_call" | custom-call | flops 1000 | bytes 1000 | tf_op jit(solution)/shard_map/pallas_call | solution.py:70
  144.4 5.9 %shard_map.268.made_ref = f32[768,1536]{1,0:T(8,128)S(1)} custom-call(bf16[2048,768]{1,0:T(8,128)(2,1)S(1)} %shard_map.250.x_ref.own_ref, bf16[2048,768]{1,0:T(8,128)(2,1)S(1)} %collective-permute-done.14.other_ref, bf16[4096,768]{1,0:T(8,128)(2,1)S(1)} %get-tuple-element.262.kv_grad_ref, bf16[512,384]{1,0:T(8,128)(2,1)S(1)} %get-tuple-element.246.query_grad_ref, ...), custom_call_target="tpu_custom_call" | custom-call | flops 1000 | bytes 1000 | tf_op jit(solution)/shard_map/pallas_call | solution.py:70
  150.4 3.5 %shard_map.269 = (f32[4,496,256]{2,1,0:T(8,128)S(1)}, bf16[4,496,256]{2,1,0:T(8,128)(2,1)S(1)}, f32[4,448,256]{2,1,0:T(8,128)S(1)}, bf16[4,448,256]{2,1,0:T(8,12...) custom-call(s32[16]{0:T(128)S(1)} %add.229.owner_ref, ...), custom_call_target="tpu_custom_call" | custom-call | flops 1000 | bytes 1000 | tf_op jit(solution)/shard_map/pallas_call | solution.py:70
  158.2 23.1 %collective-permute-done.34.refs_4_.refs_1_ = bf16[2176,256]{1,0:T(8,128)(2,1)S(1)} collective-permute-done((bf16[2176,256]{1,0:T(8,128)(2,1)S(1)}, bf16[2176,256]{1,0:T(8,128)(2,1)S(1)}, u32[]{:S(2)}, u32[]{:S(2)}) %collective-permute-start.34) | collective-permute-done | bytes 1114144 | tf_op jit(solution)/shard_map/ppermute | solution.py:23
  186.8 4.0 %collective-permute-start.42 = (bf16[48,3072]{1,0:T(8,128)(2,1)S(1)}, bf16[48,3072]{1,0:T(8,128)(2,1)S(1)}, u32[]{:S(2)}, u32[]{:S(2)}) collective-permute-start(bf16[48,3072]{1,0:T(8,128)(2,1)S(1)} %get-tuple-element.297), channel_id=1, source_target_pairs={{0,16},{2,18},{4,20},{6,22},{8,24},{10,26},{12,28},{14,30},{16,0},... | collective-permute-start | bytes 884744 | tf_op jit(solution)/shard_map/ppermute | solution.py:23
  190.8 10.9 %collective-permute-done.37.refs_3_ = bf16[2,448,256]{2,1,0:T(8,128)(2,1)S(1)} collective-permute-done((bf16[2,448,256]{2,1,0:T(8,128)(2,1)S(1)}, bf16[2,448,256]{2,1,0:T(8,128)(2,1)S(1)}, u32[]{:S(2)}, u32[]{:S(2)}) %collective-permute-start.37) | collective-permute-done | bytes 458784 | tf_op jit(solution)/shard_map/ppermute | solution.py:23
  204.9 3.5 %collective-permute-done.40.refs_3_ = bf16[1,448,256]{2,1,0:T(8,128)(2,1)S(1)} collective-permute-done((bf16[1,448,256]{2,1,0:T(8,128)(2,1)S(1)}, bf16[1,448,256]{2,1,0:T(8,128)(2,1)S(1)}, u32[]{:S(2)}, u32[]{:S(2)}) %collective-permute-start.40) | collective-permute-done | bytes 229408 | tf_op jit(solution)/shard_map/ppermute | solution.py:23
  208.9 5.9 %collective-permute-start.43 = (bf16[48,1664]{1,0:T(8,128)(2,1)S(1)}, bf16[48,1664]{1,0:T(8,128)(2,1)S(1)}, u32[]{:S(2)}, u32[]{:S(2)}) collective-permute-start(bf16[48,1664]{1,0:T(8,128)(2,1)S(1)} %get-tuple-element.305), channel_id=1, source_target_pairs={{0,16},{2,18},{4,20},{6,22},{8,24},{10,26},{12,28},{14,30},{16,0},... | collective-permute-start | bytes 479240 | tf_op jit(solution)/shard_map/ppermute | solution.py:23
  215.8 3.4 %collective-permute-done.43.came_ref = bf16[48,1664]{1,0:T(8,128)(2,1)S(1)} collective-permute-done((bf16[48,1664]{1,0:T(8,128)(2,1)S(1)}, bf16[48,1664]{1,0:T(8,128)(2,1)S(1)}, u32[]{:S(2)}, u32[]{:S(2)}) %collective-permute-start.43) | collective-permute-done | bytes 159776 | tf_op jit(solution)/shard_map/ppermute | solution.py:23
  (168 shorter events, 62.5 us)
Async XLA Ops:
  2.1 23.0 %collective-permute-start = (bf16[256,256]{1,0:T(8,128)(2,1)S(1)}, bf16[256,256]{1,0:T(8,128)(2,1)S(1)}, u32[]{:S(2)}, u32[]{:S(2)}) collective-permute-start(bf16[256,256]{1,0:T(8,128)(2,1)S(1)} %get-tuple-element.166.refs_0_), channel_id=1, source_target_pairs={{0,2},{2,0},{4,6},{6,4},{8,10},{10,8},{12,14},{14,12},{16,18},{18,... | collective-permute-start | bytes 393224 | tf_op jit(solution)/shard_map/ppermute | solution.py:23
  5.1 20.0 %collective-permute-start.1 = (bf16[256,256]{1,0:T(8,128)(2,1)S(1)}, bf16[256,256]{1,0:T(8,128)(2,1)S(1)}, u32[]{:S(2)}, u32[]{:S(2)}) collective-permute-start(bf16[256,256]{1,0:T(8,128)(2,1)S(1)} %get-tuple-element.167.refs_1_), channel_id=1, source_target_pairs={{0,4},{2,6},{4,0},{6,2},{8,12},{10,14},{12,8},{14,10},{16,20},{18,... | collective-permute-start | bytes 393224 | tf_op jit(solution)/shard_map/ppermute | solution.py:23
  6.6 18.5 %collective-permute-start.2 = (bf16[256,256]{1,0:T(8,128)(2,1)S(1)}, bf16[256,256]{1,0:T(8,128)(2,1)S(1)}, u32[]{:S(2)}, u32[]{:S(2)}) collective-permute-start(bf16[256,256]{1,0:T(8,128)(2,1)S(1)} %get-tuple-element.168.refs_2_), channel_id=1, source_target_pairs={{0,8},{2,10},{4,12},{6,14},{8,0},{10,2},{12,4},{14,6},{16,24},{18,... | collective-permute-start | bytes 393224 | tf_op jit(solution)/shard_map/ppermute | solution.py:23
  8.2 16.9 %collective-permute-start.3 = (bf16[1,48,1536]{2,1,0:T(8,128)(2,1)S(1)}, bf16[1,48,1536]{2,1,0:T(8,128)(2,1)S(1)}, u32[]{:S(2)}, u32[]{:S(2)}) collective-permute-start(bf16[1,48,1536]{2,1,0:T(8,128)(2,1)S(1)} %bitcast.56), channel_id=1, source_target_pairs={{0,16},{2,18},{4,20},{6,22},{8,24},{10,26},{12,28},{14,30},{16,0},... | collective-permute-start | bytes 442376 | tf_op jit(solution)/shard_map/ppermute | solution.py:23
  10.8 19.5 %collective-permute-start.7 = (bf16[1,48,3200]{2,1,0:T(8,128)(2,1)S(1)}, bf16[1,48,3200]{2,1,0:T(8,128)(2,1)S(1)}, u32[]{:S(2)}, u32[]{:S(2)}) collective-permute-start(bf16[1,48,3200]{2,1,0:T(8,128)(2,1)S(1)} %bitcast.54), channel_id=1, source_target_pairs={{0,16},{2,18},{4,20},{6,22},{8,24},{10,26},{12,28},{14,30},{16,0},... | collective-permute-start | bytes 921608 | tf_op jit(solution)/shard_map/ppermute | solution.py:23
  36.5 17.3 %collective-permute-start.8 = (bf16[1792,256]{1,0:T(8,128)(2,1)S(1)}, bf16[1792,256]{1,0:T(8,128)(2,1)}, u32[]{:S(2)}, u32[]{:S(2)}) collective-permute-start(bf16[1792,256]{1,0:T(8,128)(2,1)S(1)} %get-tuple-element.184.refs_0_), channel_id=1, source_target_pairs={{0,8},{2,10},{4,12},{6,14},{8,0},{10,2},{12,4},{14,6},{16,24},{18,... | collective-permute-start | bytes 2752520 | tf_op jit(solution)/shard_map/ppermute | solution.py:23
  36.9 17.0 %collective-permute-start.9 = (bf16[1792,256]{1,0:T(8,128)(2,1)}, bf16[1792,256]{1,0:T(8,128)(2,1)}, u32[]{:S(2)}, u32[]{:S(2)}) collective-permute-start(bf16[1792,256]{1,0:T(8,128)(2,1)} %get-tuple-element.175.refs_2_), channel_id=1, source_target_pairs={{0,2},{2,0},{4,6},{6,4},{8,10},{10,8},{12,14},{14,12},{16,18},{18,... | collective-permute-start | bytes 2752520 | tf_op jit(solution)/shard_map/ppermute | solution.py:23
  37.4 16.4 %collective-permute-start.10 = (bf16[1840,256]{1,0:T(8,128)(2,1)S(1)}, bf16[1840,256]{1,0:T(8,128)(2,1)S(1)}, u32[]{:S(2)}, u32[]{:S(2)}) collective-permute-start(bf16[1840,256]{1,0:T(8,128)(2,1)S(1)} %get-tuple-element.176.refs_4_), channel_id=1, source_target_pairs={{0,4},{2,6},{4,0},{6,2},{8,12},{10,14},{12,8},{14,10},{16,20},{18,... | collective-permute-start | bytes 2826248 | tf_op jit(solution)/shard_map/ppermute | solution.py:23
  58.3 29.1 %collective-permute-start.14 = (bf16[2048,768]{1,0:T(8,128)(2,1)S(1)}, bf16[2048,768]{1,0:T(8,128)(2,1)S(1)}, u32[]{:S(2)}, u32[]{:S(2)}) collective-permute-start(bf16[2048,768]{1,0:T(8,128)(2,1)S(1)} %shard_map.250.x_ref.own_ref), channel_id=1, source_target_pairs={{0,1},{1,0},{2,3},{3,2},{4,5},{5,4},{6,7},{7,6},{8,9},{9,8},{10,11... | collective-permute-start | bytes 9437192 | tf_op jit(solution)/shard_map/ppermute | solution.py:27
  58.4 21.9 %collective-permute-start.13 = (bf16[1632,256]{1,0:T(8,128)(2,1)S(1)}, bf16[1632,256]{1,0:T(8,128)(2,1)S(1)}, u32[]{:S(2)}, u32[]{:S(2)}) collective-permute-start(bf16[1632,256]{1,0:T(8,128)(2,1)S(1)} %get-tuple-element.193.refs_4_), channel_id=1, source_target_pairs={{0,8},{2,10},{4,12},{6,14},{8,0},{10,2},{12,4},{14,6},{16,24},{18,... | collective-permute-start | bytes 2506760 | tf_op jit(solution)/shard_map/ppermute | solution.py:23
  59.6 19.6 %collective-permute-start.11 = (bf16[1536,256]{1,0:T(8,128)(2,1)S(1)}, bf16[1536,256]{1,0:T(8,128)(2,1)S(1)}, u32[]{:S(2)}, u32[]{:S(2)}) collective-permute-start(bf16[1536,256]{1,0:T(8,128)(2,1)S(1)} %get-tuple-element.189.refs_0_), channel_id=1, source_target_pairs={{0,2},{2,0},{4,6},{6,4},{8,10},{10,8},{12,14},{14,12},{16,18},{18,... | collective-permute-start | bytes 2359304 | tf_op jit(solution)/shard_map/ppermute | solution.py:23
  61.0 19.3 %collective-permute-start.12 = (bf16[1536,256]{1,0:T(8,128)(2,1)S(1)}, bf16[1536,256]{1,0:T(8,128)(2,1)S(1)}, u32[]{:S(2)}, u32[]{:S(2)}) collective-permute-start(bf16[1536,256]{1,0:T(8,128)(2,1)S(1)} %get-tuple-element.191.refs_2_), channel_id=1, source_target_pairs={{0,4},{2,6},{4,0},{6,2},{8,12},{10,14},{12,8},{14,10},{16,20},{18,... | collective-permute-start | bytes 2359304 | tf_op jit(solution)/shard_map/ppermute | solution.py:23
  80.5 20.6 %collective-permute-start.18 = (bf16[1728,256]{1,0:T(8,128)(2,1)S(1)}, bf16[1728,256]{1,0:T(8,128)(2,1)S(1)}, u32[]{:S(2)}, u32[]{:S(2)}) collective-permute-start(bf16[1728,256]{1,0:T(8,128)(2,1)S(1)} %get-tuple-element.221.refs_4_), channel_id=1, source_target_pairs={{0,2},{2,0},{4,6},{6,4},{8,10},{10,8},{12,14},{14,12},{16,18},{18,... | collective-permute-start | bytes 2654216 | tf_op jit(solution)/shard_map/ppermute | solution.py:23
  81.2 18.3 %collective-permute-start.16 = (bf16[1536,256]{1,0:T(8,128)(2,1)S(1)}, bf16[1536,256]{1,0:T(8,128)(2,1)S(1)}, u32[]{:S(2)}, u32[]{:S(2)}) collective-permute-start(bf16[1536,256]{1,0:T(8,128)(2,1)S(1)} %get-tuple-element.217.refs_0_), channel_id=1, source_target_pairs={{0,4},{2,6},{4,0},{6,2},{8,12},{10,14},{12,8},{14,10},{16,20},{18,... | collective-permute-start | bytes 2359304 | tf_op jit(solution)/shard_map/ppermute | solution.py:23
  82.7 17.9 %collective-permute-start.17 = (bf16[1536,256]{1,0:T(8,128)(2,1)S(1)}, bf16[1536,256]{1,0:T(8,128)(2,1)S(1)}, u32[]{:S(2)}, u32[]{:S(2)}) collective-permute-start(bf16[1536,256]{1,0:T(8,128)(2,1)S(1)} %get-tuple-element.219.refs_2_), channel_id=1, source_target_pairs={{0,8},{2,10},{4,12},{6,14},{8,0},{10,2},{12,4},{14,6},{16,24},{18,... | collective-permute-start | bytes 2359304 | tf_op jit(solution)/shard_map/ppermute | solution.py:23
  119.4 21.5 %collective-permute-start.26 = (bf16[4,96,1024]{2,1,0:T(8,128)(2,1)}, bf16[4,96,1024]{2,1,0:T(8,128)(2,1)S(1)}, u32[]{:S(2)}, u32[]{:S(2)}) collective-permute-start(bf16[4,96,1024]{2,1,0:T(8,128)(2,1)} %bitcast.20), channel_id=1, source_target_pairs={{0,2},{2,0},{4,6},{6,4},{8,10},{10,8},{12,14},{14,12},{16,18},{18,... | collective-permute-start | bytes 2359304 | tf_op jit(solution)/shard_map/ppermute | solution.py:23
  120.3 20.6 %collective-permute-start.27 = (bf16[4,96,1024]{2,1,0:T(8,128)(2,1)}, bf16[4,96,1024]{2,1,0:T(8,128)(2,1)S(1)}, u32[]{:S(2)}, u32[]{:S(2)}) collective-permute-start(bf16[4,96,1024]{2,1,0:T(8,128)(2,1)} %bitcast.21), channel_id=1, source_target_pairs={{0,4},{2,6},{4,0},{6,2},{8,12},{10,14},{12,8},{14,10},{16,20},{18,... | collective-permute-start | bytes 2359304 | tf_op jit(solution)/shard_map/ppermute | solution.py:23
  121.6 19.3 %collective-permute-start.28 = (bf16[4,96,1024]{2,1,0:T(8,128)(2,1)S(1)}, bf16[4,96,1024]{2,1,0:T(8,128)(2,1)S(1)}, u32[]{:S(2)}, u32[]{:S(2)}) collective-permute-start(bf16[4,96,1024]{2,1,0:T(8,128)(2,1)S(1)} %bitcast.60), channel_id=1, source_target_pairs={{0,8},{2,10},{4,12},{6,14},{8,0},{10,2},{12,4},{14,6},{16,24},{18,... | collective-permute-start | bytes 2359304 | tf_op jit(solution)/shard_map/ppermute | solution.py:23
  154.7 27.7 %collective-permute-start.33 = (bf16[2368,256]{1,0:T(8,128)(2,1)S(1)}, bf16[2368,256]{1,0:T(8,128)(2,1)S(1)}, u32[]{:S(2)}, u32[]{:S(2)}) collective-permute-start(bf16[2368,256]{1,0:T(8,128)(2,1)S(1)} %get-tuple-element.279), channel_id=1, source_target_pairs={{0,2},{2,0},{4,6},{6,4},{8,10},{10,8},{12,14},{14,12},{16,18},{18,... | collective-permute-start | bytes 3637256 | tf_op jit(solution)/shard_map/ppermute | solution.py:23
  155.7 25.5 %collective-permute-start.34 = (bf16[2176,256]{1,0:T(8,128)(2,1)S(1)}, bf16[2176,256]{1,0:T(8,128)(2,1)S(1)}, u32[]{:S(2)}, u32[]{:S(2)}) collective-permute-start(bf16[2176,256]{1,0:T(8,128)(2,1)S(1)} %get-tuple-element.280), channel_id=1, source_target_pairs={{0,4},{2,6},{4,0},{6,2},{8,12},{10,14},{12,8},{14,10},{16,20},{18,... | collective-permute-start | bytes 3342344 | tf_op jit(solution)/shard_map/ppermute | solution.py:23
  157.0 24.9 %collective-permute-start.35 = (bf16[2176,256]{1,0:T(8,128)(2,1)S(1)}, bf16[2176,256]{1,0:T(8,128)(2,1)S(1)}, u32[]{:S(2)}, u32[]{:S(2)}) collective-permute-start(bf16[2176,256]{1,0:T(8,128)(2,1)S(1)} %get-tuple-element.281), channel_id=1, source_target_pairs={{0,8},{2,10},{4,12},{6,14},{8,0},{10,2},{12,4},{14,6},{16,24},{18,... | collective-permute-start | bytes 3342344 | tf_op jit(solution)/shard_map/ppermute | solution.py:23
  183.4 18.4 %collective-permute-start.36 = (bf16[2,496,256]{2,1,0:T(8,128)(2,1)S(1)}, bf16[2,496,256]{2,1,0:T(8,128)(2,1)S(1)}, u32[]{:S(2)}, u32[]{:S(2)}) collective-permute-start(bf16[2,496,256]{2,1,0:T(8,128)(2,1)S(1)} %get-tuple-element.283), channel_id=1, source_target_pairs={{0,4},{2,6},{4,0},{6,2},{8,12},{10,14},{12,8},{14,10},{16,20},{18,... | collective-permute-start | bytes 1523720 | tf_op jit(solution)/shard_map/ppermute | solution.py:23
  184.7 17.0 %collective-permute-start.37 = (bf16[2,448,256]{2,1,0:T(8,128)(2,1)S(1)}, bf16[2,448,256]{2,1,0:T(8,128)(2,1)S(1)}, u32[]{:S(2)}, u32[]{:S(2)}) collective-permute-start(bf16[2,448,256]{2,1,0:T(8,128)(2,1)S(1)} %get-tuple-element.285), channel_id=1, source_target_pairs={{0,8},{2,10},{4,12},{6,14},{8,0},{10,2},{12,4},{14,6},{16,24},{18,... | collective-permute-start | bytes 1376264 | tf_op jit(solution)/shard_map/ppermute | solution.py:23
  186.8 17.2 %collective-permute-start.42 = (bf16[48,3072]{1,0:T(8,128)(2,1)S(1)}, bf16[48,3072]{1,0:T(8,128)(2,1)S(1)}, u32[]{:S(2)}, u32[]{:S(2)}) collective-permute-start(bf16[48,3072]{1,0:T(8,128)(2,1)S(1)} %get-tuple-element.297), channel_id=1, source_target_pairs={{0,16},{2,18},{4,20},{6,22},{8,24},{10,26},{12,28},{14,30},{16,0},... | collective-permute-start | bytes 884744 | tf_op jit(solution)/shard_map/ppermute | solution.py:23
  (27 other events, 192.9 us)

commit v4 on v3

--- a/solution.py
+++ b/solution.py
@@ -610,13 +610,8 @@
     low_ref[...] = hidden.astype(jnp.bfloat16)
 
 
-def feed_kernel(
-    own_hidden_ref, other_hidden_ref, inner_ref, outer_ref, counts_ref,
-    own_ref, other_ref, active_ref, slope_ref, count_ref, total_ref, *, each
-):
-    count = jnp.sum(counts_ref[...].astype(jnp.float32), axis=0, keepdims=True) / each
-    count_ref[...] = jnp.broadcast_to(count, count_ref.shape)
-    hidden = jnp.concatenate([own_hidden_ref[...], other_hidden_ref[...]], 0)
+def feed_kernel(hidden_ref, inner_ref, outer_ref, total_ref, active_ref, slope_ref, sum_ref):
+    hidden = hidden_ref[...]
     step = 256
     for start in range(0, inner_ref.shape[1], step):
         columns = slice(start, start + step)
@@ -627,12 +622,15 @@
         slope_ref[:, columns] = chance + upper * (jnp.exp(-0.5 * upper * upper) * 0.3989422804014327)
         part = dot_cols(active, outer_ref[:, columns])
         if start:
-            total_ref[...] += part
+            sum_ref[...] += part
         else:
-            total_ref[...] = part
-    half = own_ref.shape[0]
-    own_ref[...] = total_ref[:half, :]
-    other_ref[...] = total_ref[half:, :].astype(jnp.bfloat16)
+            sum_ref[...] = part
+    total_ref[...] = sum_ref[...].astype(total_ref.dtype)
+
+
+def count_kernel(counts_ref, count_ref, *, each):
+    count = jnp.sum(counts_ref[...].astype(jnp.float32), axis=0, keepdims=True) / each
+    count_ref[...] = jnp.broadcast_to(count, count_ref.shape)
 
 
 def second_norm_kernel(
@@ -658,8 +656,8 @@
     stats_ref[4:5, :] = jnp.broadcast_to(squares, (1, stats_ref.shape[1]))
 
 
-def feed_back_kernel(own_grad_ref, other_grad_ref, slope_ref, inner_ref, outer_ref, upper_ref, own_ref, other_ref, total_ref):
-    grads = jnp.concatenate([own_grad_ref[...], other_grad_ref[...]], 0)
+def feed_back_kernel(grads_ref, slope_ref, inner_ref, outer_ref, upper_ref, total_ref, sum_ref):
+    grads = grads_ref[...]
     step = 256
     for start in range(0, inner_ref.shape[1], step):
         columns = slice(start, start + step)
@@ -667,12 +665,10 @@
         upper_ref[:, columns] = upper
         part = dot_cols(upper, inner_ref[:, columns])
         if start:
-            total_ref[...] += part
+            sum_ref[...] += part
         else:
-            total_ref[...] = part
-    half = own_ref.shape[0]
-    own_ref[...] = total_ref[:half, :]
-    other_ref[...] = total_ref[half:, :].astype(jnp.bfloat16)
+            sum_ref[...] = part
+    total_ref[...] = sum_ref[...].astype(total_ref.dtype)
 
 
 def first_back_kernel(
@@ -698,19 +694,20 @@
 
 
 def wide_kernel(
-    owner_ref, own_grad_ref, other_grad_ref, active_ref, own_hidden_ref, other_hidden_ref, upper_ref, *refs,
-    groups, far_count, rows, step
+    owner_ref, own_grad_ref, other_grad_ref, own_active_ref, other_active_ref, own_hidden_ref, other_hidden_ref,
+    own_upper_ref, other_upper_ref, *refs, groups, far_count, rows, step
 ):
     outs, made_ref = refs[:-1], refs[-1]
     grads = jnp.concatenate([own_grad_ref[...], other_grad_ref[...]], 0)
     hidden = jnp.concatenate([own_hidden_ref[...], other_hidden_ref[...]], 0)
-    width = active_ref.shape[1]
+    width = own_active_ref.shape[1]
     third_width = 2 * width // 3
     for start in range(0, 2 * width, step):
+        part = slice(start % width, start % width + step)
         if start < width:
-            made_ref[...] = dot_rows(grads, active_ref[:, start : start + step])
+            made_ref[...] = dot_rows(grads, jnp.concatenate([own_active_ref[:, part], other_active_ref[:, part]], 0))
         else:
-            made_ref[...] = dot_rows(hidden, upper_ref[:, start - width : start - width + step])
+            made_ref[...] = dot_rows(hidden, jnp.concatenate([own_upper_ref[:, part], other_upper_ref[:, part]], 0))
         third = start // third_width
         for at, masks in enumerate(groups[third]):
             write_blocks(
@@ -719,19 +716,14 @@
             )
 
 
-def wide_gradients(owner, own_grad, other_grad, active, own_hidden, other_hidden, upper, groups):
+def wide_gradients(owner, grads, active, hidden, upper, groups):
     blocks = owner.shape[0]
-    far_count, rows = blocks // 8, own_grad.shape[1] // blocks
-    width = active.shape[1]
+    far_count, rows = blocks // 8, grads[0].shape[1] // blocks
+    width = active[0].shape[1]
     third_width = 2 * width // 3
     if rows % 16:
-        made = jnp.concatenate(
-            [
-                dot_rows(jnp.concatenate([own_grad, other_grad], 0), active),
-                dot_rows(jnp.concatenate([own_hidden, other_hidden], 0), upper),
-            ],
-            1,
-        )
+        whole = [jnp.concatenate(one, 0) for one in (grads, active, hidden, upper)]
+        made = jnp.concatenate([dot_rows(whole[0], whole[1]), dot_rows(whole[2], whole[3])], 1)
         outs = []
         for third, group in enumerate(groups):
             columns = made[:, third * third_width : (third + 1) * third_width]
@@ -747,9 +739,8 @@
             )
     kernel = functools.partial(wide_kernel, groups=groups, far_count=far_count, rows=rows, step=step)
     return local_call(
-        kernel, outs, [own_grad, other_grad, active, own_hidden, other_hidden, upper], [owner],
-        [pltpu.VMEM((own_grad.shape[1], step), jnp.float32)],
-        flops=8 * own_grad.size * width, spare=12,
+        kernel, outs, [*grads, *active, *hidden, *upper], [owner],
+        [pltpu.VMEM((grads[0].shape[1], step), jnp.float32)], spare=12,
     )
 
 
@@ -785,7 +776,7 @@
 
 def token_other_kernel(kv_grad_ref, query_grad_ref, kv_weight_ref, query_weight_ref, out_ref):
     near, half = query_grad_ref.shape[0] // 2, kv_grad_ref.shape[0] // 2
-    step = 512
+    step = 1024
 
     def one_part(at, carry):
         lines = pl.ds(pl.multiple_of(half + at * step, step), step)
@@ -1139,33 +1130,41 @@
     full_inner, full_outer, counts = place_packed(
         owner, both(late, late_came), tuple(plan), (wide, wide, PAIR), each
     )
-    part_own, part_other, active, slope, count_own = local_call(
-        functools.partial(feed_kernel, each=each),
-        [half_shape, low_shape, shaped((length, wide), jnp.bfloat16), shaped((length, wide)), shaped((8, PAIR))],
-        [hidden_own, hidden_other, full_inner, full_outer, counts],
-        scratch=[pltpu.VMEM((length, width), jnp.float32)],
-        flops=4 * length * width * wide, transcendentals=2 * length * wide, spare=12,
-    )
+    active_shape, slope_shape = shaped((rows, wide), jnp.bfloat16), shaped((rows, wide))
+    sums = [pltpu.VMEM((rows, width), jnp.float32)]
+    count_own = local_call(functools.partial(count_kernel, each=each), [shaped((8, PAIR))], [counts])[0]
     count_came = swap_core(count_own)
+    part_other, active_other, slope_other = local_call(
+        feed_kernel, [low_shape, active_shape, slope_shape], [hidden_other, full_inner, full_outer],
+        scratch=sums, spare=12,
+    )
+    part_came = swap_core(part_other)
+    part_own, active_own, slope_own = local_call(
+        feed_kernel, [half_shape, active_shape, slope_shape], [tie(part_other, hidden_own), full_inner, full_outer],
+        scratch=sums, spare=12,
+    )
     token_total = devices * lax.axis_size("tensor") * rows
     grad_second, grad_ffn_own, stats_two, result = local_call(
         functools.partial(second_norm_kernel, token_total=token_total),
         [half_shape, low_shape, shaped((8, width)), low_shape],
-        [hidden, part_own, swap_core(part_other), gain_two, shift_two, teacher, valid_row, count_own, count_came],
+        [hidden, part_own, part_came, gain_two, shift_two, teacher, valid_row, count_own, count_came],
         free=1,
     )
     grad_ffn_other = swap_core(grad_ffn_own)
-    upper_grad, part_own, part_other = local_call(
-        feed_back_kernel, [shaped((length, wide), jnp.bfloat16), half_shape, low_shape],
-        [grad_ffn_own, grad_ffn_other, slope, full_inner, full_outer],
-        scratch=[pltpu.VMEM((length, width), jnp.float32)],
-        flops=4 * length * width * wide, spare=12,
+    upper_own, part_own = local_call(
+        feed_back_kernel, [active_shape, half_shape], [grad_ffn_own, slope_own, full_inner, full_outer],
+        scratch=sums, spare=12,
+    )
+    upper_other, part_other = local_call(
+        feed_back_kernel, [active_shape, low_shape],
+        [tie(part_own, grad_ffn_other), slope_other, full_inner, full_outer], scratch=sums, spare=12,
     )
     part_came = swap_core(part_other)
     scatter_masks = tuple(tuple(slot_masks(bits[::-1])) for bits in ROUTES)
     groups = tuple((one[: span // 2], one[span // 2 :]) for one in scatter_masks)
     outs = wide_gradients(
-        owner, grad_ffn_own, grad_ffn_other, active, hidden_own, hidden_other, upper_grad, groups
+        owner, (grad_ffn_own, grad_ffn_other), (active_own, active_other), (hidden_own, hidden_other),
+        (upper_own, upper_other), groups
     )
     outs = [one.reshape(span // 2, slot_rows, one.shape[2]) for one in outs]
     wide_keep, wide_came = outs[::2], step(outs[1::2], 0)

time: 221 us -> 215 us (0.973)
  starting transfers between devices: 45.8 us -> 40.4 us
  waiting for transfers between devices: 98.1 us -> 101 us
  Pallas kernels: 68.1 us -> 65.3 us
    ppermute x34, starting transfers between devices: 44 us -> 38.3 us  [swap_mask(): lax.ppermute(block, 'dp', [(one, one ^ mask) for one in range(count)])]
    ppermute x34, waiting for transfers between devices: 93.3 us -> 98.6 us  [swap_mask(): lax.ppermute(block, 'dp', [(one, one ^ mask) for one in range(count)])]
    pallas_call x31 -> x34, Pallas kernels: 66.7 us -> 63.8 us  [local_call(): pl.pallas_call(kernel, out_shape=tuple((one if len(outs) - at <= free els...]
    ppermute x10, waiting for transfers between devices: 4.84 us -> 2.06 us  [swap_core(): return lax.ppermute(block, 'tensor', [(0, 1), (1, 0)])]
  transfers between devices with their start and end apart: 44 -> 44, of which waited for: 21 -> 22; matrix products, arithmetic and copies ran while one was open for 3% -> 3% of each run, Pallas kernels for 23% -> 24%
where the time goes in v4:
time: 215 us
  waiting for transfers between devices  101 us (47%)
  Pallas kernels  65.3 us (30%)
  starting transfers between devices  40.4 us (19%)
  other arithmetic  3.88 us (2%)
  local copies, waits for them, and re-layouts  2.61 us (1%)
    ppermute x34, waiting for transfers between devices, swap_mask(): lax.ppermute(block, 'dp', [(one, one ^ mask) for one in range(count)])  98.6 us
    pallas_call x34, Pallas kernels, local_call(): pl.pallas_call(kernel, out_shape=tuple((one if len(outs) - at <= free els...  63.8 us
    ppermute x34, starting transfers between devices, swap_mask(): lax.ppermute(block, 'dp', [(one, one ^ mask) for one in range(count)])  38.3 us
  transfers between devices with their start and end apart: 44, of which 22 were waited for; matrix products, arithmetic and copies ran while one was open for 3% of the time, Pallas kernels for 24%

profile of v4, /device:TPU:0, one launch (start us, length us, event | category | flops | bytes accessed | tf_op | source)
XLA Modules:
  0.0 215.0 jit_solution(13647997024776495206)
XLA Ops:
  2.1 3.0 %collective-permute-start = (bf16[256,256]{1,0:T(8,128)(2,1)S(1)}, bf16[256,256]{1,0:T(8,128)(2,1)S(1)}, u32[]{:S(2)}, u32[]{:S(2)}) collective-permute-start(bf16[256,256]{1,0:T(8,128)(2,1)S(1)} %get-tuple-element.170.refs_0_), channel_id=1, source_target_pairs={{0,2},{2,0},{4,6},{6,4},{8,10},{10,8},{12,14},{14,12},{16,18},{18,... | collective-permute-start | bytes 393224 | tf_op jit(solution)/shard_map/ppermute | solution.py:23
  8.2 2.6 %collective-permute-start.3 = (bf16[1,48,1536]{2,1,0:T(8,128)(2,1)S(1)}, bf16[1,48,1536]{2,1,0:T(8,128)(2,1)S(1)}, u32[]{:S(2)}, u32[]{:S(2)}) collective-permute-start(bf16[1,48,1536]{2,1,0:T(8,128)(2,1)S(1)} %bitcast.56), channel_id=1, source_target_pairs={{0,16},{2,18},{4,20},{6,22},{8,24},{10,26},{12,28},{14,30},{16,0},... | collective-permute-start | bytes 442376 | tf_op jit(solution)/shard_map/ppermute | solution.py:23
  15.8 9.3 %collective-permute-done.3 = bf16[1,48,1536]{2,1,0:T(8,128)(2,1)S(1)} collective-permute-done((bf16[1,48,1536]{2,1,0:T(8,128)(2,1)S(1)}, bf16[1,48,1536]{2,1,0:T(8,128)(2,1)S(1)}, u32[]{:S(2)}, u32[]{:S(2)}) %collective-permute-start.3) | collective-permute-done | bytes 147488 | tf_op jit(solution)/shard_map/ppermute | solution.py:23
  26.3 4.0 %collective-permute-done.7 = bf16[1,48,3200]{2,1,0:T(8,128)(2,1)S(1)} collective-permute-done((bf16[1,48,3200]{2,1,0:T(8,128)(2,1)S(1)}, bf16[1,48,3200]{2,1,0:T(8,128)(2,1)S(1)}, u32[]{:S(2)}, u32[]{:S(2)}) %collective-permute-start.7) | collective-permute-done | bytes 307232 | tf_op jit(solution)/shard_map/ppermute | solution.py:23
  30.4 2.3 %collective-permute-done.4.refs_1_ = bf16[704,256]{1,0:T(8,128)(2,1)S(1)} collective-permute-done((bf16[704,256]{1,0:T(8,128)(2,1)S(1)}, bf16[704,256]{1,0:T(8,128)(2,1)S(1)}, u32[]{:S(2)}, u32[]{:S(2)}) %collective-permute-start.4) | collective-permute-done | bytes 360480 | tf_op jit(solution)/shard_map/ppermute | solution.py:23
  32.7 2.7 %collective-permute-done.5.refs_3_ = bf16[704,256]{1,0:T(8,128)(2,1)S(1)} collective-permute-done((bf16[704,256]{1,0:T(8,128)(2,1)S(1)}, bf16[704,256]{1,0:T(8,128)(2,1)S(1)}, u32[]{:S(2)}, u32[]{:S(2)}) %collective-permute-start.5) | collective-permute-done | bytes 360480 | tf_op jit(solution)/shard_map/ppermute | solution.py:23
  37.4 2.5 %collective-permute-start.10 = (bf16[1840,256]{1,0:T(8,128)(2,1)S(1)}, bf16[1840,256]{1,0:T(8,128)(2,1)S(1)}, u32[]{:S(2)}, u32[]{:S(2)}) collective-permute-start(bf16[1840,256]{1,0:T(8,128)(2,1)S(1)} %get-tuple-element.180.refs_4_), channel_id=1, source_target_pairs={{0,4},{2,6},{4,0},{6,2},{8,12},{10,14},{12,8},{14,10},{16,20},{18,... | collective-permute-start | bytes 2826248 | tf_op jit(solution)/shard_map/ppermute | solution.py:23
  42.0 11.8 %collective-permute-done.8.refs_1_ = bf16[1792,256]{1,0:T(8,128)(2,1)} collective-permute-done((bf16[1792,256]{1,0:T(8,128)(2,1)S(1)}, bf16[1792,256]{1,0:T(8,128)(2,1)}, u32[]{:S(2)}, u32[]{:S(2)}) %collective-permute-start.8) | collective-permute-done | bytes 917536 | tf_op jit(solution)/shard_map/ppermute | solution.py:23
  54.5 1.9 shard_map.249
  56.4 1.9 shard_map.250.x_ref.own_ref
  61.7 17.6 %collective-permute-done.11.refs_1_ = bf16[1536,256]{1,0:T(8,128)(2,1)S(1)} collective-permute-done((bf16[1536,256]{1,0:T(8,128)(2,1)S(1)}, bf16[1536,256]{1,0:T(8,128)(2,1)S(1)}, u32[]{:S(2)}, u32[]{:S(2)}) %collective-permute-start.11) | collective-permute-done | bytes 786464 | tf_op jit(solution)/shard_map/ppermute | solution.py:23
  83.9 3.5 %shard_map.253 = (bf16[256,384]{1,0:T(8,128)(2,1)S(1)}, bf16[2048,768]{1,0:T(8,128)(2,1)S(1)}) custom-call(bf16[2048,768]{1,0:T(8,128)(2,1)S(1)} %shard_map.250.x_ref.own_ref, bf16[768,384]{1,0:T(8,128)(2,1)S(1)} %get-tuple-element.209.query_weight_ref.refs_0_, bf16[768,768]{1,0:T(8,128)(2,1)S(1)} %get-tuple-element.200.kv_weight_ref.refs_1_), custom_call_target="tpu_custom_call" | custom-call | flops 1000 | bytes 1000 | tf_op jit(solution)/shard_map/pallas_call | solution.py:70
  87.4 10.2 %shard_map.254 = (f32[512,384]{1,0:T(8,128)S(1)}, f32[24,8,128]{2,1,0:T(8,128)S(1)}, bf16[512,384]{1,0:T(8,128)(2,1)S(1)}, bf16[4096,768]{1,0:T(8,128)(2,1)S(1)}) custom-call(s32[501]{0:T(512)S(1)} %pad_add_fusion.numbers_ref, f32[8,128]{1,0:T(8,128)S(1)} %pad_maximum_fusion.3.query_side_ref, f32[4096,128]{1,0:T(8,128)S(1)} %broadcast_in_dim.143.key_side_ref, ...), custom_call_target="tpu_custom_call" | custom-call | flops 1000 | bytes 1000 | tf_op jit(solution)/shard_map/pallas_call | solution.py:70
  112.7 3.5 %shard_map.265 = (f32[8,48,1024]{2,1,0:T(8,128)S(1)}, bf16[8,48,1024]{2,1,0:T(8,128)(2,1)S(1)}, f32[8,48,1024]{2,1,0:T(8,128)S(1)}, bf16[8,48,1024]{2,1,0:T(8,12...) custom-call(s32[16]{0:T(128)S(1)} %add.229.owner_ref, ...), custom_call_target="tpu_custom_call" | custom-call | flops 1000 | bytes 1000 | tf_op jit(solution)/shard_map/pallas_call | solution.py:70
  121.6 11.5 %shard_map.267 = (bf16[512,384]{1,0:T(8,128)(2,1)S(1)}, bf16[4096,768]{1,0:T(8,128)(2,1)S(1)}) custom-call(s32[501]{0:T(512)S(1)} %pad_add_fusion.numbers_ref, f32[8,128]{1,0:T(8,128)S(1)} %pad_maximum_fusion.3.query_side_ref, f32[4096,128]{1,0:T(8,128)S(1)} %broadcast_in_dim.143.key_side_ref, bf16[512,384]{1,0:T(8,128)(2,1)S(1)} %get-tuple-element.234.q_ref, ...), custom_call_target="tpu_custom_call" | custom-call | flops 1000 | bytes 1000 | tf_op jit(solution)/shard_map/pallas_call | solution.py:70
  133.3 2.8 %shard_map.269 = bf16[2048,768]{1,0:T(8,128)(2,1)S(1)} custom-call(bf16[4096,768]{1,0:T(8,128)(2,1)S(1)} %get-tuple-element.270.kv_grad_ref, bf16[512,384]{1,0:T(8,128)(2,1)S(1)} %get-tuple-element.254.query_grad_ref, bf16[768,768]{1,0:T(8,128)(2,1)S(1)} %get-tuple-element.255.kv_weight_ref, bf16[384,768]{1,0:T(8,128)(2,1)S(1)} %get-tuple-element.256.query_weight_ref), custom_call_target="tpu_custom_call" | custom-call | flops 1000 | bytes 1000 | tf_op jit(solution)/shard_map/pallas_call | solution.py:70
  140.8 5.9 %shard_map.271.made_ref = f32[768,1536]{1,0:T(8,128)S(1)} custom-call(bf16[2048,768]{1,0:T(8,128)(2,1)S(1)} %shard_map.250.x_ref.own_ref, bf16[2048,768]{1,0:T(8,128)(2,1)S(1)} %collective-permute-done.14.other_ref, bf16[4096,768]{1,0:T(8,128)(2,1)S(1)} %get-tuple-element.270.kv_grad_ref, bf16[512,384]{1,0:T(8,128)(2,1)S(1)} %get-tuple-element.254.query_grad_ref, ...), custom_call_target="tpu_custom_call" | custom-call | flops 1000 | bytes 1000 | tf_op jit(solution)/shard_map/pallas_call | solution.py:70
  146.7 3.5 %shard_map.272 = (f32[4,496,256]{2,1,0:T(8,128)S(1)}, bf16[4,496,256]{2,1,0:T(8,128)(2,1)S(1)}, f32[4,448,256]{2,1,0:T(8,128)S(1)}, bf16[4,448,256]{2,1,0:T(8,12...) custom-call(s32[16]{0:T(128)S(1)} %add.229.owner_ref, ...), custom_call_target="tpu_custom_call" | custom-call | flops 1000 | bytes 1000 | tf_op jit(solution)/shard_map/pallas_call | solution.py:70
  154.1 23.8 %collective-permute-done.34.refs_4_.refs_1_ = bf16[2176,256]{1,0:T(8,128)(2,1)S(1)} collective-permute-done((bf16[2176,256]{1,0:T(8,128)(2,1)S(1)}, bf16[2176,256]{1,0:T(8,128)(2,1)S(1)}, u32[]{:S(2)}, u32[]{:S(2)}) %collective-permute-start.34) | collective-permute-done | bytes 1114144 | tf_op jit(solution)/shard_map/ppermute | solution.py:23
  183.3 2.1 collective-permute-start.42
  185.5 13.1 %collective-permute-done.37.refs_3_ = bf16[2,448,256]{2,1,0:T(8,128)(2,1)S(1)} collective-permute-done((bf16[2,448,256]{2,1,0:T(8,128)(2,1)S(1)}, bf16[2,448,256]{2,1,0:T(8,128)(2,1)S(1)}, u32[]{:S(2)}, u32[]{:S(2)}) %collective-permute-start.37) | collective-permute-done | bytes 458784 | tf_op jit(solution)/shard_map/ppermute | solution.py:23
  201.8 3.3 %collective-permute-done.40.refs_3_ = bf16[1,448,256]{2,1,0:T(8,128)(2,1)S(1)} collective-permute-done((bf16[1,448,256]{2,1,0:T(8,128)(2,1)S(1)}, bf16[1,448,256]{2,1,0:T(8,128)(2,1)S(1)}, u32[]{:S(2)}, u32[]{:S(2)}) %collective-permute-start.40) | collective-permute-done | bytes 229408 | tf_op jit(solution)/shard_map/ppermute | solution.py:23
  205.5 3.1 %collective-permute-start.43 = (bf16[48,1664]{1,0:T(8,128)(2,1)S(1)}, bf16[48,1664]{1,0:T(8,128)(2,1)S(1)}, u32[]{:S(2)}, u32[]{:S(2)}) collective-permute-start(bf16[48,1664]{1,0:T(8,128)(2,1)S(1)} %get-tuple-element.313), channel_id=1, source_target_pairs={{0,16},{2,18},{4,20},{6,22},{8,24},{10,26},{12,28},{14,30},{16,0},... | collective-permute-start | bytes 479240 | tf_op jit(solution)/shard_map/ppermute | solution.py:23
  209.7 3.9 %collective-permute-done.43.came_ref = bf16[48,1664]{1,0:T(8,128)(2,1)S(1)} collective-permute-done((bf16[48,1664]{1,0:T(8,128)(2,1)S(1)}, bf16[48,1664]{1,0:T(8,128)(2,1)S(1)}, u32[]{:S(2)}, u32[]{:S(2)}) %collective-permute-start.43) | collective-permute-done | bytes 159776 | tf_op jit(solution)/shard_map/ppermute | solution.py:23
  (171 shorter events, 63.9 us)
Async XLA Ops:
  2.1 23.0 %collective-permute-start = (bf16[256,256]{1,0:T(8,128)(2,1)S(1)}, bf16[256,256]{1,0:T(8,128)(2,1)S(1)}, u32[]{:S(2)}, u32[]{:S(2)}) collective-permute-start(bf16[256,256]{1,0:T(8,128)(2,1)S(1)} %get-tuple-element.170.refs_0_), channel_id=1, source_target_pairs={{0,2},{2,0},{4,6},{6,4},{8,10},{10,8},{12,14},{14,12},{16,18},{18,... | collective-permute-start | bytes 393224 | tf_op jit(solution)/shard_map/ppermute | solution.py:23
  5.1 20.0 %collective-permute-start.1 = (bf16[256,256]{1,0:T(8,128)(2,1)S(1)}, bf16[256,256]{1,0:T(8,128)(2,1)S(1)}, u32[]{:S(2)}, u32[]{:S(2)}) collective-permute-start(bf16[256,256]{1,0:T(8,128)(2,1)S(1)} %get-tuple-element.171.refs_1_), channel_id=1, source_target_pairs={{0,4},{2,6},{4,0},{6,2},{8,12},{10,14},{12,8},{14,10},{16,20},{18,... | collective-permute-start | bytes 393224 | tf_op jit(solution)/shard_map/ppermute | solution.py:23
  6.6 18.5 %collective-permute-start.2 = (bf16[256,256]{1,0:T(8,128)(2,1)S(1)}, bf16[256,256]{1,0:T(8,128)(2,1)S(1)}, u32[]{:S(2)}, u32[]{:S(2)}) collective-permute-start(bf16[256,256]{1,0:T(8,128)(2,1)S(1)} %get-tuple-element.172.refs_2_), channel_id=1, source_target_pairs={{0,8},{2,10},{4,12},{6,14},{8,0},{10,2},{12,4},{14,6},{16,24},{18,... | collective-permute-start | bytes 393224 | tf_op jit(solution)/shard_map/ppermute | solution.py:23
  8.2 16.9 %collective-permute-start.3 = (bf16[1,48,1536]{2,1,0:T(8,128)(2,1)S(1)}, bf16[1,48,1536]{2,1,0:T(8,128)(2,1)S(1)}, u32[]{:S(2)}, u32[]{:S(2)}) collective-permute-start(bf16[1,48,1536]{2,1,0:T(8,128)(2,1)S(1)} %bitcast.56), channel_id=1, source_target_pairs={{0,16},{2,18},{4,20},{6,22},{8,24},{10,26},{12,28},{14,30},{16,0},... | collective-permute-start | bytes 442376 | tf_op jit(solution)/shard_map/ppermute | solution.py:23
  10.8 19.5 %collective-permute-start.7 = (bf16[1,48,3200]{2,1,0:T(8,128)(2,1)S(1)}, bf16[1,48,3200]{2,1,0:T(8,128)(2,1)S(1)}, u32[]{:S(2)}, u32[]{:S(2)}) collective-permute-start(bf16[1,48,3200]{2,1,0:T(8,128)(2,1)S(1)} %bitcast.54), channel_id=1, source_target_pairs={{0,16},{2,18},{4,20},{6,22},{8,24},{10,26},{12,28},{14,30},{16,0},... | collective-permute-start | bytes 921608 | tf_op jit(solution)/shard_map/ppermute | solution.py:23
  36.5 17.3 %collective-permute-start.8 = (bf16[1792,256]{1,0:T(8,128)(2,1)S(1)}, bf16[1792,256]{1,0:T(8,128)(2,1)}, u32[]{:S(2)}, u32[]{:S(2)}) collective-permute-start(bf16[1792,256]{1,0:T(8,128)(2,1)S(1)} %get-tuple-element.188.refs_0_), channel_id=1, source_target_pairs={{0,8},{2,10},{4,12},{6,14},{8,0},{10,2},{12,4},{14,6},{16,24},{18,... | collective-permute-start | bytes 2752520 | tf_op jit(solution)/shard_map/ppermute | solution.py:23
  36.9 17.0 %collective-permute-start.9 = (bf16[1792,256]{1,0:T(8,128)(2,1)}, bf16[1792,256]{1,0:T(8,128)(2,1)}, u32[]{:S(2)}, u32[]{:S(2)}) collective-permute-start(bf16[1792,256]{1,0:T(8,128)(2,1)} %get-tuple-element.179.refs_2_), channel_id=1, source_target_pairs={{0,2},{2,0},{4,6},{6,4},{8,10},{10,8},{12,14},{14,12},{16,18},{18,... | collective-permute-start | bytes 2752520 | tf_op jit(solution)/shard_map/ppermute | solution.py:23
  58.3 29.1 %collective-permute-start.14 = (bf16[2048,768]{1,0:T(8,128)(2,1)S(1)}, bf16[2048,768]{1,0:T(8,128)(2,1)S(1)}, u32[]{:S(2)}, u32[]{:S(2)}) collective-permute-start(bf16[2048,768]{1,0:T(8,128)(2,1)S(1)} %shard_map.250.x_ref.own_ref), channel_id=1, source_target_pairs={{0,1},{1,0},{2,3},{3,2},{4,5},{5,4},{6,7},{7,6},{8,9},{9,8},{10,11... | collective-permute-start | bytes 9437192 | tf_op jit(solution)/shard_map/ppermute | solution.py:27
  58.4 21.9 %collective-permute-start.13 = (bf16[1632,256]{1,0:T(8,128)(2,1)S(1)}, bf16[1632,256]{1,0:T(8,128)(2,1)S(1)}, u32[]{:S(2)}, u32[]{:S(2)}) collective-permute-start(bf16[1632,256]{1,0:T(8,128)(2,1)S(1)} %get-tuple-element.197.refs_4_), channel_id=1, source_target_pairs={{0,8},{2,10},{4,12},{6,14},{8,0},{10,2},{12,4},{14,6},{16,24},{18,... | collective-permute-start | bytes 2506760 | tf_op jit(solution)/shard_map/ppermute | solution.py:23
  59.6 19.6 %collective-permute-start.11 = (bf16[1536,256]{1,0:T(8,128)(2,1)S(1)}, bf16[1536,256]{1,0:T(8,128)(2,1)S(1)}, u32[]{:S(2)}, u32[]{:S(2)}) collective-permute-start(bf16[1536,256]{1,0:T(8,128)(2,1)S(1)} %get-tuple-element.193.refs_0_), channel_id=1, source_target_pairs={{0,2},{2,0},{4,6},{6,4},{8,10},{10,8},{12,14},{14,12},{16,18},{18,... | collective-permute-start | bytes 2359304 | tf_op jit(solution)/shard_map/ppermute | solution.py:23
  61.0 19.3 %collective-permute-start.12 = (bf16[1536,256]{1,0:T(8,128)(2,1)S(1)}, bf16[1536,256]{1,0:T(8,128)(2,1)S(1)}, u32[]{:S(2)}, u32[]{:S(2)}) collective-permute-start(bf16[1536,256]{1,0:T(8,128)(2,1)S(1)} %get-tuple-element.195.refs_2_), channel_id=1, source_target_pairs={{0,4},{2,6},{4,0},{6,2},{8,12},{10,14},{12,8},{14,10},{16,20},{18,... | collective-permute-start | bytes 2359304 | tf_op jit(solution)/shard_map/ppermute | solution.py:23
  80.5 20.6 %collective-permute-start.18 = (bf16[1728,256]{1,0:T(8,128)(2,1)S(1)}, bf16[1728,256]{1,0:T(8,128)(2,1)S(1)}, u32[]{:S(2)}, u32[]{:S(2)}) collective-permute-start(bf16[1728,256]{1,0:T(8,128)(2,1)S(1)} %get-tuple-element.225.refs_4_), channel_id=1, source_target_pairs={{0,2},{2,0},{4,6},{6,4},{8,10},{10,8},{12,14},{14,12},{16,18},{18,... | collective-permute-start | bytes 2654216 | tf_op jit(solution)/shard_map/ppermute | solution.py:23
  81.2 18.2 %collective-permute-start.16 = (bf16[1536,256]{1,0:T(8,128)(2,1)S(1)}, bf16[1536,256]{1,0:T(8,128)(2,1)S(1)}, u32[]{:S(2)}, u32[]{:S(2)}) collective-permute-start(bf16[1536,256]{1,0:T(8,128)(2,1)S(1)} %get-tuple-element.221.refs_0_), channel_id=1, source_target_pairs={{0,4},{2,6},{4,0},{6,2},{8,12},{10,14},{12,8},{14,10},{16,20},{18,... | collective-permute-start | bytes 2359304 | tf_op jit(solution)/shard_map/ppermute | solution.py:23
  82.7 17.9 %collective-permute-start.17 = (bf16[1536,256]{1,0:T(8,128)(2,1)S(1)}, bf16[1536,256]{1,0:T(8,128)(2,1)S(1)}, u32[]{:S(2)}, u32[]{:S(2)}) collective-permute-start(bf16[1536,256]{1,0:T(8,128)(2,1)S(1)} %get-tuple-element.223.refs_2_), channel_id=1, source_target_pairs={{0,8},{2,10},{4,12},{6,14},{8,0},{10,2},{12,4},{14,6},{16,24},{18,... | collective-permute-start | bytes 2359304 | tf_op jit(solution)/shard_map/ppermute | solution.py:23
  116.2 19.9 %collective-permute-start.26 = (bf16[4,96,1024]{2,1,0:T(8,128)(2,1)S(1)}, bf16[4,96,1024]{2,1,0:T(8,128)(2,1)S(1)}, u32[]{:S(2)}, u32[]{:S(2)}) collective-permute-start(bf16[4,96,1024]{2,1,0:T(8,128)(2,1)S(1)} %bitcast.62), channel_id=1, source_target_pairs={{0,2},{2,0},{4,6},{6,4},{8,10},{10,8},{12,14},{14,12},{16,18},{18,... | collective-permute-start | bytes 2359304 | tf_op jit(solution)/shard_map/ppermute | solution.py:23
  117.0 19.3 %collective-permute-start.27 = (bf16[4,96,1024]{2,1,0:T(8,128)(2,1)S(1)}, bf16[4,96,1024]{2,1,0:T(8,128)(2,1)S(1)}, u32[]{:S(2)}, u32[]{:S(2)}) collective-permute-start(bf16[4,96,1024]{2,1,0:T(8,128)(2,1)S(1)} %bitcast.61), channel_id=1, source_target_pairs={{0,4},{2,6},{4,0},{6,2},{8,12},{10,14},{12,8},{14,10},{16,20},{18,... | collective-permute-start | bytes 2359304 | tf_op jit(solution)/shard_map/ppermute | solution.py:23
  118.5 19.0 %collective-permute-start.28 = (bf16[4,96,1024]{2,1,0:T(8,128)(2,1)S(1)}, bf16[4,96,1024]{2,1,0:T(8,128)(2,1)S(1)}, u32[]{:S(2)}, u32[]{:S(2)}) collective-permute-start(bf16[4,96,1024]{2,1,0:T(8,128)(2,1)S(1)} %bitcast.60), channel_id=1, source_target_pairs={{0,8},{2,10},{4,12},{6,14},{8,0},{10,2},{12,4},{14,6},{16,24},{18,... | collective-permute-start | bytes 2359304 | tf_op jit(solution)/shard_map/ppermute | solution.py:23
  151.4 27.7 %collective-permute-start.33 = (bf16[2368,256]{1,0:T(8,128)(2,1)S(1)}, bf16[2368,256]{1,0:T(8,128)(2,1)S(1)}, u32[]{:S(2)}, u32[]{:S(2)}) collective-permute-start(bf16[2368,256]{1,0:T(8,128)(2,1)S(1)} %get-tuple-element.287), channel_id=1, source_target_pairs={{0,2},{2,0},{4,6},{6,4},{8,10},{10,8},{12,14},{14,12},{16,18},{18,... | collective-permute-start | bytes 3637256 | tf_op jit(solution)/shard_map/ppermute | solution.py:23
  152.1 25.8 %collective-permute-start.34 = (bf16[2176,256]{1,0:T(8,128)(2,1)S(1)}, bf16[2176,256]{1,0:T(8,128)(2,1)S(1)}, u32[]{:S(2)}, u32[]{:S(2)}) collective-permute-start(bf16[2176,256]{1,0:T(8,128)(2,1)S(1)} %get-tuple-element.288), channel_id=1, source_target_pairs={{0,4},{2,6},{4,0},{6,2},{8,12},{10,14},{12,8},{14,10},{16,20},{18,... | collective-permute-start | bytes 3342344 | tf_op jit(solution)/shard_map/ppermute | solution.py:23
  153.7 24.9 %collective-permute-start.35 = (bf16[2176,256]{1,0:T(8,128)(2,1)S(1)}, bf16[2176,256]{1,0:T(8,128)(2,1)S(1)}, u32[]{:S(2)}, u32[]{:S(2)}) collective-permute-start(bf16[2176,256]{1,0:T(8,128)(2,1)S(1)} %get-tuple-element.289), channel_id=1, source_target_pairs={{0,8},{2,10},{4,12},{6,14},{8,0},{10,2},{12,4},{14,6},{16,24},{18,... | collective-permute-start | bytes 3342344 | tf_op jit(solution)/shard_map/ppermute | solution.py:23
  180.0 18.6 %collective-permute-start.36 = (bf16[2,496,256]{2,1,0:T(8,128)(2,1)S(1)}, bf16[2,496,256]{2,1,0:T(8,128)(2,1)S(1)}, u32[]{:S(2)}, u32[]{:S(2)}) collective-permute-start(bf16[2,496,256]{2,1,0:T(8,128)(2,1)S(1)} %get-tuple-element.291), channel_id=1, source_target_pairs={{0,4},{2,6},{4,0},{6,2},{8,12},{10,14},{12,8},{14,10},{16,20},{18,... | collective-permute-start | bytes 1523720 | tf_op jit(solution)/shard_map/ppermute | solution.py:23
  181.4 17.2 %collective-permute-start.37 = (bf16[2,448,256]{2,1,0:T(8,128)(2,1)S(1)}, bf16[2,448,256]{2,1,0:T(8,128)(2,1)S(1)}, u32[]{:S(2)}, u32[]{:S(2)}) collective-permute-start(bf16[2,448,256]{2,1,0:T(8,128)(2,1)S(1)} %get-tuple-element.293), channel_id=1, source_target_pairs={{0,8},{2,10},{4,12},{6,14},{8,0},{10,2},{12,4},{14,6},{16,24},{18,... | collective-permute-start | bytes 1376264 | tf_op jit(solution)/shard_map/ppermute | solution.py:23
  182.0 16.6 %collective-permute-start.38 = (bf16[2,448,256]{2,1,0:T(8,128)(2,1)S(1)}, bf16[2,448,256]{2,1,0:T(8,128)(2,1)S(1)}, u32[]{:S(2)}, u32[]{:S(2)}) collective-permute-start(bf16[2,448,256]{2,1,0:T(8,128)(2,1)S(1)} %get-tuple-element.295), channel_id=1, source_target_pairs={{0,2},{2,0},{4,6},{6,4},{8,10},{10,8},{12,14},{14,12},{16,18},{18,... | collective-permute-start | bytes 1376264 | tf_op jit(solution)/shard_map/ppermute | solution.py:23
  183.3 17.6 %collective-permute-start.42 = (bf16[48,3072]{1,0:T(8,128)(2,1)S(1)}, bf16[48,3072]{1,0:T(8,128)(2,1)S(1)}, u32[]{:S(2)}, u32[]{:S(2)}) collective-permute-start(bf16[48,3072]{1,0:T(8,128)(2,1)S(1)} %get-tuple-element.305), channel_id=1, source_target_pairs={{0,16},{2,18},{4,20},{6,22},{8,24},{10,26},{12,28},{14,30},{16,0},... | collective-permute-start | bytes 884744 | tf_op jit(solution)/shard_map/ppermute | solution.py:23
  (27 other events, 180.2 us)

commit v5 on v4

--- a/solution.py
+++ b/solution.py
@@ -478,21 +478,17 @@
         put_packed(out_ref, 2 * (rows + tail), second_ref, cuts[at], cuts[at + 1] - cuts[at], slot_rows)
 
 
-def place_tokens_kernel(*refs, masks, rows):
+def third_pack_kernel(*refs, masks, rows, tail):
     out_ref = refs[6]
     columns = refs[0].shape[1]
-    for at, group in enumerate(masks):
-        third = at // 2
-        for slot, mask in enumerate(group):
-            out_ref[mask * rows : (mask + 1) * rows, third * columns : (third + 1) * columns] = refs[at][
-                slot * rows : (slot + 1) * rows, :
-            ]
-
-
-def third_pack_kernel(*refs, tokens, tail):
     for at in range(3):
+        tokens = len(masks[2 * at]) * rows
         for side in range(2):
-            piece, target = refs[2 * at + side], refs[6 + at]
+            piece, target = refs[2 * at + side], refs[7 + at]
+            for slot, mask in enumerate(masks[2 * at + side]):
+                out_ref[mask * rows : (mask + 1) * rows, at * columns : (at + 1) * columns] = piece[
+                    slot * rows : (slot + 1) * rows, :
+                ]
             target[side * tail : (side + 1) * tail, :] = piece[tokens : tokens + tail, :]
             rest = piece.shape[0] - tokens - tail
             base = 2 * tail + side * rest
@@ -1064,16 +1060,12 @@
     tables, owner, came = lax.optimization_barrier((tables, owner, came))
     sent_masks = [tuple(slot_masks(bits[:2])) for bits in ROUTES]
     came_masks = [tuple(mask ^ (1 << bits[2]) for mask in sent) for sent, bits in zip(sent_masks, ROUTES)]
-    arrived = both(held, came)
-    held = local_call(
-        functools.partial(third_pack_kernel, tokens=4 * rows, tail=2 * tail),
-        messages([4 * tail + 2 * size for size in sizes]), arrived,
+    own, *held = local_call(
+        functools.partial(third_pack_kernel, masks=tuple(both(sent_masks, came_masks)), rows=rows, tail=2 * tail),
+        [shaped((span * rows, width), jnp.bfloat16)] + messages([4 * tail + 2 * size for size in sizes]),
+        both(held, came),
     )
     came = step(held, 0)
-    own = local_call(
-        functools.partial(place_tokens_kernel, masks=tuple(both(sent_masks, came_masks)), rows=rows),
-        [shaped((span * rows, width), jnp.bfloat16)], [tie(held[0], arrived[0])] + arrived[1:],
-    )[0]
     other = swap_core(own)
     late = local_call(
         functools.partial(fourth_pack_kernel, skip=4 * tail), messages([4 * size for size in sizes]),

time: 215 us -> 214 us (level)
    pallas_call x34 -> x33, Pallas kernels: 63.8 us -> 62.1 us  [local_call(): pl.pallas_call(kernel, out_shape=tuple((one if len(outs) - at <= free els...]
where the time goes in v5:
time: 214 us; the launch traced here: 213 us
  waiting for transfers between devices  101 us (47%)
  Pallas kernels  63.6 us (30%)
  starting transfers between devices  40.4 us (19%)
  other arithmetic  3.88 us (2%)
  local copies, waits for them, and re-layouts  2.61 us (1%)
    ppermute x34, waiting for transfers between devices, swap_mask(): lax.ppermute(block, 'dp', [(one, one ^ mask) for one in range(count)])  98.6 us
    pallas_call x33, Pallas kernels, local_call(): pl.pallas_call(kernel, out_shape=tuple((one if len(outs) - at <= free els...  62.1 us
    ppermute x34, starting transfers between devices, swap_mask(): lax.ppermute(block, 'dp', [(one, one ^ mask) for one in range(count)])  38.3 us
  transfers between devices with their start and end apart: 44, of which 22 were waited for; matrix products, arithmetic and copies ran while one was open for 3% of the time, Pallas kernels for 24%

profile of v5, /device:TPU:0, one launch (start us, length us, event | category | flops | bytes accessed | tf_op | source)
XLA Modules:
  0.0 213.2 jit_solution(8544305212295068822)
XLA Ops:
  2.1 3.0 %collective-permute-start = (bf16[256,256]{1,0:T(8,128)(2,1)S(1)}, bf16[256,256]{1,0:T(8,128)(2,1)S(1)}, u32[]{:S(2)}, u32[]{:S(2)}) collective-permute-start(bf16[256,256]{1,0:T(8,128)(2,1)S(1)} %get-tuple-element.170.refs_0_), channel_id=1, source_target_pairs={{0,2},{2,0},{4,6},{6,4},{8,10},{10,8},{12,14},{14,12},{16,18},{18,... | collective-permute-start | bytes 393224 | tf_op jit(solution)/shard_map/ppermute | solution.py:23
  8.2 2.6 %collective-permute-start.3 = (bf16[1,48,1536]{2,1,0:T(8,128)(2,1)S(1)}, bf16[1,48,1536]{2,1,0:T(8,128)(2,1)S(1)}, u32[]{:S(2)}, u32[]{:S(2)}) collective-permute-start(bf16[1,48,1536]{2,1,0:T(8,128)(2,1)S(1)} %bitcast.56), channel_id=1, source_target_pairs={{0,16},{2,18},{4,20},{6,22},{8,24},{10,26},{12,28},{14,30},{16,0},... | collective-permute-start | bytes 442376 | tf_op jit(solution)/shard_map/ppermute | solution.py:23
  15.8 9.3 %collective-permute-done.3 = bf16[1,48,1536]{2,1,0:T(8,128)(2,1)S(1)} collective-permute-done((bf16[1,48,1536]{2,1,0:T(8,128)(2,1)S(1)}, bf16[1,48,1536]{2,1,0:T(8,128)(2,1)S(1)}, u32[]{:S(2)}, u32[]{:S(2)}) %collective-permute-start.3) | collective-permute-done | bytes 147488 | tf_op jit(solution)/shard_map/ppermute | solution.py:23
  26.3 4.0 %collective-permute-done.7 = bf16[1,48,3200]{2,1,0:T(8,128)(2,1)S(1)} collective-permute-done((bf16[1,48,3200]{2,1,0:T(8,128)(2,1)S(1)}, bf16[1,48,3200]{2,1,0:T(8,128)(2,1)S(1)}, u32[]{:S(2)}, u32[]{:S(2)}) %collective-permute-start.7) | collective-permute-done | bytes 307232 | tf_op jit(solution)/shard_map/ppermute | solution.py:23
  30.4 2.3 %collective-permute-done.4.refs_1_ = bf16[704,256]{1,0:T(8,128)(2,1)S(1)} collective-permute-done((bf16[704,256]{1,0:T(8,128)(2,1)S(1)}, bf16[704,256]{1,0:T(8,128)(2,1)S(1)}, u32[]{:S(2)}, u32[]{:S(2)}) %collective-permute-start.4) | collective-permute-done | bytes 360480 | tf_op jit(solution)/shard_map/ppermute | solution.py:23
  32.7 2.7 %collective-permute-done.5.refs_3_ = bf16[704,256]{1,0:T(8,128)(2,1)S(1)} collective-permute-done((bf16[704,256]{1,0:T(8,128)(2,1)S(1)}, bf16[704,256]{1,0:T(8,128)(2,1)S(1)}, u32[]{:S(2)}, u32[]{:S(2)}) %collective-permute-start.5) | collective-permute-done | bytes 360480 | tf_op jit(solution)/shard_map/ppermute | solution.py:23
  37.4 2.5 %collective-permute-start.10 = (bf16[1840,256]{1,0:T(8,128)(2,1)S(1)}, bf16[1840,256]{1,0:T(8,128)(2,1)S(1)}, u32[]{:S(2)}, u32[]{:S(2)}) collective-permute-start(bf16[1840,256]{1,0:T(8,128)(2,1)S(1)} %get-tuple-element.180.refs_4_), channel_id=1, source_target_pairs={{0,4},{2,6},{4,0},{6,2},{8,12},{10,14},{12,8},{14,10},{16,20},{18,... | collective-permute-start | bytes 2826248 | tf_op jit(solution)/shard_map/ppermute | solution.py:23
  42.0 11.8 %collective-permute-done.8.refs_1_ = bf16[1792,256]{1,0:T(8,128)(2,1)} collective-permute-done((bf16[1792,256]{1,0:T(8,128)(2,1)S(1)}, bf16[1792,256]{1,0:T(8,128)(2,1)}, u32[]{:S(2)}, u32[]{:S(2)}) %collective-permute-start.8) | collective-permute-done | bytes 917536 | tf_op jit(solution)/shard_map/ppermute | solution.py:23
  54.5 2.1 shard_map.249
  59.9 17.6 %collective-permute-done.11.refs_1_ = bf16[1536,256]{1,0:T(8,128)(2,1)S(1)} collective-permute-done((bf16[1536,256]{1,0:T(8,128)(2,1)S(1)}, bf16[1536,256]{1,0:T(8,128)(2,1)S(1)}, u32[]{:S(2)}, u32[]{:S(2)}) %collective-permute-start.11) | collective-permute-done | bytes 786464 | tf_op jit(solution)/shard_map/ppermute | solution.py:23
  82.1 3.5 %shard_map.252 = (bf16[256,384]{1,0:T(8,128)(2,1)S(1)}, bf16[2048,768]{1,0:T(8,128)(2,1)S(1)}) custom-call(bf16[2048,768]{1,0:T(8,128)(2,1)S(1)} %get-tuple-element.187.x_ref.own_ref, bf16[768,384]{1,0:T(8,128)(2,1)S(1)} %get-tuple-element.209.query_weight_ref.refs_0_, bf16[768,768]{1,0:T(8,128)(2,1)S(1)} %get-tuple-element.200.kv_weight_ref.refs_1_), custom_call_target="tpu_custom_call" | custom-call | flops 1000 | bytes 1000 | tf_op jit(solution)/shard_map/pallas_call | solution.py:70
  85.7 10.2 %shard_map.253 = (f32[512,384]{1,0:T(8,128)S(1)}, f32[24,8,128]{2,1,0:T(8,128)S(1)}, bf16[512,384]{1,0:T(8,128)(2,1)S(1)}, bf16[4096,768]{1,0:T(8,128)(2,1)S(1)}) custom-call(s32[501]{0:T(512)S(1)} %pad_add_fusion.numbers_ref, f32[8,128]{1,0:T(8,128)S(1)} %pad_maximum_fusion.3.query_side_ref, f32[4096,128]{1,0:T(8,128)S(1)} %broadcast_in_dim.143.key_side_ref, ...), custom_call_target="tpu_custom_call" | custom-call | flops 1000 | bytes 1000 | tf_op jit(solution)/shard_map/pallas_call | solution.py:70
  104.0 1.7 shard_map.259
  111.0 3.5 %shard_map.264 = (f32[8,48,1024]{2,1,0:T(8,128)S(1)}, bf16[8,48,1024]{2,1,0:T(8,128)(2,1)S(1)}, f32[8,48,1024]{2,1,0:T(8,128)S(1)}, bf16[8,48,1024]{2,1,0:T(8,12...) custom-call(s32[16]{0:T(128)S(1)} %add.229.owner_ref, ...), custom_call_target="tpu_custom_call" | custom-call | flops 1000 | bytes 1000 | tf_op jit(solution)/shard_map/pallas_call | solution.py:70
  119.9 11.5 %shard_map.266 = (bf16[512,384]{1,0:T(8,128)(2,1)S(1)}, bf16[4096,768]{1,0:T(8,128)(2,1)S(1)}) custom-call(s32[501]{0:T(512)S(1)} %pad_add_fusion.numbers_ref, f32[8,128]{1,0:T(8,128)S(1)} %pad_maximum_fusion.3.query_side_ref, f32[4096,128]{1,0:T(8,128)S(1)} %broadcast_in_dim.143.key_side_ref, bf16[512,384]{1,0:T(8,128)(2,1)S(1)} %get-tuple-element.234.q_ref, ...), custom_call_target="tpu_custom_call" | custom-call | flops 1000 | bytes 1000 | tf_op jit(solution)/shard_map/pallas_call | solution.py:70
  131.6 2.8 %shard_map.268 = bf16[2048,768]{1,0:T(8,128)(2,1)S(1)} custom-call(bf16[4096,768]{1,0:T(8,128)(2,1)S(1)} %get-tuple-element.270.kv_grad_ref, bf16[512,384]{1,0:T(8,128)(2,1)S(1)} %get-tuple-element.254.query_grad_ref, bf16[768,768]{1,0:T(8,128)(2,1)S(1)} %get-tuple-element.255.kv_weight_ref, bf16[384,768]{1,0:T(8,128)(2,1)S(1)} %get-tuple-element.256.query_weight_ref), custom_call_target="tpu_custom_call" | custom-call | flops 1000 | bytes 1000 | tf_op jit(solution)/shard_map/pallas_call | solution.py:70
  139.1 5.9 %shard_map.270.made_ref = f32[768,1536]{1,0:T(8,128)S(1)} custom-call(bf16[2048,768]{1,0:T(8,128)(2,1)S(1)} %get-tuple-element.187.x_ref.own_ref, bf16[2048,768]{1,0:T(8,128)(2,1)S(1)} %collective-permute-done.14.other_ref, bf16[4096,768]{1,0:T(8,128)(2,1)S(1)} %get-tuple-element.270.kv_grad_ref, bf16[512,384]{1,0:T(8,128)(2,1)S(1)} %get-tuple-element.254.query_grad_ref, ...), custom_call_target="tpu_custom_call" | custom-call | flops 1000 | bytes 1000 | tf_op jit(solution)/shard_map/pallas_call | solution.py:70
  145.0 3.5 %shard_map.271 = (f32[4,496,256]{2,1,0:T(8,128)S(1)}, bf16[4,496,256]{2,1,0:T(8,128)(2,1)S(1)}, f32[4,448,256]{2,1,0:T(8,128)S(1)}, bf16[4,448,256]{2,1,0:T(8,12...) custom-call(s32[16]{0:T(128)S(1)} %add.229.owner_ref, ...), custom_call_target="tpu_custom_call" | custom-call | flops 1000 | bytes 1000 | tf_op jit(solution)/shard_map/pallas_call | solution.py:70
  152.4 23.8 %collective-permute-done.34.refs_4_.refs_1_ = bf16[2176,256]{1,0:T(8,128)(2,1)S(1)} collective-permute-done((bf16[2176,256]{1,0:T(8,128)(2,1)S(1)}, bf16[2176,256]{1,0:T(8,128)(2,1)S(1)}, u32[]{:S(2)}, u32[]{:S(2)}) %collective-permute-start.34) | collective-permute-done | bytes 1114144 | tf_op jit(solution)/shard_map/ppermute | solution.py:23
  181.6 2.1 %collective-permute-start.42 = (bf16[48,3072]{1,0:T(8,128)(2,1)S(1)}, bf16[48,3072]{1,0:T(8,128)(2,1)S(1)}, u32[]{:S(2)}, u32[]{:S(2)}) collective-permute-start(bf16[48,3072]{1,0:T(8,128)(2,1)S(1)} %get-tuple-element.305), channel_id=1, source_target_pairs={{0,16},{2,18},{4,20},{6,22},{8,24},{10,26},{12,28},{14,30},{16,0},... | collective-permute-start | bytes 884744 | tf_op jit(solution)/shard_map/ppermute | solution.py:23
  183.7 13.1 %collective-permute-done.37.refs_3_ = bf16[2,448,256]{2,1,0:T(8,128)(2,1)S(1)} collective-permute-done((bf16[2,448,256]{2,1,0:T(8,128)(2,1)S(1)}, bf16[2,448,256]{2,1,0:T(8,128)(2,1)S(1)}, u32[]{:S(2)}, u32[]{:S(2)}) %collective-permute-start.37) | collective-permute-done | bytes 458784 | tf_op jit(solution)/shard_map/ppermute | solution.py:23
  200.1 3.3 %collective-permute-done.40.refs_3_ = bf16[1,448,256]{2,1,0:T(8,128)(2,1)S(1)} collective-permute-done((bf16[1,448,256]{2,1,0:T(8,128)(2,1)S(1)}, bf16[1,448,256]{2,1,0:T(8,128)(2,1)S(1)}, u32[]{:S(2)}, u32[]{:S(2)}) %collective-permute-start.40) | collective-permute-done | bytes 229408 | tf_op jit(solution)/shard_map/ppermute | solution.py:23
  203.8 3.1 %collective-permute-start.43 = (bf16[48,1664]{1,0:T(8,128)(2,1)S(1)}, bf16[48,1664]{1,0:T(8,128)(2,1)S(1)}, u32[]{:S(2)}, u32[]{:S(2)}) collective-permute-start(bf16[48,1664]{1,0:T(8,128)(2,1)S(1)} %get-tuple-element.313), channel_id=1, source_target_pairs={{0,16},{2,18},{4,20},{6,22},{8,24},{10,26},{12,28},{14,30},{16,0},... | collective-permute-start | bytes 479240 | tf_op jit(solution)/shard_map/ppermute | solution.py:23
  208.0 3.9 %collective-permute-done.43.came_ref = bf16[48,1664]{1,0:T(8,128)(2,1)S(1)} collective-permute-done((bf16[48,1664]{1,0:T(8,128)(2,1)S(1)}, bf16[48,1664]{1,0:T(8,128)(2,1)S(1)}, u32[]{:S(2)}, u32[]{:S(2)}) %collective-permute-start.43) | collective-permute-done | bytes 159776 | tf_op jit(solution)/shard_map/ppermute | solution.py:23
  (170 shorter events, 62.2 us)
Async XLA Ops:
  2.1 23.0 %collective-permute-start = (bf16[256,256]{1,0:T(8,128)(2,1)S(1)}, bf16[256,256]{1,0:T(8,128)(2,1)S(1)}, u32[]{:S(2)}, u32[]{:S(2)}) collective-permute-start(bf16[256,256]{1,0:T(8,128)(2,1)S(1)} %get-tuple-element.170.refs_0_), channel_id=1, source_target_pairs={{0,2},{2,0},{4,6},{6,4},{8,10},{10,8},{12,14},{14,12},{16,18},{18,... | collective-permute-start | bytes 393224 | tf_op jit(solution)/shard_map/ppermute | solution.py:23
  5.1 20.0 %collective-permute-start.1 = (bf16[256,256]{1,0:T(8,128)(2,1)S(1)}, bf16[256,256]{1,0:T(8,128)(2,1)S(1)}, u32[]{:S(2)}, u32[]{:S(2)}) collective-permute-start(bf16[256,256]{1,0:T(8,128)(2,1)S(1)} %get-tuple-element.171.refs_1_), channel_id=1, source_target_pairs={{0,4},{2,6},{4,0},{6,2},{8,12},{10,14},{12,8},{14,10},{16,20},{18,... | collective-permute-start | bytes 393224 | tf_op jit(solution)/shard_map/ppermute | solution.py:23
  6.6 18.5 %collective-permute-start.2 = (bf16[256,256]{1,0:T(8,128)(2,1)S(1)}, bf16[256,256]{1,0:T(8,128)(2,1)S(1)}, u32[]{:S(2)}, u32[]{:S(2)}) collective-permute-start(bf16[256,256]{1,0:T(8,128)(2,1)S(1)} %get-tuple-element.172.refs_2_), channel_id=1, source_target_pairs={{0,8},{2,10},{4,12},{6,14},{8,0},{10,2},{12,4},{14,6},{16,24},{18,... | collective-permute-start | bytes 393224 | tf_op jit(solution)/shard_map/ppermute | solution.py:23
  8.2 16.9 %collective-permute-start.3 = (bf16[1,48,1536]{2,1,0:T(8,128)(2,1)S(1)}, bf16[1,48,1536]{2,1,0:T(8,128)(2,1)S(1)}, u32[]{:S(2)}, u32[]{:S(2)}) collective-permute-start(bf16[1,48,1536]{2,1,0:T(8,128)(2,1)S(1)} %bitcast.56), channel_id=1, source_target_pairs={{0,16},{2,18},{4,20},{6,22},{8,24},{10,26},{12,28},{14,30},{16,0},... | collective-permute-start | bytes 442376 | tf_op jit(solution)/shard_map/ppermute | solution.py:23
  10.8 19.5 %collective-permute-start.7 = (bf16[1,48,3200]{2,1,0:T(8,128)(2,1)S(1)}, bf16[1,48,3200]{2,1,0:T(8,128)(2,1)S(1)}, u32[]{:S(2)}, u32[]{:S(2)}) collective-permute-start(bf16[1,48,3200]{2,1,0:T(8,128)(2,1)S(1)} %bitcast.54), channel_id=1, source_target_pairs={{0,16},{2,18},{4,20},{6,22},{8,24},{10,26},{12,28},{14,30},{16,0},... | collective-permute-start | bytes 921608 | tf_op jit(solution)/shard_map/ppermute | solution.py:23
  36.5 17.3 %collective-permute-start.8 = (bf16[1792,256]{1,0:T(8,128)(2,1)S(1)}, bf16[1792,256]{1,0:T(8,128)(2,1)}, u32[]{:S(2)}, u32[]{:S(2)}) collective-permute-start(bf16[1792,256]{1,0:T(8,128)(2,1)S(1)} %get-tuple-element.178.refs_0_), channel_id=1, source_target_pairs={{0,8},{2,10},{4,12},{6,14},{8,0},{10,2},{12,4},{14,6},{16,24},{18,... | collective-permute-start | bytes 2752520 | tf_op jit(solution)/shard_map/ppermute | solution.py:23
  36.9 17.0 %collective-permute-start.9 = (bf16[1792,256]{1,0:T(8,128)(2,1)}, bf16[1792,256]{1,0:T(8,128)(2,1)}, u32[]{:S(2)}, u32[]{:S(2)}) collective-permute-start(bf16[1792,256]{1,0:T(8,128)(2,1)} %get-tuple-element.179.refs_2_), channel_id=1, source_target_pairs={{0,2},{2,0},{4,6},{6,4},{8,10},{10,8},{12,14},{14,12},{16,18},{18,... | collective-permute-start | bytes 2752520 | tf_op jit(solution)/shard_map/ppermute | solution.py:23
  56.6 29.1 %collective-permute-start.14 = (bf16[2048,768]{1,0:T(8,128)(2,1)S(1)}, bf16[2048,768]{1,0:T(8,128)(2,1)S(1)}, u32[]{:S(2)}, u32[]{:S(2)}) collective-permute-start(bf16[2048,768]{1,0:T(8,128)(2,1)S(1)} %get-tuple-element.187.x_ref.own_ref), channel_id=1, source_target_pairs={{0,1},{1,0},{2,3},{3,2},{4,5},{5,4},{6,7},{7,6},{8,9},{9,8},{10,11... | collective-permute-start | bytes 9437192 | tf_op jit(solution)/shard_map/ppermute | solution.py:27
  56.6 21.9 %collective-permute-start.13 = (bf16[1632,256]{1,0:T(8,128)(2,1)S(1)}, bf16[1632,256]{1,0:T(8,128)(2,1)S(1)}, u32[]{:S(2)}, u32[]{:S(2)}) collective-permute-start(bf16[1632,256]{1,0:T(8,128)(2,1)S(1)} %get-tuple-element.197.refs_4_), channel_id=1, source_target_pairs={{0,8},{2,10},{4,12},{6,14},{8,0},{10,2},{12,4},{14,6},{16,24},{18,... | collective-permute-start | bytes 2506760 | tf_op jit(solution)/shard_map/ppermute | solution.py:23
  57.9 19.6 %collective-permute-start.11 = (bf16[1536,256]{1,0:T(8,128)(2,1)S(1)}, bf16[1536,256]{1,0:T(8,128)(2,1)S(1)}, u32[]{:S(2)}, u32[]{:S(2)}) collective-permute-start(bf16[1536,256]{1,0:T(8,128)(2,1)S(1)} %get-tuple-element.193.refs_0_), channel_id=1, source_target_pairs={{0,2},{2,0},{4,6},{6,4},{8,10},{10,8},{12,14},{14,12},{16,18},{18,... | collective-permute-start | bytes 2359304 | tf_op jit(solution)/shard_map/ppermute | solution.py:23
  59.2 19.3 %collective-permute-start.12 = (bf16[1536,256]{1,0:T(8,128)(2,1)S(1)}, bf16[1536,256]{1,0:T(8,128)(2,1)S(1)}, u32[]{:S(2)}, u32[]{:S(2)}) collective-permute-start(bf16[1536,256]{1,0:T(8,128)(2,1)S(1)} %get-tuple-element.195.refs_2_), channel_id=1, source_target_pairs={{0,4},{2,6},{4,0},{6,2},{8,12},{10,14},{12,8},{14,10},{16,20},{18,... | collective-permute-start | bytes 2359304 | tf_op jit(solution)/shard_map/ppermute | solution.py:23
  78.7 20.6 %collective-permute-start.18 = (bf16[1728,256]{1,0:T(8,128)(2,1)S(1)}, bf16[1728,256]{1,0:T(8,128)(2,1)S(1)}, u32[]{:S(2)}, u32[]{:S(2)}) collective-permute-start(bf16[1728,256]{1,0:T(8,128)(2,1)S(1)} %get-tuple-element.225.refs_4_), channel_id=1, source_target_pairs={{0,2},{2,0},{4,6},{6,4},{8,10},{10,8},{12,14},{14,12},{16,18},{18,... | collective-permute-start | bytes 2654216 | tf_op jit(solution)/shard_map/ppermute | solution.py:23
  79.5 18.2 %collective-permute-start.16 = (bf16[1536,256]{1,0:T(8,128)(2,1)S(1)}, bf16[1536,256]{1,0:T(8,128)(2,1)S(1)}, u32[]{:S(2)}, u32[]{:S(2)}) collective-permute-start(bf16[1536,256]{1,0:T(8,128)(2,1)S(1)} %get-tuple-element.221.refs_0_), channel_id=1, source_target_pairs={{0,4},{2,6},{4,0},{6,2},{8,12},{10,14},{12,8},{14,10},{16,20},{18,... | collective-permute-start | bytes 2359304 | tf_op jit(solution)/shard_map/ppermute | solution.py:23
  81.0 17.9 %collective-permute-start.17 = (bf16[1536,256]{1,0:T(8,128)(2,1)S(1)}, bf16[1536,256]{1,0:T(8,128)(2,1)S(1)}, u32[]{:S(2)}, u32[]{:S(2)}) collective-permute-start(bf16[1536,256]{1,0:T(8,128)(2,1)S(1)} %get-tuple-element.223.refs_2_), channel_id=1, source_target_pairs={{0,8},{2,10},{4,12},{6,14},{8,0},{10,2},{12,4},{14,6},{16,24},{18,... | collective-permute-start | bytes 2359304 | tf_op jit(solution)/shard_map/ppermute | solution.py:23
  114.5 19.9 %collective-permute-start.26 = (bf16[4,96,1024]{2,1,0:T(8,128)(2,1)S(1)}, bf16[4,96,1024]{2,1,0:T(8,128)(2,1)S(1)}, u32[]{:S(2)}, u32[]{:S(2)}) collective-permute-start(bf16[4,96,1024]{2,1,0:T(8,128)(2,1)S(1)} %bitcast.62), channel_id=1, source_target_pairs={{0,2},{2,0},{4,6},{6,4},{8,10},{10,8},{12,14},{14,12},{16,18},{18,... | collective-permute-start | bytes 2359304 | tf_op jit(solution)/shard_map/ppermute | solution.py:23
  115.2 19.3 %collective-permute-start.27 = (bf16[4,96,1024]{2,1,0:T(8,128)(2,1)S(1)}, bf16[4,96,1024]{2,1,0:T(8,128)(2,1)S(1)}, u32[]{:S(2)}, u32[]{:S(2)}) collective-permute-start(bf16[4,96,1024]{2,1,0:T(8,128)(2,1)S(1)} %bitcast.61), channel_id=1, source_target_pairs={{0,4},{2,6},{4,0},{6,2},{8,12},{10,14},{12,8},{14,10},{16,20},{18,... | collective-permute-start | bytes 2359304 | tf_op jit(solution)/shard_map/ppermute | solution.py:23
  116.8 19.0 %collective-permute-start.28 = (bf16[4,96,1024]{2,1,0:T(8,128)(2,1)S(1)}, bf16[4,96,1024]{2,1,0:T(8,128)(2,1)S(1)}, u32[]{:S(2)}, u32[]{:S(2)}) collective-permute-start(bf16[4,96,1024]{2,1,0:T(8,128)(2,1)S(1)} %bitcast.60), channel_id=1, source_target_pairs={{0,8},{2,10},{4,12},{6,14},{8,0},{10,2},{12,4},{14,6},{16,24},{18,... | collective-permute-start | bytes 2359304 | tf_op jit(solution)/shard_map/ppermute | solution.py:23
  149.7 27.7 %collective-permute-start.33 = (bf16[2368,256]{1,0:T(8,128)(2,1)S(1)}, bf16[2368,256]{1,0:T(8,128)(2,1)S(1)}, u32[]{:S(2)}, u32[]{:S(2)}) collective-permute-start(bf16[2368,256]{1,0:T(8,128)(2,1)S(1)} %get-tuple-element.287), channel_id=1, source_target_pairs={{0,2},{2,0},{4,6},{6,4},{8,10},{10,8},{12,14},{14,12},{16,18},{18,... | collective-permute-start | bytes 3637256 | tf_op jit(solution)/shard_map/ppermute | solution.py:23
  150.4 25.8 %collective-permute-start.34 = (bf16[2176,256]{1,0:T(8,128)(2,1)S(1)}, bf16[2176,256]{1,0:T(8,128)(2,1)S(1)}, u32[]{:S(2)}, u32[]{:S(2)}) collective-permute-start(bf16[2176,256]{1,0:T(8,128)(2,1)S(1)} %get-tuple-element.288), channel_id=1, source_target_pairs={{0,4},{2,6},{4,0},{6,2},{8,12},{10,14},{12,8},{14,10},{16,20},{18,... | collective-permute-start | bytes 3342344 | tf_op jit(solution)/shard_map/ppermute | solution.py:23
  151.9 24.9 %collective-permute-start.35 = (bf16[2176,256]{1,0:T(8,128)(2,1)S(1)}, bf16[2176,256]{1,0:T(8,128)(2,1)S(1)}, u32[]{:S(2)}, u32[]{:S(2)}) collective-permute-start(bf16[2176,256]{1,0:T(8,128)(2,1)S(1)} %get-tuple-element.289), channel_id=1, source_target_pairs={{0,8},{2,10},{4,12},{6,14},{8,0},{10,2},{12,4},{14,6},{16,24},{18,... | collective-permute-start | bytes 3342344 | tf_op jit(solution)/shard_map/ppermute | solution.py:23
  178.2 18.6 %collective-permute-start.36 = (bf16[2,496,256]{2,1,0:T(8,128)(2,1)S(1)}, bf16[2,496,256]{2,1,0:T(8,128)(2,1)S(1)}, u32[]{:S(2)}, u32[]{:S(2)}) collective-permute-start(bf16[2,496,256]{2,1,0:T(8,128)(2,1)S(1)} %get-tuple-element.291), channel_id=1, source_target_pairs={{0,4},{2,6},{4,0},{6,2},{8,12},{10,14},{12,8},{14,10},{16,20},{18,... | collective-permute-start | bytes 1523720 | tf_op jit(solution)/shard_map/ppermute | solution.py:23
  179.7 17.2 %collective-permute-start.37 = (bf16[2,448,256]{2,1,0:T(8,128)(2,1)S(1)}, bf16[2,448,256]{2,1,0:T(8,128)(2,1)S(1)}, u32[]{:S(2)}, u32[]{:S(2)}) collective-permute-start(bf16[2,448,256]{2,1,0:T(8,128)(2,1)S(1)} %get-tuple-element.293), channel_id=1, source_target_pairs={{0,8},{2,10},{4,12},{6,14},{8,0},{10,2},{12,4},{14,6},{16,24},{18,... | collective-permute-start | bytes 1376264 | tf_op jit(solution)/shard_map/ppermute | solution.py:23
  180.2 16.6 %collective-permute-start.38 = (bf16[2,448,256]{2,1,0:T(8,128)(2,1)S(1)}, bf16[2,448,256]{2,1,0:T(8,128)(2,1)S(1)}, u32[]{:S(2)}, u32[]{:S(2)}) collective-permute-start(bf16[2,448,256]{2,1,0:T(8,128)(2,1)S(1)} %get-tuple-element.295), channel_id=1, source_target_pairs={{0,2},{2,0},{4,6},{6,4},{8,10},{10,8},{12,14},{14,12},{16,18},{18,... | collective-permute-start | bytes 1376264 | tf_op jit(solution)/shard_map/ppermute | solution.py:23
  181.6 17.6 %collective-permute-start.42 = (bf16[48,3072]{1,0:T(8,128)(2,1)S(1)}, bf16[48,3072]{1,0:T(8,128)(2,1)S(1)}, u32[]{:S(2)}, u32[]{:S(2)}) collective-permute-start(bf16[48,3072]{1,0:T(8,128)(2,1)S(1)} %get-tuple-element.305), channel_id=1, source_target_pairs={{0,16},{2,18},{4,20},{6,22},{8,24},{10,26},{12,28},{14,30},{16,0},... | collective-permute-start | bytes 884744 | tf_op jit(solution)/shard_map/ppermute | solution.py:23
  (27 other events, 180.1 us)
